TPU v7x, 256 devices: a whole 4x4x8 slice. The times are simulated.
256 devices in a mesh: dp: 32 (over z, y), mp: 8 (over x, core).
Axes of the slice: x: 4, y: 4, z: 8, core: 2. Of those that a mesh axis runs over, the one named last changes fastest.
Arguments:
- activations: bfloat16 [8192, 8192], P('dp'), may hold values from -6 to 6
- cotangents: bfloat16 [2, 8192, 1024], P(None, 'dp', 'mp'), may hold values from -0.0625 to 0.0625
- worker_of: int32 [32], replicated, may hold values from 0 to 31, as said below
- left_stats: float32 [32, 2, 512, 512], P('dp'), as said below
Outputs:
- new_stats: float32 [32, 2, 512, 512], P('dp')
- roots: float32 [32, 2, 512, 512], P('dp')
- update: bfloat16 [32, 512, 1024], P('dp', None, 'mp')
Inputs may be any that keep to these rules, and one draw needn't show every extreme that they name: `worker_of`: no worker is named by more than 2 blocks; some worker is named by exactly 2: the blocks k * 2 to k * 2 + 1 for some k. `left_stats`: every slot holds a symmetric positive definite matrix; slots that no block occupies are ignored.
All inputs are finite; a program needn't handle non-finite values.
Results may differ from a plain program's by a relative error of at most 0.005.
Values may be sent and summed in bfloat16 or wider, within the bound.
No kernel may reach another device: no remote copies, remote signals or barrier semaphores. Data moves between devices by JAX's collectives and lax.ppermute only.
A program may use at most 128 MiB of HBM per device.

v0:
```python
import jax
import jax.numpy as jnp
from jax import lax
from jax.sharding import PartitionSpec as P

KV = 1024
ITERS = 3


def batch_product(left, right):
    return jnp.einsum("sij,sjk->sik", left, right, precision=lax.Precision.HIGHEST)


def fourth_roots(matrices):
    dimension = matrices.shape[-1]
    identity = jnp.eye(dimension, dtype=jnp.float32)
    norm_values = jnp.sqrt(jnp.sum(matrices * matrices, axis=(1, 2)))[:, None, None]
    root_mats = identity[None] * norm_values ** (-0.25)
    powers = matrices / norm_values
    for iteration in range(ITERS):
        factor = (5.0 * identity[None] - powers) * 0.25
        root_mats = batch_product(root_mats, factor)
        square = batch_product(factor, factor)
        powers = batch_product(batch_product(square, square), powers)
    return root_mats


def local(activations, cotangents, worker_of, left_stats):
    token_count = activations.shape[0]
    feature_count = activations.shape[1]
    block_rows = left_stats.shape[-1]
    slot_count = left_stats.shape[1]
    columns = cotangents.shape[-1]
    per_matrix = feature_count // block_rows
    block_count = 2 * per_matrix
    workers = lax.axis_size("dp")
    owned_count = block_count // workers
    worker_index = lax.axis_index("dp")
    column_tiles = activations.reshape(token_count, per_matrix, block_rows)
    block_index = jnp.arange(block_count, dtype=jnp.int32)
    earlier = (worker_of[None, :] == worker_of[:, None]) & (
        block_index[None, :] < block_index[:, None]
    )
    slot_of = jnp.sum(earlier.astype(jnp.int32), axis=1)
    slot_range = jnp.arange(slot_count, dtype=jnp.int32)
    matching = (worker_of[None, :] == worker_index) & (slot_of[None, :] == slot_range[:, None])
    occupied = jnp.any(matching, axis=1).astype(jnp.float32)
    selector = matching.astype(jnp.bfloat16)
    blocks = jnp.arange(owned_count * lax.axis_size("dp"), dtype=jnp.int32)
    picked = jnp.take(column_tiles, blocks % per_matrix, axis=1)
    matrix_of = (blocks // per_matrix)[:, None, None]
    chosen = jnp.where(matrix_of == 0, cotangents[0][None], cotangents[1][None])
    chosen = jnp.where(
        jnp.ones((owned_count * lax.axis_size("dp"),), bool)[:, None, None],
        chosen,
        jnp.zeros((), chosen.dtype),
    )
    owned = lax.psum_scatter(
        jnp.einsum("tcb,ctk->cbk", picked, chosen, preferred_element_type=jnp.float32),
        "dp",
        scatter_dimension=0,
        tiled=True,
    ).astype(jnp.bfloat16)
    target = lax.dynamic_slice_in_dim(worker_of, worker_index * owned_count, owned_count)
    onehot = jnp.arange(workers, dtype=jnp.int32)[:, None] == target[None, :]
    outgoing = jnp.where(onehot[:, :, None, None], owned[None], jnp.zeros((), jnp.bfloat16))
    arrived = lax.all_to_all(outgoing, "dp", split_axis=0, concat_axis=0, tiled=True)
    arrived = arrived.reshape(block_count, block_rows, columns)
    local_grads = jnp.einsum(
        "sn,nbk->sbk", selector, arrived, preferred_element_type=jnp.float32
    ).astype(jnp.bfloat16)
    partial_gram = jnp.einsum(
        "sbk,sck->sbc", local_grads, local_grads, preferred_element_type=jnp.float32
    ) * (1.0 / KV)
    gram_total = lax.psum(partial_gram.astype(jnp.bfloat16), "mp").astype(jnp.float32)
    new_stats = (left_stats[0] + gram_total) * occupied[:, None, None]
    root_mats = fourth_roots(left_stats[0])
    root_mats = root_mats * occupied[:, None, None]
    preconditioned = jnp.einsum(
        "sbc,sck->sbk", root_mats, local_grads.astype(jnp.float32), precision=lax.Precision.HIGHEST
    ).astype(jnp.bfloat16)
    returning = jnp.einsum(
        "sn,sbk->nbk", selector, preconditioned, preferred_element_type=jnp.float32
    ).astype(jnp.bfloat16)
    returning = returning.reshape(workers, owned_count, block_rows, columns)
    received = lax.all_to_all(returning, "dp", split_axis=0, concat_axis=0, tiled=True)
    update = jnp.sum(received, axis=0, dtype=jnp.float32).astype(jnp.bfloat16)
    return (new_stats[None], root_mats[None], update)


def solution(mesh):
    return jax.shard_map(
        local,
        mesh=mesh,
        in_specs=(P("dp", None), P(None, "dp", "mp"), P(), P("dp", None, None, None)),
        out_specs=(P("dp", None, None, None), P("dp", None, None, None), P("dp", None, "mp")),
        check_vma=False,
    )
```

profile of v0, /device:TPU:7, one launch (start us, length us, event | category | flops | bytes accessed | tf_op | source)
XLA Modules:
  0.0 604.1 jit_solution(16846645916727868422)
XLA Ops:
  7.2 0.0 reduce-scatter.2.cloned.1.call-start
  7.2 0.9 slice_bitcast_fusion.1
  8.1 6.4 %copy.28 = bf16[256,8192]{0,1:T(8,128)(2,1)} copy(bf16[256,8192]{1,0:T(8,128)(2,1)} %param.4) | data formatting | bytes 8388608 | tf_op args[0]
  14.5 6.4 %copy.29 = bf16[256,16,512]{2,0,1:T(8,128)(2,1)} copy(bf16[256,16,512]{0,2,1:T(8,128)(2,1)} %bitcast.56) | data formatting | bytes 8388608 | tf_op jit(solution)/shard_map/reshape | solution.py:39
  20.9 6.9 %gather_fusion = bf16[32,256,512]{2,1,0:T(8,128)(2,1)} fusion(bf16[256,16,512]{2,0,1:T(8,128)(2,1)} %copy.29, s32[1024]{0:T(1024)S(1)} %pad_clamp_fusion), kind=kCustom, calls=%fused_computation | custom fusion | bytes 16777344 | tf_op jit(solution)/shard_map/jit(_take)/gather | solution.py:50
  27.8 9.2 %fusion = f32[32,512,128]{2,1,0:T(8,128)} fusion(bf16[32,256,512]{2,1,0:T(8,128)(2,1)} %gather_fusion, pred[32]{0:T(512)(128)(4,1)S(1)} %get-tuple-element.9, pred[32]{0:T(512)(128)(4,1)S(1)} %get-tuple-element.10, bf16[256,128]{1,0:T(8,128)(2,1)S(1)} %get-tuple-element.6, bf16[256,128]{1,0:T(8,128)(2,1)S(1)} %get-tuple-element.5), kind=kOutput, calls=%fused_computation.1 | convolution fusion | flops 1078984704 | bytes 16908352 | tf_op jit(solution)/shard_map/tcb,ctk->cbk/dot_general | solution.py:59
  37.0 0.0 copy-start.3
  37.0 0.0 reduce-scatter.2.cloned.1.call-update
  37.0 0.6 copy-done.3
  37.6 0.6 dynamic_slice.3
  38.2 0.6 iota_compare_fusion.2
  38.9 226.1 %reduce-scatter.2.cloned.1.call-done = f32[1,512,128]{2,1,0:T(8,128)} async-done(((f32[32,512,128]{2,1,0:T(8,128)}), f32[1,512,128]{2,1,0:T(8,128)}) %reduce-scatter.2.cloned.1.call-update) | async-done | bytes 262160 | tf_op jit(solution)/shard_map/reduce_scatter | solution.py:58
  264.9 1.0 convert_bitcast_fusion.1
  265.9 2.3 broadcast_select_fusion
  268.2 6.9 %all-to-all-start = ((bf16[32,1,512,128]{3,2,1,0:T(8,128)(2,1)}), bf16[32,1,512,128]{3,2,1,0:T(8,128)(2,1)}, u32[]{:S(2)}, u32[]{:S(2)}) async-start(bf16[32,1,512,128]{3,2,1,0:T(8,128)(2,1)} %broadcast_select_fusion), calls=%async_computation.1 | async-start | bytes 8388608 | tf_op jit(solution)/shard_map/all_to_all | solution.py:67
  275.1 0.6 all-reduce.2.cloned.1.call-start
  275.7 0.2 convert_reduce_fusion
  275.9 88.8 %all-to-all-done = bf16[32,1,512,128]{3,2,1,0:T(8,128)(2,1)} async-done(((bf16[32,1,512,128]{3,2,1,0:T(8,128)(2,1)}), bf16[32,1,512,128]{3,2,1,0:T(8,128)(2,1)}, u32[]{:S(2)}, u32[]{:S(2)}) %all-to-all-start) | async-done | bytes 4194336 | tf_op jit(solution)/shard_map/all_to_all | solution.py:67
  364.6 4.6 fusion.26
  369.2 0.0 copy-start
  369.2 1.4 multiply_convert_fusion
  370.7 0.0 all-reduce.2.cloned.1.call-update
  370.7 0.1 fusion.60
  370.8 0.1 fusion.41
  370.9 1.1 fusion.42
  372.1 68.3 %all-reduce.2.cloned.1.call-done = bf16[2,512,512]{2,1,0:T(8,128)(2,1)} async-done(((bf16[2,512,512]{2,1,0:T(8,128)(2,1)}), bf16[2,512,512]{2,1,0:T(8,128)(2,1)}) %all-reduce.2.cloned.1.call-update) | async-done | bytes 1048592 | tf_op jit(solution)/shard_map/psum | solution.py:75
  440.4 0.0 copy-done
  440.4 3.2 fusion.10
  443.6 4.0 fusion.20
  447.6 0.0 copy-start.1
  447.6 3.5 fusion.63
  451.1 0.0 copy-done.1
  451.1 3.8 fusion.61
  455.0 3.7 fusion.21
  458.7 3.5 fusion.64
  462.3 0.0 copy-start.2
  462.3 3.6 fusion.65
  465.8 0.0 copy-done.2
  465.9 4.1 fusion.14
  470.0 3.7 fusion.22
  473.7 3.7 fusion.11
  477.3 1.2 fusion.23
  478.5 1.3 convert_bitcast_fusion
  479.9 3.8 copy.36
  483.7 9.7 %all-to-all-start.1 = ((bf16[32,1,512,128]{3,2,1,0:T(8,128)(2,1)}), bf16[32,1,512,128]{3,2,1,0:T(8,128)(2,1)}, u32[]{:S(2)}, u32[]{:S(2)}) async-start(bf16[32,1,512,128]{3,2,1,0:T(8,128)(2,1)} %copy.36), calls=%async_computation.2 | async-start | bytes 8388608 | tf_op jit(solution)/shard_map/all_to_all | solution.py:86
  493.4 1.7 multiply_bitcast_fusion
  495.1 98.5 %all-to-all-done.1 = bf16[32,1,512,128]{3,2,1,0:T(8,128)(2,1)} async-done(((bf16[32,1,512,128]{3,2,1,0:T(8,128)(2,1)}), bf16[32,1,512,128]{3,2,1,0:T(8,128)(2,1)}, u32[]{:S(2)}, u32[]{:S(2)}) %all-to-all-start.1) | async-done | bytes 4194336 | tf_op jit(solution)/shard_map/all_to_all | solution.py:86
  593.6 3.5 reduce_sum.34
  (6 shorter events, 0.0 us)
Async XLA Ops:
  7.2 257.8 %reduce-scatter.2.cloned.1.call-start = ((), (), s32[]{:S(2)}) async-start(), calls=%async_computation.3 | async-start | bytes 8650752 | tf_op jit(solution)/shard_map/reduce_scatter | solution.py:58
  37.0 0.7 copy-start.3
  268.2 96.4 %all-to-all-start = ((bf16[32,1,512,128]{3,2,1,0:T(8,128)(2,1)}), bf16[32,1,512,128]{3,2,1,0:T(8,128)(2,1)}, u32[]{:S(2)}, u32[]{:S(2)}) async-start(bf16[32,1,512,128]{3,2,1,0:T(8,128)(2,1)} %broadcast_select_fusion), calls=%async_computation.1 | async-start | bytes 8388608 | tf_op jit(solution)/shard_map/all_to_all | solution.py:67
  275.1 165.3 %all-reduce.2.cloned.1.call-start = ((), (), s32[]{:S(2)}) async-start(), calls=%async_computation.4 | async-start | bytes 2097152 | tf_op jit(solution)/shard_map/psum | solution.py:75
  369.2 71.1 %copy-start = (f32[1,2,512,512]{3,2,1,0:T(8,128)S(1)}, f32[1,2,512,512]{3,2,1,0:T(8,128)}, u32[]{:S(2)}) copy-start(f32[1,2,512,512]{3,2,1,0:T(8,128)} %param.7) | copy-start | bytes 6291460
  447.6 3.5 copy-start.1
  462.3 3.6 copy-start.2
  483.7 109.9 %all-to-all-start.1 = ((bf16[32,1,512,128]{3,2,1,0:T(8,128)(2,1)}), bf16[32,1,512,128]{3,2,1,0:T(8,128)(2,1)}, u32[]{:S(2)}, u32[]{:S(2)}) async-start(bf16[32,1,512,128]{3,2,1,0:T(8,128)(2,1)} %copy.36), calls=%async_computation.2 | async-start | bytes 8388608 | tf_op jit(solution)/shard_map/all_to_all | solution.py:86
Sparse Core Ops, SparseCore 0:
  37.1 227.7 reduce-scatter.1
  370.8 69.5 all-reduce.1
where the time goes:
time: 609 us; the launch traced here: 604 us
  waiting for transfers between devices  482 us (79%)
  matrix products  51.4 us (8%)
  local copies, waits for them, and re-layouts  25.6 us (4%)
  starting transfers between devices  17.2 us (3%)
  between operations  14.5 us (2%)
  other arithmetic  13.8 us (2%)
    reduce_scatter x1, waiting for transfers between devices, local(): lax.psum_scatter(jnp.einsum('tcb,ctk->cbk', picked, chosen, preferred_ele...  226 us
    all_to_all x1, waiting for transfers between devices, local(): lax.all_to_all(returning, 'dp', split_axis=0, concat_axis=0, tiled=True)  98.5 us
    all_to_all x1, waiting for transfers between devices, local(): lax.all_to_all(outgoing, 'dp', split_axis=0, concat_axis=0, tiled=True)  88.8 us
    psum x1, waiting for transfers between devices, local(): lax.psum(partial_gram.astype(jnp.bfloat16), 'mp').astype(jnp.float32)  68.3 us
    dot_general x9, matrix products, batch_product(): jnp.einsum('sij,sjk->sik', left, right, precision=lax.Precision.HIGHEST)  33.7 us
  transfers between devices with their start and end apart: 4, of which 4 were waited for; matrix products, arithmetic and copies ran while one was open for 1% of the time, Pallas kernels for 0%

commit v1 on v0

v1 whole, which is shorter than its diff:
```python
import jax
import jax.numpy as jnp
from jax import lax
from jax.sharding import Mesh, PartitionSpec as P

KV = 1024
NZ, NY, NX, NC = 8, 4, 4, 2
BF = jnp.bfloat16
F32 = jnp.float32


def shift(x, axis, size, offset):
    return lax.ppermute(x, axis, [(i, (i + offset) % size) for i in range(size)])


def pick(parts, index):
    return lax.dynamic_index_in_dim(parts, index, 0, keepdims=False)


def batch_product(left, right):
    return jnp.einsum("sij,sjk->sik", left, right, precision=lax.Precision.HIGH, preferred_element_type=F32)


def fourth_roots(matrices):
    identity = jnp.eye(matrices.shape[-1], dtype=F32)[None]
    norm_values = jnp.sqrt(jnp.sum(matrices * matrices, axis=(1, 2)))[:, None, None]
    m = matrices / norm_values
    m2 = batch_product(m, m)
    z = (5.0 * identity - m) * 0.25
    z2 = (25.0 * identity - 10.0 * m + m2) * (1.0 / 16.0)
    u = (5.0 * m - m2) * 0.25
    z4 = batch_product(z2, z2)
    x1 = 1.25 * z - 0.25 * batch_product(z4, u)
    s = batch_product(x1, x1)
    t = batch_product(x1, m)
    s2 = batch_product(s, s)
    x = 1.25 * x1 - 0.25 * batch_product(s2, t)
    return x * norm_values ** (-0.25)


def in_order(parts, index, size):
    ring = [parts[0]] + parts[:0:-1]
    ring = jnp.stack(ring + ring)
    return lax.dynamic_slice_in_dim(ring, size - index, size, 0)


def local(activations, cotangents, worker_of, left_stats):
    z, y = lax.axis_index("z"), lax.axis_index("y")
    x, c = lax.axis_index("x"), lax.axis_index("c")
    left = left_stats[0]
    block = jnp.arange(32, dtype=jnp.int32)
    slot_of = jnp.sum(
        ((worker_of[None, :] == worker_of[:, None]) & (block[None, :] < block[:, None])).astype(jnp.int32), axis=1
    )
    mine = z * 4 + y

    cots = jnp.transpose(cotangents, (1, 0, 2)).reshape(256, 256)
    cots_in = [shift(cots, "y", NY, o) for o in (1, 2, 3)]
    halves = [lax.dynamic_slice_in_dim(t, c * 128, 128, 0) for t in cots_in]
    others = [lax.dynamic_slice_in_dim(t, 128 - c * 128, 128, 0) for t in cots_in]
    cots_all = jnp.concatenate([cots] + halves + others, axis=0)
    got = []
    kept = None
    for k in (0, 1, 3, 2):
        first = ((z + k) % 4) * 2048
        own = lax.dynamic_slice(activations, (0, first + y * 512), (256, 512))
        pieces = []
        for o in (1, 2, 3):
            piece = lax.dynamic_slice(activations, (c * 128, first + ((y + o) % 4) * 512), (128, 512))
            pieces.append(shift(piece, "y", NY, o))
        direct = jnp.concatenate(pieces, axis=0)
        swapped = shift(direct, "c", NC, 1)
        acts = jnp.concatenate([own, direct, swapped], axis=0)
        part = jnp.einsum("tn,tf->nf", cots_all, acts, preferred_element_type=F32).reshape(2, 128, 512)
        matrix = ((z + k) % 8) // 4
        near, far = pick(part, matrix), pick(part, 1 - matrix)
        if k == 0:
            kept = near
        else:
            got.append(shift(near.astype(BF), "z", NZ, k))
        got.append(shift(far.astype(BF), "z", NZ, k + 4))
    total = kept
    for piece in got:
        total = total + piece.astype(F32)
    grad = total.astype(BF)

    occupied = jnp.stack([jnp.any((worker_of == mine) & (slot_of == s)) for s in range(2)]).astype(F32)
    roots = fourth_roots(left) * occupied[:, None, None]
    row = (c * 4 + x) * 64
    rows = lax.dynamic_slice(roots, (0, row, 0), (2, 64, 512)).astype(BF)
    items = jnp.stack([rows] + [shift(rows, "y", NY, o) for o in (1, 2, 3)]).reshape(8, 64, 512)
    routed = []
    for o in range(8):
        b = ((z + o) % 8) * 4 + y
        item = pick(items, ((y - worker_of[b] % 4) % 4) * 2 + slot_of[b])
        routed.append(item if o == 0 else shift(item, "z", NZ, o))
    mine_rows = pick(jnp.stack(routed), (z - worker_of[mine] // 4) % 8)
    by_x = in_order([mine_rows] + [shift(mine_rows, "x", NX, o) for o in (1, 2, 3)], x, NX).reshape(256, 512)
    by_c = shift(by_x, "c", NC, 1)
    root = jnp.where(c == 0, jnp.concatenate([by_x, by_c]), jnp.concatenate([by_c, by_x]))
    update = jnp.einsum("bc,kc->bk", root, grad, preferred_element_type=F32).astype(BF)

    gram = jnp.einsum("kb,kc->bc", grad, grad, preferred_element_type=F32) * (1.0 / KV)
    gram = gram.reshape(2, 256, 512)
    half = pick(gram, c) + shift(pick(gram, 1 - c).astype(BF), "c", NC, 1).astype(F32)
    half = half.reshape(4, 64, 512)
    quarter = pick(half, x)
    for o in (1, 2, 3):
        quarter = quarter + shift(pick(half, (x + o) % 4).astype(BF), "x", NX, o).astype(F32)
    quarter = quarter.astype(BF)
    column = jnp.stack([quarter] + [shift(quarter, "z", NZ, o) for o in range(1, 8)])
    blocks = jnp.arange(8, dtype=jnp.int32) * 4 + y
    arrived = None
    for o in range(4):
        target = z * 4 + (y + o) % 4
        pair = []
        for s in range(2):
            match = (worker_of[blocks] == target) & (slot_of[blocks] == s)
            source = jnp.sum(jnp.where(match, jnp.arange(8, dtype=jnp.int32), 0))
            item = pick(column, (z - source) % 8)
            pair.append(jnp.where(jnp.any(match), item, jnp.zeros((), BF)))
        pair = jnp.stack(pair)
        if o:
            pair = shift(pair, "y", NY, o)
        arrived = pair if arrived is None else arrived + pair
    by_x = in_order([arrived] + [shift(arrived, "x", NX, o) for o in (1, 2, 3)], x, NX)
    by_c = shift(by_x, "c", NC, 1)
    both = jnp.where(c == 0, jnp.stack([by_x, by_c]), jnp.stack([by_c, by_x]))
    gram_total = jnp.transpose(both, (2, 0, 1, 3, 4)).reshape(2, 512, 512).astype(F32)
    new_stats = (left + gram_total) * occupied[:, None, None]
    return new_stats[None], roots[None], update[None]


def solution(mesh):
    fine = Mesh(mesh.devices.reshape(NZ, NY, NX, NC), ("z", "y", "x", "c"))
    dp, mp = ("z", "y"), ("x", "c")
    return jax.shard_map(
        local,
        mesh=fine,
        in_specs=(P(dp, None), P(None, dp, mp), P(), P(dp, None, None, None)),
        out_specs=(P(dp, None, None, None), P(dp, None, None, None), P(dp, None, mp)),
        check_vma=False,
    )
```

time: 609 us -> 251 us (0.41)
  the two profiles are of different devices: /device:TPU:7 before, /device:TPU:1 now
where the time goes in v1:
time: 251 us; the launch traced here: 247 us
  waiting for transfers between devices  82.6 us (33%)
  starting transfers between devices  81.5 us (32%)
  between operations  30.1 us (12%)
  matrix products  26.5 us (11%)
  other arithmetic  14.8 us (6%)
  local copies, waits for them, and re-layouts  11.5 us (5%)
    ppermute x58, waiting for transfers between devices, shift(): lax.ppermute(x, axis, [(i, (i + offset) % size) for i in range(size)])  82.6 us
    ppermute x58, starting transfers between devices, shift(): lax.ppermute(x, axis, [(i, (i + offset) % size) for i in range(size)])  81.5 us
    dot_general x7, matrix products, batch_product(): jnp.einsum('sij,sjk->sik', left, right, precision=lax.Precision.HIGH, pre...  23.4 us
    unnamed x64, local copies, waits for them, and re-layouts  5.04 us
  transfers between devices with their start and end apart: 58, of which 26 were waited for; matrix products, arithmetic and copies ran while one was open for 17% of the time, Pallas kernels for 0%

profile of v1, /device:TPU:1, one launch (start us, length us, event | category | flops | bytes accessed | tf_op | source)
XLA Modules:
  0.0 247.0 jit_solution(128227578398114396)
XLA Ops:
  0.8 2.6 %fusion.69 = (bf16[128,512]{1,0:T(8,128)(2,1)}, bf16[128,512]{1,0:T(8,128)(2,1)S(1)}, bf16[128,512]{1,0:T(8,128)(2,1)}, bf16[128,512]{1,0:T(8,128)(2,1)}, bf16[1...) fusion(bf16[256,8192]{1,0:T(8,128)(2,1)} %param.4, ...), kind=kLoop, calls=%fused_computation.204 | loop fusion | bytes 3145780 | tf_op jit(solution)/shard_map/dynamic_slice | solution.py:69
  3.4 2.2 collective-permute-start.20
  5.6 2.6 %collective-permute-start.21 = (bf16[128,512]{1,0:T(8,128)(2,1)}, bf16[128,512]{1,0:T(8,128)(2,1)S(1)}, u32[]{:S(2)}, u32[]{:S(2)}) collective-permute-start(bf16[128,512]{1,0:T(8,128)(2,1)} %get-tuple-element.36), channel_id=1, source_target_pairs={{0,16},{8,24},{16,0},{24,8},{1,17},{9,25},{17,1},{25,9},{2,18},{10... | collective-permute-start | bytes 393224 | tf_op jit(solution)/shard_map/ppermute | solution.py:13
  8.2 1.1 collective-permute-start.22
  18.8 2.0 fusion.58
  20.8 2.5 %fusion.5 = f32[2,512,512]{2,1,0:T(8,128)S(1)} fusion(f32[2,512,512]{2,1,0:T(8,128)S(1)} %fusion.58, f32[512,512]{1,0:T(8,128)S(1)} %fusion.19, f32[1,2,512,512]{3,2,1,0:T(8,128)S(1)} %copy-done.1, f32[2]{0:T(128)S(1)} %get-tuple-element.100), kind=kOutput, calls=%fused_computation.11 | convolution fusion | flops 1613234176 | bytes 7340040 | tf_op jit(solution)/shard_map/sij,sjk->sik/dot_general | solution.py:21
  23.3 2.3 multiply_subtract_fusion
  25.7 3.3 %fusion.76 = f32[2,512,512]{2,1,0:T(8,128)} fusion(f32[2,512,512]{2,1,0:T(8,128)S(1)} %multiply_subtract_fusion), kind=kOutput, calls=%fused_computation.211 | convolution fusion | flops 1610612736 | bytes 4194304 | tf_op jit(solution)/shard_map/sij,sjk->sik/dot_general | solution.py:21
  28.9 3.3 %fusion.57 = f32[2,512,512]{2,1,0:T(8,128)} fusion(f32[2,512,512]{2,1,0:T(8,128)S(1)} %multiply_subtract_fusion, f32[1,2,512,512]{3,2,1,0:T(8,128)S(1)} %copy-done.2, f32[2]{0:T(128)S(1)} %get-tuple-element.100), kind=kOutput, calls=%fused_computation.194 | convolution fusion | flops 1611137024 | bytes 6291464 | tf_op jit(solution)/shard_map/sij,sjk->sik/dot_general | solution.py:21
  32.9 5.8 %fusion.77 = f32[2,512,512]{2,1,0:T(8,128)} fusion(f32[2,512,512]{2,1,0:T(8,128)} %fusion.76), kind=kOutput, calls=%fused_computation.212 | convolution fusion | flops 1610612736 | bytes 4194304 | tf_op jit(solution)/shard_map/sij,sjk->sik/dot_general | solution.py:21
  38.7 1.4 add_convert_fusion
  40.1 4.3 %multiply_multiply_fusion = f32[2,512,512]{2,1,0:T(8,128)S(1)} fusion(f32[2,512,512]{2,1,0:T(8,128)S(1)} %multiply_subtract_fusion, f32[2,512,512]{2,1,0:T(8,128)} %fusion.77, f32[2,512,512]{2,1,0:T(8,128)} %fusion.57, f32[2]{0:T(128)S(1)} %add_convert_fusion, f32[2]{0:T(128)S(1)} %get-tuple-element.99), kind=kOutput, calls=%fused_computation.5 | convolution fusion | flops 1613234176 | bytes 8388624 | tf_op jit(solution)/shard_map/sij,sjk->sik/dot_general | solution.py:21
  47.1 2.1 dynamic-slice_dynamic-update-slice_fusion.3
  64.1 1.8 collective-permute-start.16
  77.2 1.8 collective-permute-start.9
  79.0 2.1 collective-permute-start.10
  81.2 1.2 collective-permute-start.4
  82.4 1.8 collective-permute-start.5
  84.6 2.0 collective-permute-start.1
  87.5 2.3 collective-permute-done.3
  90.4 1.2 collective-permute-done.5
  91.8 5.2 %collective-permute-done = bf16[256,256]{0,1:T(8,128)(2,1)S(1)} collective-permute-done((bf16[256,256]{0,1:T(8,128)(2,1)S(1)}, bf16[256,256]{0,1:T(8,128)(2,1)S(1)}, u32[]{:S(2)}, u32[]{:S(2)}) %collective-permute-start) | collective-permute-done | bytes 131104 | tf_op jit(solution)/shard_map/ppermute | solution.py:13
  97.2 5.5 %collective-permute-start.23 = (bf16[384,512]{1,0:T(8,128)(2,1)S(1)}, bf16[384,512]{1,0:T(8,128)(2,1)S(1)}, u32[]{:S(2)}, u32[]{:S(2)}) collective-permute-start(bf16[384,512]{1,0:T(8,128)(2,1)S(1)} %pad_maximum_fusion.4), channel_id=1, source_target_pairs={{0,1},{1,0},{2,3},{3,2},{4,5},{5,4},{6,7},{7,6},{8,9},{9,8},{10,11... | collective-permute-start | bytes 1179656 | tf_op jit(solution)/shard_map/ppermute | solution.py:13
  102.7 2.0 collective-permute-start.11
  107.2 4.3 %collective-permute-done.47 = bf16[64,512]{1,0:T(8,128)(2,1)S(1)} collective-permute-done((bf16[64,512]{1,0:T(8,128)(2,1)S(1)}, bf16[64,512]{1,0:T(8,128)(2,1)S(1)}, u32[]{:S(2)}, u32[]{:S(2)}) %collective-permute-start.47) | collective-permute-done | bytes 65568 | tf_op jit(solution)/shard_map/ppermute | solution.py:13
  111.6 5.8 %collective-permute-done.48 = bf16[64,512]{1,0:T(8,128)(2,1)S(1)} collective-permute-done((bf16[64,512]{1,0:T(8,128)(2,1)S(1)}, bf16[64,512]{1,0:T(8,128)(2,1)S(1)}, u32[]{:S(2)}, u32[]{:S(2)}) %collective-permute-start.48) | collective-permute-done | bytes 65568 | tf_op jit(solution)/shard_map/ppermute | solution.py:13
  117.4 6.8 %collective-permute-done.49 = bf16[64,512]{1,0:T(8,128)(2,1)S(1)} collective-permute-done((bf16[64,512]{1,0:T(8,128)(2,1)S(1)}, bf16[64,512]{1,0:T(8,128)(2,1)S(1)}, u32[]{:S(2)}, u32[]{:S(2)}) %collective-permute-start.49) | collective-permute-done | bytes 65568 | tf_op jit(solution)/shard_map/ppermute | solution.py:13
  124.1 3.3 %collective-permute-start.50 = (bf16[64,512]{1,0:T(8,128)(2,1)S(1)}, bf16[64,512]{1,0:T(8,128)(2,1)S(1)}, u32[]{:S(2)}, u32[]{:S(2)}) collective-permute-start(bf16[64,512]{1,0:T(8,128)(2,1)S(1)} %get-tuple-element.46), channel_id=1, source_target_pairs={{0,128},{32,160},{64,192},{96,224},{128,0},{160,32},{192,64},{224,... | collective-permute-start | bytes 196616 | tf_op jit(solution)/shard_map/ppermute | solution.py:13
  127.4 4.4 %collective-permute-done.50 = bf16[64,512]{1,0:T(8,128)(2,1)S(1)} collective-permute-done((bf16[64,512]{1,0:T(8,128)(2,1)S(1)}, bf16[64,512]{1,0:T(8,128)(2,1)S(1)}, u32[]{:S(2)}, u32[]{:S(2)}) %collective-permute-start.50) | collective-permute-done | bytes 65568 | tf_op jit(solution)/shard_map/ppermute | solution.py:13
  132.5 5.5 %collective-permute-done.51 = bf16[64,512]{1,0:T(8,128)(2,1)S(1)} collective-permute-done((bf16[64,512]{1,0:T(8,128)(2,1)S(1)}, bf16[64,512]{1,0:T(8,128)(2,1)S(1)}, u32[]{:S(2)}, u32[]{:S(2)}) %collective-permute-start.51) | collective-permute-done | bytes 65568 | tf_op jit(solution)/shard_map/ppermute | solution.py:13
  138.1 1.0 collective-permute-start.52
  139.1 4.0 %collective-permute-done.52 = bf16[64,512]{1,0:T(8,128)(2,1)S(1)} collective-permute-done((bf16[64,512]{1,0:T(8,128)(2,1)S(1)}, bf16[64,512]{1,0:T(8,128)(2,1)S(1)}, u32[]{:S(2)}, u32[]{:S(2)}) %collective-permute-start.52) | collective-permute-done | bytes 65568 | tf_op jit(solution)/shard_map/ppermute | solution.py:13
  143.1 2.0 collective-permute-start.53
  145.1 1.9 collective-permute-done.53
  147.1 2.6 %collective-permute-start.54 = (bf16[64,512]{1,0:T(8,128)(2,1)S(1)}, bf16[64,512]{1,0:T(8,128)(2,1)S(1)}, u32[]{:S(2)}, u32[]{:S(2)}) collective-permute-start(bf16[64,512]{1,0:T(8,128)(2,1)S(1)} %get-tuple-element.41), channel_id=1, source_target_pairs={{0,6},{2,0},{4,2},{6,4},{1,7},{3,1},{5,3},{7,5},{8,14},{10,8},{12,... | collective-permute-start | bytes 196616 | tf_op jit(solution)/shard_map/ppermute | solution.py:13
  150.2 2.4 collective-permute-start.25
  153.1 4.3 %collective-permute-start.19 = (bf16[128,512]{1,0:T(8,128)(2,1)S(1)}, bf16[128,512]{1,0:T(8,128)(2,1)S(1)}, u32[]{:S(2)}, u32[]{:S(2)}) collective-permute-start(bf16[128,512]{1,0:T(8,128)(2,1)S(1)} %get-tuple-element.65), channel_id=1, source_target_pairs={{0,224},{32,0},{64,32},{96,64},{128,96},{160,128},{192,160},{224,1... | collective-permute-start | bytes 393224 | tf_op jit(solution)/shard_map/ppermute | solution.py:13
  158.8 4.5 %collective-permute-start.13 = (bf16[128,512]{1,0:T(8,128)(2,1)S(1)}, bf16[128,512]{1,0:T(8,128)(2,1)S(1)}, u32[]{:S(2)}, u32[]{:S(2)}) collective-permute-start(bf16[128,512]{1,0:T(8,128)(2,1)S(1)} %get-tuple-element.63), channel_id=1, source_target_pairs={{0,160},{32,192},{64,224},{96,0},{128,32},{160,64},{192,96},{224,1... | collective-permute-start | bytes 393224 | tf_op jit(solution)/shard_map/ppermute | solution.py:13
  163.3 1.6 collective-permute-start.7
  165.6 2.7 %collective-permute-done.18 = bf16[128,512]{1,0:T(8,128)(2,1)S(1)} collective-permute-done((bf16[128,512]{1,0:T(8,128)(2,1)S(1)}, bf16[128,512]{1,0:T(8,128)(2,1)S(1)}, u32[]{:S(2)}, u32[]{:S(2)}) %collective-permute-start.18) | collective-permute-done | bytes 131104 | tf_op jit(solution)/shard_map/ppermute | solution.py:13
  168.3 1.5 collective-permute-done.13
  169.8 6.4 %collective-permute-done.12 = bf16[128,512]{1,0:T(8,128)(2,1)S(1)} collective-permute-done((bf16[128,512]{1,0:T(8,128)(2,1)S(1)}, bf16[128,512]{1,0:T(8,128)(2,1)S(1)}, u32[]{:S(2)}, u32[]{:S(2)}) %collective-permute-start.12) | collective-permute-done | bytes 131104 | tf_op jit(solution)/shard_map/ppermute | solution.py:13
  176.7 6.9 %collective-permute-start.26 = (bf16[256,512]{1,0:T(8,128)(2,1)S(1)}, bf16[256,512]{1,0:T(8,128)(2,1)S(1)}, u32[]{:S(2)}, u32[]{:S(2)}) collective-permute-start(bf16[256,512]{1,0:T(8,128)(2,1)S(1)} %fusion.27), channel_id=1, source_target_pairs={{0,1},{1,0},{2,3},{3,2},{4,5},{5,4},{6,7},{7,6},{8,9},{9,8},{10,11... | collective-permute-start | bytes 786440 | tf_op jit(solution)/shard_map/ppermute | solution.py:13
  183.6 1.1 collective-permute-done.26
  184.9 1.1 collective-permute-start.29
  186.9 1.2 collective-permute-done.29
  188.1 2.6 %collective-permute-done.28 = bf16[64,512]{1,0:T(8,128)(2,1)S(1)} collective-permute-done((bf16[64,512]{1,0:T(8,128)(2,1)S(1)}, bf16[64,512]{1,0:T(8,128)(2,1)S(1)}, u32[]{:S(2)}, u32[]{:S(2)}) %collective-permute-start.28) | collective-permute-done | bytes 65568 | tf_op jit(solution)/shard_map/ppermute | solution.py:13
  190.7 1.3 collective-permute-done.27
  192.0 3.3 %collective-permute-start.30 = (bf16[64,512]{1,0:T(8,128)(2,1)S(1)}, bf16[64,512]{1,0:T(8,128)(2,1)S(1)}, u32[]{:S(2)}, u32[]{:S(2)}) collective-permute-start(bf16[64,512]{1,0:T(8,128)(2,1)S(1)} %get-tuple-element.24), channel_id=1, source_target_pairs={{0,32},{32,64},{64,96},{96,128},{128,160},{160,192},{192,224},{224... | collective-permute-start | bytes 196616 | tf_op jit(solution)/shard_map/ppermute | solution.py:13
  196.2 4.7 %collective-permute-start.33 = (bf16[64,512]{1,0:T(8,128)(2,1)S(1)}, bf16[64,512]{1,0:T(8,128)(2,1)S(1)}, u32[]{:S(2)}, u32[]{:S(2)}) collective-permute-start(bf16[64,512]{1,0:T(8,128)(2,1)S(1)} %get-tuple-element.24), channel_id=1, source_target_pairs={{0,128},{32,160},{64,192},{96,224},{128,0},{160,32},{192,64},{224,... | collective-permute-start | bytes 196616 | tf_op jit(solution)/shard_map/ppermute | solution.py:13
  200.8 2.3 collective-permute-start.34
  204.0 1.5 collective-permute-start.36
  205.6 1.4 collective-permute-done.34
  207.0 6.1 %collective-permute-done.35 = bf16[64,512]{1,0:T(8,128)(2,1)S(1)} collective-permute-done((bf16[64,512]{1,0:T(8,128)(2,1)S(1)}, bf16[64,512]{1,0:T(8,128)(2,1)S(1)}, u32[]{:S(2)}, u32[]{:S(2)}) %collective-permute-start.35) | collective-permute-done | bytes 65568 | tf_op jit(solution)/shard_map/ppermute | solution.py:13
  213.1 5.0 %dynamic-slice_select_fusion.7 = (bf16[1,64,512]{2,1,0:T(8,128)(2,1)S(1)}, bf16[1,64,512]{2,1,0:T(8,128)(2,1)S(1)}, bf16[1,64,512]{2,1,0:T(8,128)(2,1)S(1)}, bf1...) fusion(bf16[8,64,512]{2,1,0:T(8,128)(2,1)S(1)} %constant_dynami, ...), kind=kLoop, calls=%fused_computation.157 | loop fusion | flops 262144 | bytes 1048616 | tf_op jit(solution)/shard_map/jit(_where)/select_n | solution.py:121
  218.2 1.2 collective-permute-start.39
  219.4 2.4 collective-permute-start.38
  222.2 2.6 %collective-permute-done.38 = bf16[2,64,512]{2,1,0:T(8,128)(2,1)S(1)} collective-permute-done((bf16[2,64,512]{2,1,0:T(8,128)(2,1)S(1)}, bf16[2,64,512]{2,1,0:T(8,128)(2,1)S(1)}, u32[]{:S(2)}, u32[]{:S(2)}) %collective-permute-start.38) | collective-permute-done | bytes 131104 | tf_op jit(solution)/shard_map/ppermute | solution.py:13
  224.8 4.3 %collective-permute-done.37 = bf16[2,64,512]{2,1,0:T(8,128)(2,1)S(1)} collective-permute-done((bf16[2,64,512]{2,1,0:T(8,128)(2,1)S(1)}, bf16[2,64,512]{2,1,0:T(8,128)(2,1)S(1)}, u32[]{:S(2)}, u32[]{:S(2)}) %collective-permute-start.37) | collective-permute-done | bytes 131104 | tf_op jit(solution)/shard_map/ppermute | solution.py:13
  229.9 1.9 collective-permute-start.57
  233.1 5.3 %collective-permute-done.41 = bf16[2,64,512]{2,1,0:T(8,128)(2,1)S(1)} collective-permute-done((bf16[2,64,512]{2,1,0:T(8,128)(2,1)S(1)}, bf16[2,64,512]{2,1,0:T(8,128)(2,1)S(1)}, u32[]{:S(2)}, u32[]{:S(2)}) %collective-permute-start.41) | collective-permute-done | bytes 131104 | tf_op jit(solution)/shard_map/ppermute | solution.py:13
  238.4 3.2 %collective-permute-done.42 = bf16[2,64,512]{2,1,0:T(8,128)(2,1)S(1)} collective-permute-done((bf16[2,64,512]{2,1,0:T(8,128)(2,1)S(1)}, bf16[2,64,512]{2,1,0:T(8,128)(2,1)S(1)}, u32[]{:S(2)}, u32[]{:S(2)}) %collective-permute-start.42) | collective-permute-done | bytes 131104 | tf_op jit(solution)/shard_map/ppermute | solution.py:13
  242.2 1.0 fusion.12
  244.8 1.9 add_multiply_fusion
  (184 shorter events, 27.6 us)
Async XLA Ops:
  0.6 10.0 %copy-start = (s32[32]{0:T(128)S(1)}, s32[32]{0:T(128)}, u32[]{:S(2)}) copy-start(s32[32]{0:T(128)} %param.6) | copy-start | bytes 388
  3.4 15.0 %copy-start.1 = (f32[1,2,512,512]{3,2,1,0:T(8,128)S(1)}, f32[1,2,512,512]{3,2,1,0:T(8,128)}, u32[]{:S(2)}) copy-start(f32[1,2,512,512]{3,2,1,0:T(8,128)} %param.7) | copy-start | bytes 6291460
  3.4 60.7 %collective-permute-start.20 = (bf16[128,512]{1,0:T(8,128)(2,1)S(1)}, bf16[128,512]{1,0:T(8,128)(2,1)S(1)}, u32[]{:S(2)}, u32[]{:S(2)}) collective-permute-start(bf16[128,512]{1,0:T(8,128)(2,1)S(1)} %get-tuple-element.26), channel_id=1, source_target_pairs={{0,8},{8,16},{16,24},{24,0},{1,9},{9,17},{17,25},{25,1},{2,10},{10... | collective-permute-start | bytes 393224 | tf_op jit(solution)/shard_map/ppermute | solution.py:13
  5.6 60.3 %collective-permute-start.21 = (bf16[128,512]{1,0:T(8,128)(2,1)}, bf16[128,512]{1,0:T(8,128)(2,1)S(1)}, u32[]{:S(2)}, u32[]{:S(2)}) collective-permute-start(bf16[128,512]{1,0:T(8,128)(2,1)} %get-tuple-element.36), channel_id=1, source_target_pairs={{0,16},{8,24},{16,0},{24,8},{1,17},{9,25},{17,1},{25,9},{2,18},{10... | collective-permute-start | bytes 393224 | tf_op jit(solution)/shard_map/ppermute | solution.py:13
  8.2 69.0 %collective-permute-start.22 = (bf16[128,512]{1,0:T(8,128)(2,1)}, bf16[128,512]{1,0:T(8,128)(2,1)S(1)}, u32[]{:S(2)}, u32[]{:S(2)}) collective-permute-start(bf16[128,512]{1,0:T(8,128)(2,1)} %get-tuple-element.35), channel_id=1, source_target_pairs={{0,24},{8,0},{16,8},{24,16},{1,25},{9,1},{17,9},{25,17},{2,26},{10... | collective-permute-start | bytes 393224 | tf_op jit(solution)/shard_map/ppermute | solution.py:13
  9.3 69.7 %collective-permute-start.14 = (bf16[128,512]{1,0:T(8,128)(2,1)}, bf16[128,512]{1,0:T(8,128)(2,1)S(1)}, u32[]{:S(2)}, u32[]{:S(2)}) collective-permute-start(bf16[128,512]{1,0:T(8,128)(2,1)} %get-tuple-element.29), channel_id=1, source_target_pairs={{0,8},{8,16},{16,24},{24,0},{1,9},{9,17},{17,25},{25,1},{2,10},{10... | collective-permute-start | bytes 393224 | tf_op jit(solution)/shard_map/ppermute | solution.py:13
  9.7 71.4 %collective-permute-start.15 = (bf16[128,512]{1,0:T(8,128)(2,1)}, bf16[128,512]{1,0:T(8,128)(2,1)S(1)}, u32[]{:S(2)}, u32[]{:S(2)}) collective-permute-start(bf16[128,512]{1,0:T(8,128)(2,1)} %get-tuple-element.28), channel_id=1, source_target_pairs={{0,16},{8,24},{16,0},{24,8},{1,17},{9,25},{17,1},{25,9},{2,18},{10... | collective-permute-start | bytes 393224 | tf_op jit(solution)/shard_map/ppermute | solution.py:13
  44.4 19.5 %copy-start.8 = (bf16[2,256,128]{2,1,0:T(8,128)(2,1)S(1)}, bf16[2,256,128]{2,1,0:T(8,128)(2,1)}, u32[]{:S(2)}) copy-start(bf16[2,256,128]{2,1,0:T(8,128)(2,1)} %param.5) | copy-start | bytes 393220
  64.1 17.1 %collective-permute-start.16 = (bf16[128,512]{1,0:T(8,128)(2,1)}, bf16[128,512]{1,0:T(8,128)(2,1)S(1)}, u32[]{:S(2)}, u32[]{:S(2)}) collective-permute-start(bf16[128,512]{1,0:T(8,128)(2,1)} %get-tuple-element.27), channel_id=1, source_target_pairs={{0,24},{8,0},{16,8},{24,16},{1,25},{9,1},{17,9},{25,17},{2,26},{10... | collective-permute-start | bytes 393224 | tf_op jit(solution)/shard_map/ppermute | solution.py:13
  65.9 16.5 %collective-permute-start.8 = (bf16[128,512]{1,0:T(8,128)(2,1)}, bf16[128,512]{1,0:T(8,128)(2,1)}, u32[]{:S(2)}, u32[]{:S(2)}) collective-permute-start(bf16[128,512]{1,0:T(8,128)(2,1)} %get-tuple-element.32), channel_id=1, source_target_pairs={{0,8},{8,16},{16,24},{24,0},{1,9},{9,17},{17,25},{25,1},{2,10},{10... | collective-permute-start | bytes 393224 | tf_op jit(solution)/shard_map/ppermute | solution.py:13
  77.2 12.6 %copy-start.9 = (bf16[2,64,512]{2,1,0:T(8,128)(2,1)S(1)}, bf16[2,64,512]{2,1,0:T(8,128)(2,1)}, u32[]{:S(2)}) copy-start(bf16[2,64,512]{2,1,0:T(8,128)(2,1)} %dynamic-slice_convert_fusion.1) | copy-start | bytes 393220
  77.2 27.5 %copy-start.7 = (bf16[1,2,64,512]{3,2,1,0:T(8,128)(2,1)S(1)}, bf16[1,2,64,512]{3,2,1,0:T(8,128)(2,1)}, u32[]{:S(2)}) copy-start(bf16[1,2,64,512]{3,2,1,0:T(8,128)(2,1)} %fusion.97) | copy-start | bytes 393220
  77.2 7.0 %collective-permute-start.9 = (bf16[128,512]{1,0:T(8,128)(2,1)}, bf16[128,512]{1,0:T(8,128)(2,1)S(1)}, u32[]{:S(2)}, u32[]{:S(2)}) collective-permute-start(bf16[128,512]{1,0:T(8,128)(2,1)} %get-tuple-element.31), channel_id=1, source_target_pairs={{0,16},{8,24},{16,0},{24,8},{1,17},{9,25},{17,1},{25,9},{2,18},{10... | collective-permute-start | bytes 393224 | tf_op jit(solution)/shard_map/ppermute | solution.py:13
  79.0 5.6 %collective-permute-start.10 = (bf16[128,512]{1,0:T(8,128)(2,1)}, bf16[128,512]{1,0:T(8,128)(2,1)S(1)}, u32[]{:S(2)}, u32[]{:S(2)}) collective-permute-start(bf16[128,512]{1,0:T(8,128)(2,1)} %get-tuple-element.30), channel_id=1, source_target_pairs={{0,24},{8,0},{16,8},{24,16},{1,25},{9,1},{17,9},{25,17},{2,26},{10... | collective-permute-start | bytes 393224 | tf_op jit(solution)/shard_map/ppermute | solution.py:13
  81.1 8.7 %collective-permute-start.3 = (bf16[128,512]{1,0:T(8,128)(2,1)}, bf16[128,512]{1,0:T(8,128)(2,1)S(1)}, u32[]{:S(2)}, u32[]{:S(2)}) collective-permute-start(bf16[128,512]{1,0:T(8,128)(2,1)} %get-tuple-element.34), channel_id=1, source_target_pairs={{0,8},{8,16},{16,24},{24,0},{1,9},{9,17},{17,25},{25,1},{2,10},{10... | collective-permute-start | bytes 393224 | tf_op jit(solution)/shard_map/ppermute | solution.py:13
  81.2 8.6 %collective-permute-start.4 = (bf16[128,512]{1,0:T(8,128)(2,1)}, bf16[128,512]{1,0:T(8,128)(2,1)S(1)}, u32[]{:S(2)}, u32[]{:S(2)}) collective-permute-start(bf16[128,512]{1,0:T(8,128)(2,1)} %get-tuple-element.33), channel_id=1, source_target_pairs={{0,16},{8,24},{16,0},{24,8},{1,17},{9,25},{17,1},{25,9},{2,18},{10... | collective-permute-start | bytes 393224 | tf_op jit(solution)/shard_map/ppermute | solution.py:13
  82.4 9.2 %collective-permute-start.5 = (bf16[128,512]{1,0:T(8,128)(2,1)}, bf16[128,512]{1,0:T(8,128)(2,1)S(1)}, u32[]{:S(2)}, u32[]{:S(2)}) collective-permute-start(bf16[128,512]{1,0:T(8,128)(2,1)} %get-tuple-element.25), channel_id=1, source_target_pairs={{0,24},{8,0},{16,8},{24,16},{1,25},{9,1},{17,9},{25,17},{2,26},{10... | collective-permute-start | bytes 393224 | tf_op jit(solution)/shard_map/ppermute | solution.py:13
  84.2 21.9 %copy-start.5 = (bf16[1024,512]{1,0:T(8,128)(2,1)S(1)}, bf16[1024,512]{1,0:T(8,128)(2,1)}, u32[]{:S(2)}) copy-start(bf16[1024,512]{1,0:T(8,128)(2,1)} %get-tuple-element.38) | copy-start | bytes 3145732
  84.2 12.8 %collective-permute-start = (bf16[256,256]{0,1:T(8,128)(2,1)S(1)}, bf16[256,256]{0,1:T(8,128)(2,1)S(1)}, u32[]{:S(2)}, u32[]{:S(2)}) collective-permute-start(bf16[256,256]{0,1:T(8,128)(2,1)S(1)} %bitcast.219), channel_id=1, source_target_pairs={{0,8},{8,16},{16,24},{24,0},{1,9},{9,17},{17,25},{25,1},{2,10},{10... | collective-permute-start | bytes 393224 | tf_op jit(solution)/shard_map/ppermute | solution.py:13
  84.6 20.2 %collective-permute-start.1 = (bf16[256,256]{0,1:T(8,128)(2,1)S(1)}, bf16[256,256]{0,1:T(8,128)(2,1)S(1)}, u32[]{:S(2)}, u32[]{:S(2)}) collective-permute-start(bf16[256,256]{0,1:T(8,128)(2,1)S(1)} %bitcast.220), channel_id=1, source_target_pairs={{0,16},{8,24},{16,0},{24,8},{1,17},{9,25},{17,1},{25,9},{2,18},{10... | collective-permute-start | bytes 393224 | tf_op jit(solution)/shard_map/ppermute | solution.py:13
  89.8 7.4 %collective-permute-start.46 = (bf16[2,64,512]{2,1,0:T(8,128)(2,1)S(1)}, bf16[2,64,512]{2,1,0:T(8,128)(2,1)S(1)}, u32[]{:S(2)}, u32[]{:S(2)}) collective-permute-start(bf16[2,64,512]{2,1,0:T(8,128)(2,1)S(1)} %copy-done.9), channel_id=1, source_target_pairs={{0,24},{8,0},{16,8},{24,16},{1,25},{9,1},{17,9},{25,17},{2,26},{10... | collective-permute-start | bytes 393224 | tf_op jit(solution)/shard_map/ppermute | solution.py:13
  89.8 12.9 %collective-permute-start.45 = (bf16[2,64,512]{2,1,0:T(8,128)(2,1)S(1)}, bf16[2,64,512]{2,1,0:T(8,128)(2,1)S(1)}, u32[]{:S(2)}, u32[]{:S(2)}) collective-permute-start(bf16[2,64,512]{2,1,0:T(8,128)(2,1)S(1)} %copy-done.9), channel_id=1, source_target_pairs={{0,16},{8,24},{16,0},{24,8},{1,17},{9,25},{17,1},{25,9},{2,18},{10... | collective-permute-start | bytes 393224 | tf_op jit(solution)/shard_map/ppermute | solution.py:13
  91.6 11.2 %collective-permute-start.44 = (bf16[2,64,512]{2,1,0:T(8,128)(2,1)S(1)}, bf16[2,64,512]{2,1,0:T(8,128)(2,1)S(1)}, u32[]{:S(2)}, u32[]{:S(2)}) collective-permute-start(bf16[2,64,512]{2,1,0:T(8,128)(2,1)S(1)} %copy-done.9), channel_id=1, source_target_pairs={{0,8},{8,16},{16,24},{24,0},{1,9},{9,17},{17,25},{25,1},{2,10},{10... | collective-permute-start | bytes 393224 | tf_op jit(solution)/shard_map/ppermute | solution.py:13
  97.0 8.0 %collective-permute-start.2 = (bf16[256,256]{0,1:T(8,128)(2,1)S(1)}, bf16[256,256]{0,1:T(8,128)(2,1)S(1)}, u32[]{:S(2)}, u32[]{:S(2)}) collective-permute-start(bf16[256,256]{0,1:T(8,128)(2,1)S(1)} %bitcast.221), channel_id=1, source_target_pairs={{0,24},{8,0},{16,8},{24,16},{1,25},{9,1},{17,9},{25,17},{2,26},{10... | collective-permute-start | bytes 393224 | tf_op jit(solution)/shard_map/ppermute | solution.py:13
  97.2 52.4 %collective-permute-start.23 = (bf16[384,512]{1,0:T(8,128)(2,1)S(1)}, bf16[384,512]{1,0:T(8,128)(2,1)S(1)}, u32[]{:S(2)}, u32[]{:S(2)}) collective-permute-start(bf16[384,512]{1,0:T(8,128)(2,1)S(1)} %pad_maximum_fusion.4), channel_id=1, source_target_pairs={{0,1},{1,0},{2,3},{3,2},{4,5},{5,4},{6,7},{7,6},{8,9},{9,8},{10,11... | collective-permute-start | bytes 1179656 | tf_op jit(solution)/shard_map/ppermute | solution.py:13
  102.7 49.8 %collective-permute-start.17 = (bf16[384,512]{1,0:T(8,128)(2,1)S(1)}, bf16[384,512]{1,0:T(8,128)(2,1)S(1)}, u32[]{:S(2)}, u32[]{:S(2)}) collective-permute-start(bf16[384,512]{1,0:T(8,128)(2,1)S(1)} %pad_maximum_fusion.3), channel_id=1, source_target_pairs={{0,1},{1,0},{2,3},{3,2},{4,5},{5,4},{6,7},{7,6},{8,9},{9,8},{10,11... | collective-permute-start | bytes 1179656 | tf_op jit(solution)/shard_map/ppermute | solution.py:13
  102.7 50.4 %collective-permute-start.11 = (bf16[384,512]{1,0:T(8,128)(2,1)S(1)}, bf16[384,512]{1,0:T(8,128)(2,1)S(1)}, u32[]{:S(2)}, u32[]{:S(2)}) collective-permute-start(bf16[384,512]{1,0:T(8,128)(2,1)S(1)} %pad_maximum_fusion.2), channel_id=1, source_target_pairs={{0,1},{1,0},{2,3},{3,2},{4,5},{5,4},{6,7},{7,6},{8,9},{9,8},{10,11... | collective-permute-start | bytes 1179656 | tf_op jit(solution)/shard_map/ppermute | solution.py:13
  104.8 53.1 %collective-permute-start.6 = (bf16[384,512]{1,0:T(8,128)(2,1)S(1)}, bf16[384,512]{1,0:T(8,128)(2,1)S(1)}, u32[]{:S(2)}, u32[]{:S(2)}) collective-permute-start(bf16[384,512]{1,0:T(8,128)(2,1)S(1)} %pad_maximum_fusion.1), channel_id=1, source_target_pairs={{0,1},{1,0},{2,3},{3,2},{4,5},{5,4},{6,7},{7,6},{8,9},{9,8},{10,11... | collective-permute-start | bytes 1179656 | tf_op jit(solution)/shard_map/ppermute | solution.py:13
  105.0 6.5 %collective-permute-start.47 = (bf16[64,512]{1,0:T(8,128)(2,1)S(1)}, bf16[64,512]{1,0:T(8,128)(2,1)S(1)}, u32[]{:S(2)}, u32[]{:S(2)}) collective-permute-start(bf16[64,512]{1,0:T(8,128)(2,1)S(1)} %get-tuple-element.49), channel_id=1, source_target_pairs={{0,32},{32,64},{64,96},{96,128},{128,160},{160,192},{192,224},{224... | collective-permute-start | bytes 196616 | tf_op jit(solution)/shard_map/ppermute | solution.py:13
  111.6 5.8 %collective-permute-start.48 = (bf16[64,512]{1,0:T(8,128)(2,1)S(1)}, bf16[64,512]{1,0:T(8,128)(2,1)S(1)}, u32[]{:S(2)}, u32[]{:S(2)}) collective-permute-start(bf16[64,512]{1,0:T(8,128)(2,1)S(1)} %get-tuple-element.48), channel_id=1, source_target_pairs={{0,64},{32,96},{64,128},{96,160},{128,192},{160,224},{192,0},{224,... | collective-permute-start | bytes 196616 | tf_op jit(solution)/shard_map/ppermute | solution.py:13
  117.4 6.8 %collective-permute-start.49 = (bf16[64,512]{1,0:T(8,128)(2,1)S(1)}, bf16[64,512]{1,0:T(8,128)(2,1)S(1)}, u32[]{:S(2)}, u32[]{:S(2)}) collective-permute-start(bf16[64,512]{1,0:T(8,128)(2,1)S(1)} %get-tuple-element.47), channel_id=1, source_target_pairs={{0,96},{32,128},{64,160},{96,192},{128,224},{160,0},{192,32},{224,... | collective-permute-start | bytes 196616 | tf_op jit(solution)/shard_map/ppermute | solution.py:13
  124.1 7.7 %collective-permute-start.50 = (bf16[64,512]{1,0:T(8,128)(2,1)S(1)}, bf16[64,512]{1,0:T(8,128)(2,1)S(1)}, u32[]{:S(2)}, u32[]{:S(2)}) collective-permute-start(bf16[64,512]{1,0:T(8,128)(2,1)S(1)} %get-tuple-element.46), channel_id=1, source_target_pairs={{0,128},{32,160},{64,192},{96,224},{128,0},{160,32},{192,64},{224,... | collective-permute-start | bytes 196616 | tf_op jit(solution)/shard_map/ppermute | solution.py:13
  131.8 6.3 %collective-permute-start.51 = (bf16[64,512]{1,0:T(8,128)(2,1)S(1)}, bf16[64,512]{1,0:T(8,128)(2,1)S(1)}, u32[]{:S(2)}, u32[]{:S(2)}) collective-permute-start(bf16[64,512]{1,0:T(8,128)(2,1)S(1)} %get-tuple-element.45), channel_id=1, source_target_pairs={{0,160},{32,192},{64,224},{96,0},{128,32},{160,64},{192,96},{224,1... | collective-permute-start | bytes 196616 | tf_op jit(solution)/shard_map/ppermute | solution.py:13
  138.1 5.0 %collective-permute-start.52 = (bf16[64,512]{1,0:T(8,128)(2,1)S(1)}, bf16[64,512]{1,0:T(8,128)(2,1)S(1)}, u32[]{:S(2)}, u32[]{:S(2)}) collective-permute-start(bf16[64,512]{1,0:T(8,128)(2,1)S(1)} %get-tuple-element.44), channel_id=1, source_target_pairs={{0,192},{32,224},{64,0},{96,32},{128,64},{160,96},{192,128},{224,1... | collective-permute-start | bytes 196616 | tf_op jit(solution)/shard_map/ppermute | solution.py:13
  143.1 3.9 %collective-permute-start.53 = (bf16[64,512]{1,0:T(8,128)(2,1)S(1)}, bf16[64,512]{1,0:T(8,128)(2,1)S(1)}, u32[]{:S(2)}, u32[]{:S(2)}) collective-permute-start(bf16[64,512]{1,0:T(8,128)(2,1)S(1)} %get-tuple-element.43), channel_id=1, source_target_pairs={{0,224},{32,0},{64,32},{96,64},{128,96},{160,128},{192,160},{224,1... | collective-permute-start | bytes 196616 | tf_op jit(solution)/shard_map/ppermute | solution.py:13
  147.1 11.7 %collective-permute-start.54 = (bf16[64,512]{1,0:T(8,128)(2,1)S(1)}, bf16[64,512]{1,0:T(8,128)(2,1)S(1)}, u32[]{:S(2)}, u32[]{:S(2)}) collective-permute-start(bf16[64,512]{1,0:T(8,128)(2,1)S(1)} %get-tuple-element.41), channel_id=1, source_target_pairs={{0,6},{2,0},{4,2},{6,4},{1,7},{3,1},{5,3},{7,5},{8,14},{10,8},{12,... | collective-permute-start | bytes 196616 | tf_op jit(solution)/shard_map/ppermute | solution.py:13
  150.2 13.2 %collective-permute-start.25 = (bf16[128,512]{1,0:T(8,128)(2,1)S(1)}, bf16[128,512]{1,0:T(8,128)(2,1)S(1)}, u32[]{:S(2)}, u32[]{:S(2)}) collective-permute-start(bf16[128,512]{1,0:T(8,128)(2,1)S(1)} %get-tuple-element.67), channel_id=1, source_target_pairs={{0,192},{32,224},{64,0},{96,32},{128,64},{160,96},{192,128},{224,1... | collective-permute-start | bytes 393224 | tf_op jit(solution)/shard_map/ppermute | solution.py:13
  152.5 10.8 %collective-permute-start.24 = (bf16[128,512]{1,0:T(8,128)(2,1)S(1)}, bf16[128,512]{1,0:T(8,128)(2,1)S(1)}, u32[]{:S(2)}, u32[]{:S(2)}) collective-permute-start(bf16[128,512]{1,0:T(8,128)(2,1)S(1)} %get-tuple-element.66), channel_id=1, source_target_pairs={{0,64},{32,96},{64,128},{96,160},{128,192},{160,224},{192,0},{224,... | collective-permute-start | bytes 393224 | tf_op jit(solution)/shard_map/ppermute | solution.py:13
  153.1 11.8 %collective-permute-start.19 = (bf16[128,512]{1,0:T(8,128)(2,1)S(1)}, bf16[128,512]{1,0:T(8,128)(2,1)S(1)}, u32[]{:S(2)}, u32[]{:S(2)}) collective-permute-start(bf16[128,512]{1,0:T(8,128)(2,1)S(1)} %get-tuple-element.65), channel_id=1, source_target_pairs={{0,224},{32,0},{64,32},{96,64},{128,96},{160,128},{192,160},{224,1... | collective-permute-start | bytes 393224 | tf_op jit(solution)/shard_map/ppermute | solution.py:13
  157.9 10.4 %collective-permute-start.18 = (bf16[128,512]{1,0:T(8,128)(2,1)S(1)}, bf16[128,512]{1,0:T(8,128)(2,1)S(1)}, u32[]{:S(2)}, u32[]{:S(2)}) collective-permute-start(bf16[128,512]{1,0:T(8,128)(2,1)S(1)} %get-tuple-element.64), channel_id=1, source_target_pairs={{0,96},{32,128},{64,160},{96,192},{128,224},{160,0},{192,32},{224,... | collective-permute-start | bytes 393224 | tf_op jit(solution)/shard_map/ppermute | solution.py:13
  158.8 11.0 %collective-permute-start.13 = (bf16[128,512]{1,0:T(8,128)(2,1)S(1)}, bf16[128,512]{1,0:T(8,128)(2,1)S(1)}, u32[]{:S(2)}, u32[]{:S(2)}) collective-permute-start(bf16[128,512]{1,0:T(8,128)(2,1)S(1)} %get-tuple-element.63), channel_id=1, source_target_pairs={{0,160},{32,192},{64,224},{96,0},{128,32},{160,64},{192,96},{224,1... | collective-permute-start | bytes 393224 | tf_op jit(solution)/shard_map/ppermute | solution.py:13
  163.3 12.9 %collective-permute-start.12 = (bf16[128,512]{1,0:T(8,128)(2,1)S(1)}, bf16[128,512]{1,0:T(8,128)(2,1)S(1)}, u32[]{:S(2)}, u32[]{:S(2)}) collective-permute-start(bf16[128,512]{1,0:T(8,128)(2,1)S(1)} %get-tuple-element.62), channel_id=1, source_target_pairs={{0,32},{32,64},{64,96},{96,128},{128,160},{160,192},{192,224},{224... | collective-permute-start | bytes 393224 | tf_op jit(solution)/shard_map/ppermute | solution.py:13
  163.3 12.9 %collective-permute-start.7 = (bf16[128,512]{1,0:T(8,128)(2,1)S(1)}, bf16[128,512]{1,0:T(8,128)(2,1)S(1)}, u32[]{:S(2)}, u32[]{:S(2)}) collective-permute-start(bf16[128,512]{1,0:T(8,128)(2,1)S(1)} %fusion.35), channel_id=1, source_target_pairs={{0,128},{32,160},{64,192},{96,224},{128,0},{160,32},{192,64},{224,... | collective-permute-start | bytes 393224 | tf_op jit(solution)/shard_map/ppermute | solution.py:13
  164.9 18.7 %collective-permute-start.55 = (bf16[64,512]{1,0:T(8,128)(2,1)S(1)}, bf16[64,512]{1,0:T(8,128)(2,1)S(1)}, u32[]{:S(2)}, u32[]{:S(2)}) collective-permute-start(bf16[64,512]{1,0:T(8,128)(2,1)S(1)} %get-tuple-element.41), channel_id=1, source_target_pairs={{0,4},{2,6},{4,0},{6,2},{1,5},{3,7},{5,1},{7,3},{8,12},{10,14},{12... | collective-permute-start | bytes 196616 | tf_op jit(solution)/shard_map/ppermute | solution.py:13
  168.3 15.3 %collective-permute-start.56 = (bf16[64,512]{1,0:T(8,128)(2,1)S(1)}, bf16[64,512]{1,0:T(8,128)(2,1)S(1)}, u32[]{:S(2)}, u32[]{:S(2)}) collective-permute-start(bf16[64,512]{1,0:T(8,128)(2,1)S(1)} %get-tuple-element.41), channel_id=1, source_target_pairs={{0,2},{2,4},{4,6},{6,0},{1,3},{3,5},{5,7},{7,1},{8,10},{10,12},{12... | collective-permute-start | bytes 196616 | tf_op jit(solution)/shard_map/ppermute | solution.py:13
  176.7 8.1 %collective-permute-start.26 = (bf16[256,512]{1,0:T(8,128)(2,1)S(1)}, bf16[256,512]{1,0:T(8,128)(2,1)S(1)}, u32[]{:S(2)}, u32[]{:S(2)}) collective-permute-start(bf16[256,512]{1,0:T(8,128)(2,1)S(1)} %fusion.27), channel_id=1, source_target_pairs={{0,1},{1,0},{2,3},{3,2},{4,5},{5,4},{6,7},{7,6},{8,9},{9,8},{10,11... | collective-permute-start | bytes 786440 | tf_op jit(solution)/shard_map/ppermute | solution.py:13
  184.9 3.2 %collective-permute-start.29 = (bf16[64,512]{1,0:T(8,128)(2,1)S(1)}, bf16[64,512]{1,0:T(8,128)(2,1)S(1)}, u32[]{:S(2)}, u32[]{:S(2)}) collective-permute-start(bf16[64,512]{1,0:T(8,128)(2,1)S(1)} %get-tuple-element.60), channel_id=1, source_target_pairs={{0,6},{2,0},{4,2},{6,4},{1,7},{3,1},{5,3},{7,5},{8,14},{10,8},{12,... | collective-permute-start | bytes 196616 | tf_op jit(solution)/shard_map/ppermute | solution.py:13
  186.0 4.7 %collective-permute-start.28 = (bf16[64,512]{1,0:T(8,128)(2,1)S(1)}, bf16[64,512]{1,0:T(8,128)(2,1)S(1)}, u32[]{:S(2)}, u32[]{:S(2)}) collective-permute-start(bf16[64,512]{1,0:T(8,128)(2,1)S(1)} %get-tuple-element.61), channel_id=1, source_target_pairs={{0,4},{2,6},{4,0},{6,2},{1,5},{3,7},{5,1},{7,3},{8,12},{10,14},{12... | collective-permute-start | bytes 196616 | tf_op jit(solution)/shard_map/ppermute | solution.py:13
  186.5 5.5 %collective-permute-start.27 = (bf16[64,512]{1,0:T(8,128)(2,1)S(1)}, bf16[64,512]{1,0:T(8,128)(2,1)S(1)}, u32[]{:S(2)}, u32[]{:S(2)}) collective-permute-start(bf16[64,512]{1,0:T(8,128)(2,1)S(1)} %get-tuple-element.59), channel_id=1, source_target_pairs={{0,2},{2,4},{4,6},{6,0},{1,3},{3,5},{5,7},{7,1},{8,10},{10,12},{12... | collective-permute-start | bytes 196616 | tf_op jit(solution)/shard_map/ppermute | solution.py:13
  192.0 11.1 %collective-permute-start.30 = (bf16[64,512]{1,0:T(8,128)(2,1)S(1)}, bf16[64,512]{1,0:T(8,128)(2,1)S(1)}, u32[]{:S(2)}, u32[]{:S(2)}) collective-permute-start(bf16[64,512]{1,0:T(8,128)(2,1)S(1)} %get-tuple-element.24), channel_id=1, source_target_pairs={{0,32},{32,64},{64,96},{96,128},{128,160},{160,192},{192,224},{224... | collective-permute-start | bytes 196616 | tf_op jit(solution)/shard_map/ppermute | solution.py:13
  195.4 8.7 %collective-permute-start.31 = (bf16[64,512]{1,0:T(8,128)(2,1)S(1)}, bf16[64,512]{1,0:T(8,128)(2,1)S(1)}, u32[]{:S(2)}, u32[]{:S(2)}) collective-permute-start(bf16[64,512]{1,0:T(8,128)(2,1)S(1)} %get-tuple-element.24), channel_id=1, source_target_pairs={{0,64},{32,96},{64,128},{96,160},{128,192},{160,224},{192,0},{224,... | collective-permute-start | bytes 196616 | tf_op jit(solution)/shard_map/ppermute | solution.py:13
  196.2 9.4 %collective-permute-start.32 = (bf16[64,512]{1,0:T(8,128)(2,1)S(1)}, bf16[64,512]{1,0:T(8,128)(2,1)S(1)}, u32[]{:S(2)}, u32[]{:S(2)}) collective-permute-start(bf16[64,512]{1,0:T(8,128)(2,1)S(1)} %get-tuple-element.24), channel_id=1, source_target_pairs={{0,96},{32,128},{64,160},{96,192},{128,224},{160,0},{192,32},{224,... | collective-permute-start | bytes 196616 | tf_op jit(solution)/shard_map/ppermute | solution.py:13
  196.2 9.5 %collective-permute-start.33 = (bf16[64,512]{1,0:T(8,128)(2,1)S(1)}, bf16[64,512]{1,0:T(8,128)(2,1)S(1)}, u32[]{:S(2)}, u32[]{:S(2)}) collective-permute-start(bf16[64,512]{1,0:T(8,128)(2,1)S(1)} %get-tuple-element.24), channel_id=1, source_target_pairs={{0,128},{32,160},{64,192},{96,224},{128,0},{160,32},{192,64},{224,... | collective-permute-start | bytes 196616 | tf_op jit(solution)/shard_map/ppermute | solution.py:13
  200.8 6.2 %collective-permute-start.34 = (bf16[64,512]{1,0:T(8,128)(2,1)S(1)}, bf16[64,512]{1,0:T(8,128)(2,1)S(1)}, u32[]{:S(2)}, u32[]{:S(2)}) collective-permute-start(bf16[64,512]{1,0:T(8,128)(2,1)S(1)} %get-tuple-element.24), channel_id=1, source_target_pairs={{0,160},{32,192},{64,224},{96,0},{128,32},{160,64},{192,96},{224,1... | collective-permute-start | bytes 196616 | tf_op jit(solution)/shard_map/ppermute | solution.py:13
  203.1 10.0 %collective-permute-start.35 = (bf16[64,512]{1,0:T(8,128)(2,1)S(1)}, bf16[64,512]{1,0:T(8,128)(2,1)S(1)}, u32[]{:S(2)}, u32[]{:S(2)}) collective-permute-start(bf16[64,512]{1,0:T(8,128)(2,1)S(1)} %get-tuple-element.24), channel_id=1, source_target_pairs={{0,192},{32,224},{64,0},{96,32},{128,64},{160,96},{192,128},{224,1... | collective-permute-start | bytes 196616 | tf_op jit(solution)/shard_map/ppermute | solution.py:13
  204.0 9.1 %collective-permute-start.36 = (bf16[64,512]{1,0:T(8,128)(2,1)S(1)}, bf16[64,512]{1,0:T(8,128)(2,1)S(1)}, u32[]{:S(2)}, u32[]{:S(2)}) collective-permute-start(bf16[64,512]{1,0:T(8,128)(2,1)S(1)} %get-tuple-element.24), channel_id=1, source_target_pairs={{0,224},{32,0},{64,32},{96,64},{128,96},{160,128},{192,160},{224,1... | collective-permute-start | bytes 196616 | tf_op jit(solution)/shard_map/ppermute | solution.py:13
  218.2 4.1 %collective-permute-start.39 = (bf16[2,64,512]{2,1,0:T(8,128)(2,1)S(1)}, bf16[2,64,512]{2,1,0:T(8,128)(2,1)S(1)}, u32[]{:S(2)}, u32[]{:S(2)}) collective-permute-start(bf16[2,64,512]{2,1,0:T(8,128)(2,1)S(1)} %pad_maximum_fusion.7), channel_id=1, source_target_pairs={{0,24},{8,0},{16,8},{24,16},{1,25},{9,1},{17,9},{25,17},{2,26},{10... | collective-permute-start | bytes 393224 | tf_op jit(solution)/shard_map/ppermute | solution.py:13
  219.4 5.4 %collective-permute-start.38 = (bf16[2,64,512]{2,1,0:T(8,128)(2,1)S(1)}, bf16[2,64,512]{2,1,0:T(8,128)(2,1)S(1)}, u32[]{:S(2)}, u32[]{:S(2)}) collective-permute-start(bf16[2,64,512]{2,1,0:T(8,128)(2,1)S(1)} %pad_maximum_fusion.6), channel_id=1, source_target_pairs={{0,16},{8,24},{16,0},{24,8},{1,17},{9,25},{17,1},{25,9},{2,18},{10... | collective-permute-start | bytes 393224 | tf_op jit(solution)/shard_map/ppermute | solution.py:13
  221.8 7.3 %collective-permute-start.37 = (bf16[2,64,512]{2,1,0:T(8,128)(2,1)S(1)}, bf16[2,64,512]{2,1,0:T(8,128)(2,1)S(1)}, u32[]{:S(2)}, u32[]{:S(2)}) collective-permute-start(bf16[2,64,512]{2,1,0:T(8,128)(2,1)S(1)} %pad_maximum_fusion.5), channel_id=1, source_target_pairs={{0,8},{8,16},{16,24},{24,0},{1,9},{9,17},{17,25},{25,1},{2,10},{10... | collective-permute-start | bytes 393224 | tf_op jit(solution)/shard_map/ppermute | solution.py:13
  229.2 3.9 %collective-permute-start.40 = (bf16[2,64,512]{2,1,0:T(8,128)(2,1)S(1)}, bf16[2,64,512]{2,1,0:T(8,128)(2,1)S(1)}, u32[]{:S(2)}, u32[]{:S(2)}) collective-permute-start(bf16[2,64,512]{2,1,0:T(8,128)(2,1)S(1)} %get-tuple-element.6), channel_id=1, source_target_pairs={{0,6},{2,0},{4,2},{6,4},{1,7},{3,1},{5,3},{7,5},{8,14},{10,8},{12,... | collective-permute-start | bytes 393224 | tf_op jit(solution)/shard_map/ppermute | solution.py:13
  229.9 12.4 %collective-permute-start.57 = (bf16[256,512]{1,0:T(8,128)(2,1)S(1)}, bf16[256,512]{1,0:T(8,128)(2,1)S(1)}, u32[]{:S(2)}, u32[]{:S(2)}) collective-permute-start(bf16[256,512]{1,0:T(8,128)(2,1)S(1)} %bitcast.223), channel_id=1, source_target_pairs={{0,1},{1,0},{2,3},{3,2},{4,5},{5,4},{6,7},{7,6},{8,9},{9,8},{10,11... | collective-permute-start | bytes 786440 | tf_op jit(solution)/shard_map/ppermute | solution.py:13
  231.7 6.6 %collective-permute-start.41 = (bf16[2,64,512]{2,1,0:T(8,128)(2,1)S(1)}, bf16[2,64,512]{2,1,0:T(8,128)(2,1)S(1)}, u32[]{:S(2)}, u32[]{:S(2)}) collective-permute-start(bf16[2,64,512]{2,1,0:T(8,128)(2,1)S(1)} %get-tuple-element.6), channel_id=1, source_target_pairs={{0,4},{2,6},{4,0},{6,2},{1,5},{3,7},{5,1},{7,3},{8,12},{10,14},{12... | collective-permute-start | bytes 393224 | tf_op jit(solution)/shard_map/ppermute | solution.py:13
  232.0 9.5 %collective-permute-start.42 = (bf16[2,64,512]{2,1,0:T(8,128)(2,1)S(1)}, bf16[2,64,512]{2,1,0:T(8,128)(2,1)S(1)}, u32[]{:S(2)}, u32[]{:S(2)}) collective-permute-start(bf16[2,64,512]{2,1,0:T(8,128)(2,1)S(1)} %get-tuple-element.6), channel_id=1, source_target_pairs={{0,2},{2,4},{4,6},{6,0},{1,3},{3,5},{5,7},{7,1},{8,10},{10,12},{12... | collective-permute-start | bytes 393224 | tf_op jit(solution)/shard_map/ppermute | solution.py:13
  241.7 2.1 collective-permute-start.43
  (4 other events, 7.8 us)

commit v2 on v1

v2 whole, which is shorter than its diff:
```python
import functools

import jax
import jax.numpy as jnp
from jax import lax
from jax.experimental import pallas as pl
from jax.experimental.pallas import tpu as pltpu
from jax.sharding import Mesh, PartitionSpec as P

KV = 1024
NZ, NY, NX, NC = 8, 4, 4, 2
BF = jnp.bfloat16
F32 = jnp.float32
PAIRS = [(i, j) for i in range(4) for j in range(i, 4)]
SMEM = pl.BlockSpec(memory_space=pltpu.SMEM)
VMEM = pl.BlockSpec(memory_space=pltpu.VMEM)
HBM = pl.BlockSpec(memory_space=pltpu.HBM)
CHUNKS = ((0, 1, 2, 3),)


def vmem(mebibytes):
    return pltpu.CompilerParams(vmem_limit_bytes=mebibytes * 1024 * 1024)


TOKENS_FIRST = (((0,), (0,)), ((), ()))


def shift(x, axis, size, offset):
    return lax.ppermute(x, axis, [(i, (i + offset) % size) for i in range(size)])


def position():
    return [lax.axis_index(axis) for axis in ("z", "y", "x", "c")]


def struct(shape, dtype):
    return jax.ShapeDtypeStruct(shape, dtype)


def feature_block(place, k, offset):
    return ((place[0] + k) & 3) * 4 + ((place[1] + offset) & 3)


def pack_kernel(ks, with_cots, act, cot, *refs):
    outs, own, sems = refs[:3], refs[3], refs[4]
    place = position()
    c = place[3]
    copies = []
    for o in (1, 2, 3):
        out = outs[o - 1]
        for i, k in enumerate(ks):
            column = pl.multiple_of(feature_block(place, k, o) * 512, 512)
            source = act.at[pl.ds(pl.multiple_of(c * 128, 128), 128), pl.ds(column, 512)]
            copies.append((source, out.at[:, pl.ds(i * 512, 512)]))
        if with_cots:
            for h in range(2):
                for m in range(2):
                    lane = len(ks) * 512 + h * 256 + m * 128
                    copies.append((cot.at[m, pl.ds(h * 128, 128), :], out.at[:, pl.ds(lane, 128)]))
    for i, k in enumerate(ks):
        column = pl.multiple_of(feature_block(place, k, 0) * 512, 512)
        copies.append((act.at[:, pl.ds(column, 512)], own.at[:, pl.ds(i * 512, 512)]))
    started = []
    for n, (source, target) in enumerate(copies):
        copy = pltpu.make_async_copy(source, target, sems.at[n])
        copy.start()
        started.append(copy)
    for copy in started:
        copy.wait()


def pack(act, cot, ks, with_cots):
    width = len(ks) * 512 + (512 if with_cots else 0)
    count = 3 * (len(ks) + (4 if with_cots else 0)) + len(ks)
    return pl.pallas_call(
        functools.partial(pack_kernel, ks, with_cots),
        out_shape=[struct((128, width), BF)] * 3 + [struct((256, len(ks) * 512), BF)],
        in_specs=[HBM, HBM],
        out_specs=[VMEM] * 4,
        scratch_shapes=[pltpu.SemaphoreType.DMA((count,))],
        compiler_params=vmem(12),
        name="pack",
    )(act, cot)


def product_kernel(ks, lane0, own, cot, *refs):
    count = 2 * len(ks)
    cots, pieces, swaps, outs = refs[:3], refs[3:6], refs[6:9], refs[9 : 9 + count]
    lhs, acc = refs[9 + count :]
    z, _, _, c = position()
    near = pl.multiple_of(c * 256, 256)
    far = pl.multiple_of(256 - c * 256, 256)
    for m in range(2):
        lhs[pl.ds(m * 128, 128), pl.ds(0, 256)] = cot[m].T
    for o in range(3):
        for n, lane in enumerate((near, far)):
            lhs[:, pl.ds(256 + (2 * o + n) * 128, 128)] = cots[o][:, pl.ds(lane0 + lane, 256)].T
    for i, k in enumerate(ks):
        m = ((z + k) & 7) >> 2
        for half in range(2):
            column = pl.ds(i * 512 + half * 256, 256)
            total = jnp.dot(lhs[:, pl.ds(0, 256)], own[:, column], preferred_element_type=F32)
            for o in range(3):
                for n, piece in enumerate((pieces[o], swaps[o])):
                    left = lhs[:, pl.ds(256 + (2 * o + n) * 128, 128)]
                    total = total + jnp.dot(left, piece[:, column], preferred_element_type=F32)
            acc[...] = total
            for j, matrix in enumerate((m, 1 - m)):
                row = pl.multiple_of(matrix * 128, 128)
                out = outs[2 * i + j]
                out[:, pl.ds(half * 256, 256)] = acc[pl.ds(row, 128), :].astype(out.dtype)


def products(own, cot, cots, pieces, swaps, ks, lane0):
    types = [F32 if k == 0 and j == 0 else BF for k in ks for j in range(2)]
    return pl.pallas_call(
        functools.partial(product_kernel, ks, lane0),
        out_shape=[struct((128, 512), dtype) for dtype in types],
        in_specs=[VMEM] * 11,
        out_specs=[VMEM] * len(types),
        scratch_shapes=[pltpu.VMEM((256, 1024), BF), pltpu.VMEM((256, 256), F32)],
        compiler_params=vmem(16),
        cost_estimate=pl.CostEstimate(flops=2 * 512 * 256 * 1024 * len(ks), bytes_accessed=4 << 20, transcendentals=0),
        name="products",
    )(own, cot, *cots, *pieces, *swaps)


def mul(left, right):
    return jnp.dot(left.astype(BF), right.astype(BF), preferred_element_type=F32)


def plan_kernel(worker_of, plan):
    z, y, _, _ = position()
    for o in range(4):
        target = z * 4 + ((y + o) & 3)

        def step(b, state):
            count, first, second = state
            hit = worker_of[b] == target
            offset = jnp.where((b & 3) == y, b >> 2, -1)
            first = jnp.where(hit & (count == 0), offset, first)
            second = jnp.where(hit & (count == 1), offset, second)
            return count + hit.astype(jnp.int32), first, second

        none = jnp.int32(-1)
        _, first, second = lax.fori_loop(0, 32, step, (jnp.int32(0), none, none))
        plan[2 * o] = first
        plan[2 * o + 1] = second
        worker = worker_of[target]
        slot = lax.fori_loop(0, target, lambda b, n: n + (worker_of[b] == worker).astype(jnp.int32), jnp.int32(0))
        plan[8 + o] = jnp.where((worker & 3) == y, ((z - (worker >> 2)) & 7) * 2 + slot, -1)
    for n in range(12, 16):
        plan[n] = 0


def make_plan(worker_of):
    return pl.pallas_call(
        plan_kernel,
        out_shape=struct((16,), jnp.int32),
        in_specs=[SMEM],
        out_specs=SMEM,
        name="plan",
    )(worker_of)


def root_kernel(worker_of, left, root, strips, occupied):
    a = 1.5625
    slot = pl.program_id(0)
    z, y, x_place, c = position()
    mine = z * 4 + y
    count = lax.fori_loop(0, 32, lambda b, n: n + (worker_of[b] == mine).astype(jnp.int32), jnp.int32(0))
    matrix = left[0]
    norm = jnp.sqrt(jnp.sum(jnp.sum(matrix * matrix, axis=1, keepdims=True), axis=0, keepdims=True))
    m = matrix / norm
    m2 = mul(m, m)
    p = m2 * 0.0625 - m * 0.625
    u = m * 1.25 - m2 * 0.25
    q = p * (2 * a) + mul(p, p)
    v = u * (a * a) + mul(q, u)
    r = m * -0.3125 - v * 0.25
    s = r * (2 * a) + mul(r, r)
    t = m * a + mul(r, m)
    f = s * (2 * a * a) + mul(s, s)
    w = t * (a * a * a * a) + mul(f, t)
    held = (count > slot).astype(F32)
    occupied[0] = jnp.full((8, 128), held, F32)
    scale = lax.rsqrt(jnp.sqrt(norm)) * held
    row = lax.broadcasted_iota(jnp.int32, (512, 512), 0)
    column = lax.broadcasted_iota(jnp.int32, (512, 512), 1)
    x = jnp.where(row == column, 1.25 * a, 0.0) + r * 1.25 - w * 0.25
    root[0] = x * scale
    strip = c * 64 + x_place * 16
    for n, (i, j) in enumerate(PAIRS):
        rows = pl.ds(pl.multiple_of(i * 128 + strip, 16), 16)
        strips[0, n] = root[0, rows, pl.ds(j * 128, 128)].astype(BF)


def make_roots(worker_of, left):
    return pl.pallas_call(
        root_kernel,
        grid=(2,),
        out_shape=[struct((2, 512, 512), F32), struct((2, 10, 16, 128), BF), struct((2, 8, 128), F32)],
        in_specs=[SMEM, pl.BlockSpec((1, 512, 512), lambda s: (s, 0, 0))],
        out_specs=[pl.BlockSpec((1, 512, 512), lambda s: (s, 0, 0)), pl.BlockSpec((1, 10, 16, 128), lambda s: (s, 0, 0, 0)), pl.BlockSpec((1, 8, 128), lambda s: (s, 0, 0))],
        compiler_params=vmem(32),
        cost_estimate=pl.CostEstimate(flops=2 * 7 * 2 * 512**3, bytes_accessed=4 << 20, transcendentals=0),
        name="roots",
    )(worker_of, left)


def gram_kernel(mine, theirs, keep, send1, send2, send3, acc):
    _, _, x, c = position()
    for n, (i, j) in enumerate(PAIRS):
        total = 0.0
        for part in (mine, theirs):
            total = total + lax.dot_general(
                part[:, pl.ds(i * 128, 128)], part[:, pl.ds(j * 128, 128)], TOKENS_FIRST, preferred_element_type=F32
            )
        acc[n] = total * (1.0 / KV)
    for o, out in enumerate((keep, send1, send2, send3)):
        row = pl.multiple_of(c * 64 + ((x + o) & 3) * 16, 16)
        out[...] = acc[:, pl.ds(row, 16), :].astype(out.dtype)


def grams(mine, theirs):
    return pl.pallas_call(
        gram_kernel,
        out_shape=[struct((10, 16, 128), F32)] + [struct((10, 16, 128), BF)] * 3,
        in_specs=[VMEM, VMEM],
        out_specs=[VMEM] * 4,
        scratch_shapes=[pltpu.VMEM((10, 128, 128), F32)],
        compiler_params=vmem(8),
        name="grams",
    )(mine, theirs)


def choose_kernel(plan, column, *refs):
    roots, outs, held = refs[:8], refs[8:12], refs[12]
    for o in range(8):
        held[pl.ds(2 * o, 2)] = roots[o][...]
    for o in range(4):
        for s in range(2):
            index = plan[2 * o + s]
            item = column[jnp.maximum(index, 0)]
            outs[o][s] = jnp.where(index >= 0, item, jnp.zeros_like(item))
        index = plan[8 + o]
        item = held[jnp.maximum(index, 0)]
        outs[o][2] = jnp.where(index >= 0, item, jnp.zeros_like(item))


def choose(plan, roots, column):
    return pl.pallas_call(
        choose_kernel,
        out_shape=[struct((3, 10, 16, 128), BF)] * 4,
        in_specs=[SMEM] + [VMEM] * 9,
        out_specs=[VMEM] * 4,
        scratch_shapes=[pltpu.VMEM((16, 10, 16, 128), BF)],
        compiler_params=vmem(8),
        name="choose",
    )(plan, column, *roots)


def finish_kernel(left, occupied, grad, *refs):
    mine, theirs, (stats, update, whole, root) = refs[:4], refs[4:8], refs[8:]
    slot = pl.program_id(0)
    _, _, x, c = position()

    @pl.when(slot == 0)
    def _():
        for side, part in ((c, mine), (1 - c, theirs)):
            for o in range(4):
                row = pl.multiple_of(side * 64 + ((x - o) & 3) * 16, 16)
                whole[:, :, pl.ds(row, 16), :] = part[o][...]

    held = occupied[0, pl.ds(0, 1), :]
    for n, (i, j) in enumerate(PAIRS):
        block = whole[slot, n].astype(F32)
        above = (0, pl.ds(i * 128, 128), pl.ds(j * 128, 128))
        stats[above] = (left[above] + block) * held
        if i != j:
            below = (0, pl.ds(j * 128, 128), pl.ds(i * 128, 128))
            stats[below] = (left[below] + block.T) * held

    @pl.when(slot == 1)
    def _():
        for n, (i, j) in enumerate(PAIRS):
            block = whole[2, n]
            root[pl.ds(i * 128, 128), pl.ds(j * 128, 128)] = block
            if i != j:
                root[pl.ds(j * 128, 128), pl.ds(i * 128, 128)] = block.astype(F32).T.astype(BF)
        update[...] = lax.dot_general(
            root[...], grad[...], (((1,), (1,)), ((), ())), preferred_element_type=F32
        ).astype(BF)


def finish(left, occupied, grad, mine, theirs):
    by_slot = pl.BlockSpec((1, 512, 512), lambda s: (s, 0, 0))
    piece = pl.BlockSpec((3, 10, 16, 128), lambda s: (0, 0, 0, 0))
    return pl.pallas_call(
        finish_kernel,
        grid=(2,),
        out_shape=[struct((2, 512, 512), F32), struct((512, 128), BF)],
        in_specs=[by_slot, pl.BlockSpec((1, 8, 128), lambda s: (s, 0, 0)), pl.BlockSpec((128, 512), lambda s: (0, 0))]
        + [piece] * 8,
        out_specs=[by_slot, pl.BlockSpec((512, 128), lambda s: (0, 0))],
        scratch_shapes=[pltpu.VMEM((3, 10, 128, 128), BF), pltpu.VMEM((512, 512), BF)],
        compiler_params=vmem(16),
        name="finish",
    )(left, occupied, grad, *mine, *theirs)


def local(activations, cotangents, worker_of, left_stats):
    left = left_stats[0]

    packed = [pack(activations, cotangents, ks, n == 0) for n, ks in enumerate(CHUNKS)]
    sent = packed[0][:3]
    first = arriving = [shift(p, "y", NY, o + 1) for o, p in enumerate(sent)]
    later, _ = lax.optimization_barrier((left, sent))
    roots, strips, occupied = make_roots(worker_of, later)
    plan = make_plan(worker_of)
    root_strips = [strips] + [shift(strips, "z", NZ, o) for o in range(1, 8)]
    first, arriving, root_strips = lax.optimization_barrier((first, arriving, root_strips))
    got, kept = [], None
    for n, ks in enumerate(CHUNKS):
        if n + 1 < len(CHUNKS):
            arriving, sent = lax.optimization_barrier((arriving, packed[n + 1][:3]))
            following = [shift(p, "y", NY, o + 1) for o, p in enumerate(sent)]
        swapped = [shift(p, "c", NC, 1) for p in arriving]
        parts = products(packed[n][3], cotangents, first, arriving, swapped, ks, 512 * len(CHUNKS[0]))
        for i, k in enumerate(ks):
            near, far = parts[2 * i : 2 * i + 2]
            if k == 0:
                kept = near
            else:
                got.append(shift(near, "z", NZ, k))
            got.append(shift(far, "z", NZ, k + 4))
        if n + 1 < len(CHUNKS):
            arriving = following
    total = kept
    for piece in got:
        total = total + piece.astype(F32)
    grad = total.astype(BF)

    theirs = shift(grad, "c", NC, 1)
    strip, *sends = grams(grad, theirs)
    for o, send in enumerate(sends):
        strip = strip + shift(send, "x", NX, o + 1).astype(F32)
    strip = strip.astype(BF)
    column = lax.all_to_all(jnp.broadcast_to(strip[None], (8, 10, 16, 128)), "z", 0, 0, tiled=True)
    routed = choose(plan, root_strips, column)
    arrived = routed[0]
    for o in (1, 2, 3):
        arrived = arrived + shift(routed[o], "y", NY, o)
    by_x = [arrived] + [shift(arrived, "x", NX, o) for o in (1, 2, 3)]
    by_c = [shift(piece, "c", NC, 1) for piece in by_x]
    new_stats, update = finish(left, occupied, grad, by_x, by_c)
    return new_stats[None], roots[None], update[None]


def solution(mesh):
    fine = Mesh(mesh.devices.reshape(NZ, NY, NX, NC), ("z", "y", "x", "c"))
    dp, mp = ("z", "y"), ("x", "c")
    return jax.shard_map(
        local,
        mesh=fine,
        in_specs=(P(dp, None), P(None, dp, mp), P(), P(dp, None, None, None)),
        out_specs=(P(dp, None, None, None), P(dp, None, None, None), P(dp, None, mp)),
        check_vma=False,
    )
```

time: 251 us -> 137 us (0.55); the launches traced: 247 us -> 137 us
  waiting for transfers between devices: 82.6 us -> 48.5 us
  between operations: 30.1 us -> 0.73 us
  matrix products: 26.5 us -> 0 us
  Pallas kernels: 0 us -> 15.9 us
  starting transfers between devices: 81.5 us -> 66.8 us
  other arithmetic: 14.8 us -> 0.2 us
  local copies, waits for them, and re-layouts: 11.5 us -> 4.52 us
    ppermute x58 -> x34, waiting for transfers between devices: 82.6 us -> 40.4 us  [shift(): lax.ppermute(x, axis, [(i, (i + offset) % size) for i in range(size)])]
    dot_general x13 -> x0, matrix products: 26.5 us -> none  [the longest x7 23.4 us: batch_product(): jnp.einsum('sij,sjk->sik', left, right, precision=lax.Precision.HIGH, pre...]
    ppermute x58 -> x34, starting transfers between devices: 81.5 us -> 61.9 us  [shift(): lax.ppermute(x, axis, [(i, (i + offset) % size) for i in range(size)])]
    pallas_call x0 -> x7, Pallas kernels: none -> 15.9 us  [the longest x1 7.41 us: make_roots(): pl.pallas_call(root_kernel, grid=(2,), out_shape=[struct((2, 512, 512), F...]
    all_to_all x0 -> x1, waiting for transfers between devices: none -> 8.1 us  [local(): lax.all_to_all(jnp.broadcast_to(strip[None], (8, 10, 16, 128)), 'z', 0, 0...]
    select_n x2 -> x0, other arithmetic: 5 us -> none  [the longest x1 4.99 us: local(): pair.append(jnp.where(jnp.any(match), item, jnp.zeros((), BF)))]
    all_to_all x0 -> x1, starting transfers between devices: none -> 4.96 us  [local(): lax.all_to_all(jnp.broadcast_to(strip[None], (8, 10, 16, 128)), 'z', 0, 0...]
    dynamic_slice x4 -> x0, local copies, waits for them, and re-layouts: 3.39 us -> none  [the longest x1 2.58 us: local(): lax.dynamic_slice(activations, (c * 128, first + (y + o) % 4 * 512), (128...]
  transfers between devices with their start and end apart: 58 -> 35, of which waited for: 26 -> 23; matrix products, arithmetic and copies ran while one was open for 17% -> 0% of each run, Pallas kernels for 0% -> 7%
where the time goes in v2:
time: 137 us
  starting transfers between devices  66.8 us (49%)
  waiting for transfers between devices  48.5 us (35%)
  Pallas kernels  15.9 us (12%)
  local copies, waits for them, and re-layouts  4.52 us (3%)
    ppermute x34, starting transfers between devices, shift(): lax.ppermute(x, axis, [(i, (i + offset) % size) for i in range(size)])  61.9 us
    ppermute x34, waiting for transfers between devices, shift(): lax.ppermute(x, axis, [(i, (i + offset) % size) for i in range(size)])  40.4 us
    all_to_all x1, waiting for transfers between devices, local(): lax.all_to_all(jnp.broadcast_to(strip[None], (8, 10, 16, 128)), 'z', 0, 0...  8.1 us
    pallas_call x1, Pallas kernels, make_roots(): pl.pallas_call(root_kernel, grid=(2,), out_shape=[struct((2, 512, 512), F...  7.41 us
    all_to_all x1, starting transfers between devices, local(): lax.all_to_all(jnp.broadcast_to(strip[None], (8, 10, 16, 128)), 'z', 0, 0...  4.96 us
    unnamed x12, local copies, waits for them, and re-layouts  3.75 us
  transfers between devices with their start and end apart: 35, of which 23 were waited for; matrix products, arithmetic and copies ran while one was open for 0% of the time, Pallas kernels for 7%

profile of v2, /device:TPU:1, one launch (start us, length us, event | category | flops | bytes accessed | tf_op | source)
XLA Modules:
  0.0 136.7 jit_solution(11049667507080315568)
XLA Ops:
  0.6 2.2 %copy-done = bf16[256,8192]{1,0:T(8,128)(2,1)S(1)} copy-done((bf16[256,8192]{1,0:T(8,128)(2,1)S(1)}, bf16[256,8192]{1,0:T(8,128)(2,1)}, u32[]{:S(2)}) %copy-start) | copy-done | bytes 4194328
  2.8 0.9 copy-done.2
  3.7 0.7 pack.1
  4.5 2.2 %collective-permute-start = (bf16[128,2560]{1,0:T(8,128)(2,1)S(1)}, bf16[128,2560]{1,0:T(8,128)(2,1)S(1)}, u32[]{:S(2)}, u32[]{:S(2)}) collective-permute-start(bf16[128,2560]{1,0:T(8,128)(2,1)S(1)} %get-tuple-element.43), channel_id=1, source_target_pairs={{0,8},{8,16},{16,24},{24,0},{1,9},{9,17},{17,25},{25,1},{2,10},{10... | collective-permute-start | bytes 1966088 | tf_op jit(solution)/shard_map/ppermute | solution.py:29
  6.7 2.6 %collective-permute-start.1 = (bf16[128,2560]{1,0:T(8,128)(2,1)S(1)}, bf16[128,2560]{1,0:T(8,128)(2,1)S(1)}, u32[]{:S(2)}, u32[]{:S(2)}) collective-permute-start(bf16[128,2560]{1,0:T(8,128)(2,1)S(1)} %get-tuple-element.44), channel_id=1, source_target_pairs={{0,16},{8,24},{16,0},{24,8},{1,17},{9,25},{17,1},{25,9},{2,18},{10... | collective-permute-start | bytes 1966088 | tf_op jit(solution)/shard_map/ppermute | solution.py:29
  9.3 1.1 collective-permute-start.2
  10.4 7.4 %roots.1 = (f32[2,512,512]{2,1,0:T(8,128)}, bf16[2,10,16,128]{3,2,1,0:T(8,128)(2,1)S(1)}, f32[2,8,128]{2,1,0:T(8,128)S(1)}) custom-call(s32[32]{0:T(128)S(1)} %copy-done.5, f32[2,512,512]{2,1,0:T(8,128)S(1)} %bitcast.4), custom_call_target="tpu_custom_call" | custom-call | flops 3758096384 | bytes 4194304 | tf_op jit(solution)/shard_map/roots/pallas_call | solution.py:199
  17.8 1.6 %collective-permute-start.3 = (bf16[2,10,16,128]{3,2,1,0:T(8,128)(2,1)S(1)}, bf16[2,10,16,128]{3,2,1,0:T(8,128)(2,1)S(1)}, u32[]{:S(2)}, u32[]{:S(2)}) collective-permute-start(bf16[2,10,16,128]{3,2,1,0:T(8,128)(2,1)S(1)} %get-tuple-element.68.refs_0_), channel_id=1, source_target_pairs={{0,32},{32,64},{64,96},{96,128},{128,160},{160,192},{192,224},{224... | collective-permute-start | bytes 245768 | tf_op jit(solution)/shard_map/ppermute | solution.py:29
  19.4 3.0 %collective-permute-start.4 = (bf16[2,10,16,128]{3,2,1,0:T(8,128)(2,1)S(1)}, bf16[2,10,16,128]{3,2,1,0:T(8,128)(2,1)S(1)}, u32[]{:S(2)}, u32[]{:S(2)}) collective-permute-start(bf16[2,10,16,128]{3,2,1,0:T(8,128)(2,1)S(1)} %get-tuple-element.68.refs_0_), channel_id=1, source_target_pairs={{0,64},{32,96},{64,128},{96,160},{128,192},{160,224},{192,0},{224,... | collective-permute-start | bytes 245768 | tf_op jit(solution)/shard_map/ppermute | solution.py:29
  22.4 2.8 %collective-permute-done.3.refs_1_ = bf16[2,10,16,128]{3,2,1,0:T(8,128)(2,1)S(1)} collective-permute-done((bf16[2,10,16,128]{3,2,1,0:T(8,128)(2,1)S(1)}, bf16[2,10,16,128]{3,2,1,0:T(8,128)(2,1)S(1)}, u32[]{:S(2)}, u32[]{:S(2)}) %collective-permute-start.3) | collective-permute-done | bytes 81952 | tf_op jit(solution)/shard_map/ppermute | solution.py:29
  25.2 1.3 collective-permute-start.5
  26.5 2.2 %collective-permute-done.4.refs_2_ = bf16[2,10,16,128]{3,2,1,0:T(8,128)(2,1)S(1)} collective-permute-done((bf16[2,10,16,128]{3,2,1,0:T(8,128)(2,1)S(1)}, bf16[2,10,16,128]{3,2,1,0:T(8,128)(2,1)S(1)}, u32[]{:S(2)}, u32[]{:S(2)}) %collective-permute-start.4) | collective-permute-done | bytes 81952 | tf_op jit(solution)/shard_map/ppermute | solution.py:29
  28.7 3.0 %collective-permute-start.6 = (bf16[2,10,16,128]{3,2,1,0:T(8,128)(2,1)S(1)}, bf16[2,10,16,128]{3,2,1,0:T(8,128)(2,1)S(1)}, u32[]{:S(2)}, u32[]{:S(2)}) collective-permute-start(bf16[2,10,16,128]{3,2,1,0:T(8,128)(2,1)S(1)} %get-tuple-element.68.refs_0_), channel_id=1, source_target_pairs={{0,128},{32,160},{64,192},{96,224},{128,0},{160,32},{192,64},{224,... | collective-permute-start | bytes 245768 | tf_op jit(solution)/shard_map/ppermute | solution.py:29
  31.7 1.6 %collective-permute-done.5.refs_3_ = bf16[2,10,16,128]{3,2,1,0:T(8,128)(2,1)S(1)} collective-permute-done((bf16[2,10,16,128]{3,2,1,0:T(8,128)(2,1)S(1)}, bf16[2,10,16,128]{3,2,1,0:T(8,128)(2,1)S(1)}, u32[]{:S(2)}, u32[]{:S(2)}) %collective-permute-start.5) | collective-permute-done | bytes 81952 | tf_op jit(solution)/shard_map/ppermute | solution.py:29
  33.3 3.7 %collective-permute-start.7 = (bf16[2,10,16,128]{3,2,1,0:T(8,128)(2,1)S(1)}, bf16[2,10,16,128]{3,2,1,0:T(8,128)(2,1)S(1)}, u32[]{:S(2)}, u32[]{:S(2)}) collective-permute-start(bf16[2,10,16,128]{3,2,1,0:T(8,128)(2,1)S(1)} %get-tuple-element.68.refs_0_), channel_id=1, source_target_pairs={{0,160},{32,192},{64,224},{96,0},{128,32},{160,64},{192,96},{224,1... | collective-permute-start | bytes 245768 | tf_op jit(solution)/shard_map/ppermute | solution.py:29
  37.0 3.0 %collective-permute-done.6.refs_4_ = bf16[2,10,16,128]{3,2,1,0:T(8,128)(2,1)S(1)} collective-permute-done((bf16[2,10,16,128]{3,2,1,0:T(8,128)(2,1)S(1)}, bf16[2,10,16,128]{3,2,1,0:T(8,128)(2,1)S(1)}, u32[]{:S(2)}, u32[]{:S(2)}) %collective-permute-start.6) | collective-permute-done | bytes 81952 | tf_op jit(solution)/shard_map/ppermute | solution.py:29
  40.0 1.0 collective-permute-start.8
  41.0 1.2 collective-permute-done.7.refs_5_
  42.2 4.4 %collective-permute-done.8.refs_6_ = bf16[2,10,16,128]{3,2,1,0:T(8,128)(2,1)S(1)} collective-permute-done((bf16[2,10,16,128]{3,2,1,0:T(8,128)(2,1)S(1)}, bf16[2,10,16,128]{3,2,1,0:T(8,128)(2,1)S(1)}, u32[]{:S(2)}, u32[]{:S(2)}) %collective-permute-start.8) | collective-permute-done | bytes 81952 | tf_op jit(solution)/shard_map/ppermute | solution.py:29
  46.6 1.0 collective-permute-done.9.refs_7_
  47.6 4.5 %collective-permute-start.10 = (bf16[128,2560]{1,0:T(8,128)(2,1)S(1)}, bf16[128,2560]{1,0:T(8,128)(2,1)S(1)}, u32[]{:S(2)}, u32[]{:S(2)}) collective-permute-start(bf16[128,2560]{1,0:T(8,128)(2,1)S(1)} %collective-permute-done.refs_0_.refs_3_), channel_id=1, source_target_pairs={{0,1},{1,0},{2,3},{3,2},{4,5},{5,4},{6,7},{7,6},{8,9},{9,8},{10,11... | collective-permute-start | bytes 1966088 | tf_op jit(solution)/shard_map/ppermute | solution.py:29
  52.2 0.4 collective-permute-start.12
  52.6 1.2 collective-permute-done.10.refs_6_
  53.9 0.9 collective-permute-done.11.refs_7_
  54.8 0.9 collective-permute-done.12.refs_8_
  55.7 2.5 %products.1 = (f32[128,512]{1,0:T(8,128)S(1)}, bf16[128,512]{1,0:T(8,128)(2,1)S(1)}, bf16[128,512]{1,0:T(8,128)(2,1)S(1)}, bf16[128,512]{1,0:T(8,128)(2,1)S(1)},...) custom-call(bf16[256,2048]{1,0:T(8,128)(2,1)S(1)} %get-tuple-element, ...), custom_call_target="tpu_custom_call" | custom-call | flops 1073741824 | bytes 4194304 | tf_op jit(solution)/shard_map/products/pallas_call | solution.py:116
  58.3 3.3 %collective-permute-start.13 = (bf16[128,512]{1,0:T(8,128)(2,1)S(1)}, bf16[128,512]{1,0:T(8,128)(2,1)S(1)}, u32[]{:S(2)}, u32[]{:S(2)}) collective-permute-start(bf16[128,512]{1,0:T(8,128)(2,1)S(1)} %get-tuple-element.57), channel_id=1, source_target_pairs={{0,128},{32,160},{64,192},{96,224},{128,0},{160,32},{192,64},{224,... | collective-permute-start | bytes 393224 | tf_op jit(solution)/shard_map/ppermute | solution.py:29
  61.5 1.2 collective-permute-start.14
  62.8 3.5 %collective-permute-start.16 = (bf16[128,512]{1,0:T(8,128)(2,1)S(1)}, bf16[128,512]{1,0:T(8,128)(2,1)S(1)}, u32[]{:S(2)}, u32[]{:S(2)}) collective-permute-start(bf16[128,512]{1,0:T(8,128)(2,1)S(1)} %get-tuple-element.60), channel_id=1, source_target_pairs={{0,64},{32,96},{64,128},{96,160},{128,192},{160,224},{192,0},{224,... | collective-permute-start | bytes 393224 | tf_op jit(solution)/shard_map/ppermute | solution.py:29
  66.3 0.8 collective-permute-start.17
  67.1 2.8 %collective-permute-done.13 = bf16[128,512]{1,0:T(8,128)(2,1)S(1)} collective-permute-done((bf16[128,512]{1,0:T(8,128)(2,1)S(1)}, bf16[128,512]{1,0:T(8,128)(2,1)S(1)}, u32[]{:S(2)}, u32[]{:S(2)}) %collective-permute-start.13) | collective-permute-done | bytes 131104 | tf_op jit(solution)/shard_map/ppermute | solution.py:29
  69.9 0.5 collective-permute-start.18
  70.4 4.1 %collective-permute-start.19 = (bf16[128,512]{1,0:T(8,128)(2,1)S(1)}, bf16[128,512]{1,0:T(8,128)(2,1)S(1)}, u32[]{:S(2)}, u32[]{:S(2)}) collective-permute-start(bf16[128,512]{1,0:T(8,128)(2,1)S(1)} %get-tuple-element.63), channel_id=1, source_target_pairs={{0,224},{32,0},{64,32},{96,64},{128,96},{160,128},{192,160},{224,1... | collective-permute-start | bytes 393224 | tf_op jit(solution)/shard_map/ppermute | solution.py:29
  74.5 3.7 %collective-permute-done.15 = bf16[128,512]{1,0:T(8,128)(2,1)S(1)} collective-permute-done((bf16[128,512]{1,0:T(8,128)(2,1)S(1)}, bf16[128,512]{1,0:T(8,128)(2,1)S(1)}, u32[]{:S(2)}, u32[]{:S(2)}) %collective-permute-start.15) | collective-permute-done | bytes 131104 | tf_op jit(solution)/shard_map/ppermute | solution.py:29
  78.2 6.4 %collective-permute-done.17 = bf16[128,512]{1,0:T(8,128)(2,1)S(1)} collective-permute-done((bf16[128,512]{1,0:T(8,128)(2,1)S(1)}, bf16[128,512]{1,0:T(8,128)(2,1)S(1)}, u32[]{:S(2)}, u32[]{:S(2)}) %collective-permute-start.17) | collective-permute-done | bytes 131104 | tf_op jit(solution)/shard_map/ppermute | solution.py:29
  84.5 1.3 collective-permute-done.19
  85.9 1.2 collective-permute-start.20
  87.1 1.0 collective-permute-done.20.theirs
  88.1 0.4 grams.1
  88.5 1.3 collective-permute-start.21
  89.8 2.3 %collective-permute-start.22 = (bf16[10,16,128]{2,1,0:T(8,128)(2,1)S(1)}, bf16[10,16,128]{2,1,0:T(8,128)(2,1)S(1)}, u32[]{:S(2)}, u32[]{:S(2)}) collective-permute-start(bf16[10,16,128]{2,1,0:T(8,128)(2,1)S(1)} %get-tuple-element.66), channel_id=1, source_target_pairs={{0,4},{2,6},{4,0},{6,2},{1,5},{3,7},{5,1},{7,3},{8,12},{10,14},{12... | collective-permute-start | bytes 122888 | tf_op jit(solution)/shard_map/ppermute | solution.py:29
  92.1 1.2 collective-permute-start.23
  93.3 1.1 collective-permute-done.22
  94.4 0.8 collective-permute-done.23
  95.3 0.8 broadcast_in_dim.15
  96.0 5.0 %all-to-all-start = ((bf16[8,10,16,128]{3,2,1,0:T(8,128)(2,1)}), bf16[8,10,16,128]{3,2,1,0:T(8,128)(2,1)S(1)}, u32[]{:S(2)}, u32[]{:S(2)}) async-start(bf16[8,10,16,128]{3,2,1,0:T(8,128)(2,1)} %broadcast_in_dim.15), calls=%async_computation | async-start | bytes 655360 | tf_op jit(solution)/shard_map/all_to_all | solution.py:349
  101.0 2.3 %plan.1 = s32[16]{0:T(128)} custom-call(s32[32]{0:T(128)} %worker_of.3), custom_call_target="tpu_custom_call" | custom-call | tf_op jit(solution)/shard_map/plan/pallas_call | solution.py:157
  103.3 8.1 %all-to-all-done.column = bf16[8,10,16,128]{3,2,1,0:T(8,128)(2,1)S(1)} async-done(((bf16[8,10,16,128]{3,2,1,0:T(8,128)(2,1)}), bf16[8,10,16,128]{3,2,1,0:T(8,128)(2,1)S(1)}, u32[]{:S(2)}, u32[]{:S(2)}) %all-to-all-start) | async-done | bytes 327712 | tf_op jit(solution)/shard_map/all_to_all | solution.py:349
  111.4 0.7 copy-done.4
  112.0 0.7 choose.1
  112.7 1.4 %collective-permute-start.24 = (bf16[3,10,16,128]{3,2,1,0:T(8,128)(2,1)S(1)}, bf16[3,10,16,128]{3,2,1,0:T(8,128)(2,1)S(1)}, u32[]{:S(2)}, u32[]{:S(2)}) collective-permute-start(bf16[3,10,16,128]{3,2,1,0:T(8,128)(2,1)S(1)} %get-tuple-element.77), channel_id=1, source_target_pairs={{0,8},{8,16},{16,24},{24,0},{1,9},{9,17},{17,25},{25,1},{2,10},{10... | collective-permute-start | bytes 368648 | tf_op jit(solution)/shard_map/ppermute | solution.py:29
  114.1 0.7 collective-permute-start.25
  114.8 1.8 %collective-permute-start.26 = (bf16[3,10,16,128]{3,2,1,0:T(8,128)(2,1)S(1)}, bf16[3,10,16,128]{3,2,1,0:T(8,128)(2,1)S(1)}, u32[]{:S(2)}, u32[]{:S(2)}) collective-permute-start(bf16[3,10,16,128]{3,2,1,0:T(8,128)(2,1)S(1)} %get-tuple-element.79), channel_id=1, source_target_pairs={{0,24},{8,0},{16,8},{24,16},{1,25},{9,1},{17,9},{25,17},{2,26},{10... | collective-permute-start | bytes 368648 | tf_op jit(solution)/shard_map/ppermute | solution.py:29
  116.6 1.1 collective-permute-done.24
  117.7 1.6 %collective-permute-done.25 = bf16[3,10,16,128]{3,2,1,0:T(8,128)(2,1)S(1)} collective-permute-done((bf16[3,10,16,128]{3,2,1,0:T(8,128)(2,1)S(1)}, bf16[3,10,16,128]{3,2,1,0:T(8,128)(2,1)S(1)}, u32[]{:S(2)}, u32[]{:S(2)}) %collective-permute-start.25) | collective-permute-done | bytes 122912 | tf_op jit(solution)/shard_map/ppermute | solution.py:29
  119.7 0.9 collective-permute-start.27
  120.6 2.2 %collective-permute-start.28 = (bf16[3,10,16,128]{3,2,1,0:T(8,128)(2,1)S(1)}, bf16[3,10,16,128]{3,2,1,0:T(8,128)(2,1)S(1)}, u32[]{:S(2)}, u32[]{:S(2)}) collective-permute-start(bf16[3,10,16,128]{3,2,1,0:T(8,128)(2,1)S(1)} %add_add_fusion.refs_0_), channel_id=1, source_target_pairs={{0,4},{2,6},{4,0},{6,2},{1,5},{3,7},{5,1},{7,3},{8,12},{10,14},{12... | collective-permute-start | bytes 368648 | tf_op jit(solution)/shard_map/ppermute | solution.py:29
  122.8 0.9 collective-permute-start.29
  123.7 5.6 %collective-permute-start.30 = (bf16[3,10,16,128]{3,2,1,0:T(8,128)(2,1)S(1)}, bf16[3,10,16,128]{3,2,1,0:T(8,128)(2,1)S(1)}, u32[]{:S(2)}, u32[]{:S(2)}) collective-permute-start(bf16[3,10,16,128]{3,2,1,0:T(8,128)(2,1)S(1)} %add_add_fusion.refs_0_), channel_id=1, source_target_pairs={{0,1},{1,0},{2,3},{3,2},{4,5},{5,4},{6,7},{7,6},{8,9},{9,8},{10,11... | collective-permute-start | bytes 368648 | tf_op jit(solution)/shard_map/ppermute | solution.py:29
  129.3 1.8 %collective-permute-start.31 = (bf16[3,10,16,128]{3,2,1,0:T(8,128)(2,1)S(1)}, bf16[3,10,16,128]{3,2,1,0:T(8,128)(2,1)S(1)}, u32[]{:S(2)}, u32[]{:S(2)}) collective-permute-start(bf16[3,10,16,128]{3,2,1,0:T(8,128)(2,1)S(1)} %collective-permute-done.27.refs_1_), channel_id=1, source_target_pairs={{0,1},{1,0},{2,3},{3,2},{4,5},{5,4},{6,7},{7,6},{8,9},{9,8},{10,11... | collective-permute-start | bytes 368648 | tf_op jit(solution)/shard_map/ppermute | solution.py:29
  131.1 2.0 %collective-permute-start.32 = (bf16[3,10,16,128]{3,2,1,0:T(8,128)(2,1)S(1)}, bf16[3,10,16,128]{3,2,1,0:T(8,128)(2,1)S(1)}, u32[]{:S(2)}, u32[]{:S(2)}) collective-permute-start(bf16[3,10,16,128]{3,2,1,0:T(8,128)(2,1)S(1)} %collective-permute-done.28.refs_2_), channel_id=1, source_target_pairs={{0,1},{1,0},{2,3},{3,2},{4,5},{5,4},{6,7},{7,6},{8,9},{9,8},{10,11... | collective-permute-start | bytes 368648 | tf_op jit(solution)/shard_map/ppermute | solution.py:29
  133.2 0.7 collective-permute-start.33
  134.2 0.7 collective-permute-done.33.refs_7_
  134.9 1.8 %finish.1 = (f32[2,512,512]{2,1,0:T(8,128)}, bf16[512,128]{1,0:T(8,128)(2,1)}) custom-call(f32[2,512,512]{2,1,0:T(8,128)S(1)} %bitcast.5, f32[2,8,128]{2,1,0:T(8,128)S(1)} %get-tuple-element.47.occupied, bf16[128,512]{1,0:T(8,128)(2,1)S(1)} %add_convert_fusion.mine.grad, bf16[3,10,16,128]{3,2,1,0:T(8,128)(2,1)S(1)} %add_add_fusion.refs_0_, ...), custom_call_target="tpu_custom_call" | custom-call | tf_op jit(solution)/shard_map/finish/pallas_call | solution.py:299
  (29 shorter events, 1.0 us)
Async XLA Ops:
  0.6 2.2 %copy-start = (bf16[256,8192]{1,0:T(8,128)(2,1)S(1)}, bf16[256,8192]{1,0:T(8,128)(2,1)}, u32[]{:S(2)}) copy-start(bf16[256,8192]{1,0:T(8,128)(2,1)} %act.1) | copy-start | bytes 12582916
  2.8 0.9 copy-start.2
  3.7 6.6 %copy-start.1 = (f32[1,2,512,512]{3,2,1,0:T(8,128)S(1)}, f32[1,2,512,512]{3,2,1,0:T(8,128)}, u32[]{:S(2)}) copy-start(f32[1,2,512,512]{3,2,1,0:T(8,128)} %param.7) | copy-start | bytes 6291460
  3.7 6.6 %copy-start.5 = (s32[32]{0:T(128)S(1)}, s32[32]{0:T(128)}, u32[]{:S(2)}) copy-start(s32[32]{0:T(128)} %worker_of.3) | copy-start | bytes 388
  4.5 43.2 %collective-permute-start = (bf16[128,2560]{1,0:T(8,128)(2,1)S(1)}, bf16[128,2560]{1,0:T(8,128)(2,1)S(1)}, u32[]{:S(2)}, u32[]{:S(2)}) collective-permute-start(bf16[128,2560]{1,0:T(8,128)(2,1)S(1)} %get-tuple-element.43), channel_id=1, source_target_pairs={{0,8},{8,16},{16,24},{24,0},{1,9},{9,17},{17,25},{25,1},{2,10},{10... | collective-permute-start | bytes 1966088 | tf_op jit(solution)/shard_map/ppermute | solution.py:29
  6.7 41.0 %collective-permute-start.1 = (bf16[128,2560]{1,0:T(8,128)(2,1)S(1)}, bf16[128,2560]{1,0:T(8,128)(2,1)S(1)}, u32[]{:S(2)}, u32[]{:S(2)}) collective-permute-start(bf16[128,2560]{1,0:T(8,128)(2,1)S(1)} %get-tuple-element.44), channel_id=1, source_target_pairs={{0,16},{8,24},{16,0},{24,8},{1,17},{9,25},{17,1},{25,9},{2,18},{10... | collective-permute-start | bytes 1966088 | tf_op jit(solution)/shard_map/ppermute | solution.py:29
  9.3 38.3 %collective-permute-start.2 = (bf16[128,2560]{1,0:T(8,128)(2,1)S(1)}, bf16[128,2560]{1,0:T(8,128)(2,1)S(1)}, u32[]{:S(2)}, u32[]{:S(2)}) collective-permute-start(bf16[128,2560]{1,0:T(8,128)(2,1)S(1)} %get-tuple-element.45), channel_id=1, source_target_pairs={{0,24},{8,0},{16,8},{24,16},{1,25},{9,1},{17,9},{25,17},{2,26},{10... | collective-permute-start | bytes 1966088 | tf_op jit(solution)/shard_map/ppermute | solution.py:29
  10.4 45.4 %copy-start.3 = (bf16[2,256,128]{2,1,0:T(8,128)(2,1)S(1)}, bf16[2,256,128]{2,1,0:T(8,128)(2,1)}, u32[]{:S(2)}) copy-start(bf16[2,256,128]{2,1,0:T(8,128)(2,1)} %cot.3) | copy-start | bytes 393220
  17.8 7.4 %collective-permute-start.3 = (bf16[2,10,16,128]{3,2,1,0:T(8,128)(2,1)S(1)}, bf16[2,10,16,128]{3,2,1,0:T(8,128)(2,1)S(1)}, u32[]{:S(2)}, u32[]{:S(2)}) collective-permute-start(bf16[2,10,16,128]{3,2,1,0:T(8,128)(2,1)S(1)} %get-tuple-element.68.refs_0_), channel_id=1, source_target_pairs={{0,32},{32,64},{64,96},{96,128},{128,160},{160,192},{192,224},{224... | collective-permute-start | bytes 245768 | tf_op jit(solution)/shard_map/ppermute | solution.py:29
  19.4 9.3 %collective-permute-start.4 = (bf16[2,10,16,128]{3,2,1,0:T(8,128)(2,1)S(1)}, bf16[2,10,16,128]{3,2,1,0:T(8,128)(2,1)S(1)}, u32[]{:S(2)}, u32[]{:S(2)}) collective-permute-start(bf16[2,10,16,128]{3,2,1,0:T(8,128)(2,1)S(1)} %get-tuple-element.68.refs_0_), channel_id=1, source_target_pairs={{0,64},{32,96},{64,128},{96,160},{128,192},{160,224},{192,0},{224,... | collective-permute-start | bytes 245768 | tf_op jit(solution)/shard_map/ppermute | solution.py:29
  25.2 8.1 %collective-permute-start.5 = (bf16[2,10,16,128]{3,2,1,0:T(8,128)(2,1)S(1)}, bf16[2,10,16,128]{3,2,1,0:T(8,128)(2,1)S(1)}, u32[]{:S(2)}, u32[]{:S(2)}) collective-permute-start(bf16[2,10,16,128]{3,2,1,0:T(8,128)(2,1)S(1)} %get-tuple-element.68.refs_0_), channel_id=1, source_target_pairs={{0,96},{32,128},{64,160},{96,192},{128,224},{160,0},{192,32},{224,... | collective-permute-start | bytes 245768 | tf_op jit(solution)/shard_map/ppermute | solution.py:29
  28.7 11.3 %collective-permute-start.6 = (bf16[2,10,16,128]{3,2,1,0:T(8,128)(2,1)S(1)}, bf16[2,10,16,128]{3,2,1,0:T(8,128)(2,1)S(1)}, u32[]{:S(2)}, u32[]{:S(2)}) collective-permute-start(bf16[2,10,16,128]{3,2,1,0:T(8,128)(2,1)S(1)} %get-tuple-element.68.refs_0_), channel_id=1, source_target_pairs={{0,128},{32,160},{64,192},{96,224},{128,0},{160,32},{192,64},{224,... | collective-permute-start | bytes 245768 | tf_op jit(solution)/shard_map/ppermute | solution.py:29
  33.3 8.9 %collective-permute-start.7 = (bf16[2,10,16,128]{3,2,1,0:T(8,128)(2,1)S(1)}, bf16[2,10,16,128]{3,2,1,0:T(8,128)(2,1)S(1)}, u32[]{:S(2)}, u32[]{:S(2)}) collective-permute-start(bf16[2,10,16,128]{3,2,1,0:T(8,128)(2,1)S(1)} %get-tuple-element.68.refs_0_), channel_id=1, source_target_pairs={{0,160},{32,192},{64,224},{96,0},{128,32},{160,64},{192,96},{224,1... | collective-permute-start | bytes 245768 | tf_op jit(solution)/shard_map/ppermute | solution.py:29
  40.0 6.6 %collective-permute-start.8 = (bf16[2,10,16,128]{3,2,1,0:T(8,128)(2,1)S(1)}, bf16[2,10,16,128]{3,2,1,0:T(8,128)(2,1)S(1)}, u32[]{:S(2)}, u32[]{:S(2)}) collective-permute-start(bf16[2,10,16,128]{3,2,1,0:T(8,128)(2,1)S(1)} %get-tuple-element.68.refs_0_), channel_id=1, source_target_pairs={{0,192},{32,224},{64,0},{96,32},{128,64},{160,96},{192,128},{224,1... | collective-permute-start | bytes 245768 | tf_op jit(solution)/shard_map/ppermute | solution.py:29
  42.2 5.4 %collective-permute-start.9 = (bf16[2,10,16,128]{3,2,1,0:T(8,128)(2,1)S(1)}, bf16[2,10,16,128]{3,2,1,0:T(8,128)(2,1)S(1)}, u32[]{:S(2)}, u32[]{:S(2)}) collective-permute-start(bf16[2,10,16,128]{3,2,1,0:T(8,128)(2,1)S(1)} %get-tuple-element.68.refs_0_), channel_id=1, source_target_pairs={{0,224},{32,0},{64,32},{96,64},{128,96},{160,128},{192,160},{224,1... | collective-permute-start | bytes 245768 | tf_op jit(solution)/shard_map/ppermute | solution.py:29
  47.6 6.2 %collective-permute-start.10 = (bf16[128,2560]{1,0:T(8,128)(2,1)S(1)}, bf16[128,2560]{1,0:T(8,128)(2,1)S(1)}, u32[]{:S(2)}, u32[]{:S(2)}) collective-permute-start(bf16[128,2560]{1,0:T(8,128)(2,1)S(1)} %collective-permute-done.refs_0_.refs_3_), channel_id=1, source_target_pairs={{0,1},{1,0},{2,3},{3,2},{4,5},{5,4},{6,7},{7,6},{8,9},{9,8},{10,11... | collective-permute-start | bytes 1966088 | tf_op jit(solution)/shard_map/ppermute | solution.py:29
  52.1 2.7 %collective-permute-start.11 = (bf16[128,2560]{1,0:T(8,128)(2,1)S(1)}, bf16[128,2560]{1,0:T(8,128)(2,1)S(1)}, u32[]{:S(2)}, u32[]{:S(2)}) collective-permute-start(bf16[128,2560]{1,0:T(8,128)(2,1)S(1)} %collective-permute-done.1.refs_1_.refs_4_), channel_id=1, source_target_pairs={{0,1},{1,0},{2,3},{3,2},{4,5},{5,4},{6,7},{7,6},{8,9},{9,8},{10,11... | collective-permute-start | bytes 1966088 | tf_op jit(solution)/shard_map/ppermute | solution.py:29
  52.2 3.5 %collective-permute-start.12 = (bf16[128,2560]{1,0:T(8,128)(2,1)S(1)}, bf16[128,2560]{1,0:T(8,128)(2,1)S(1)}, u32[]{:S(2)}, u32[]{:S(2)}) collective-permute-start(bf16[128,2560]{1,0:T(8,128)(2,1)S(1)} %collective-permute-done.2.refs_2_.refs_5_), channel_id=1, source_target_pairs={{0,1},{1,0},{2,3},{3,2},{4,5},{5,4},{6,7},{7,6},{8,9},{9,8},{10,11... | collective-permute-start | bytes 1966088 | tf_op jit(solution)/shard_map/ppermute | solution.py:29
  58.3 11.6 %collective-permute-start.13 = (bf16[128,512]{1,0:T(8,128)(2,1)S(1)}, bf16[128,512]{1,0:T(8,128)(2,1)S(1)}, u32[]{:S(2)}, u32[]{:S(2)}) collective-permute-start(bf16[128,512]{1,0:T(8,128)(2,1)S(1)} %get-tuple-element.57), channel_id=1, source_target_pairs={{0,128},{32,160},{64,192},{96,224},{128,0},{160,32},{192,64},{224,... | collective-permute-start | bytes 393224 | tf_op jit(solution)/shard_map/ppermute | solution.py:29
  61.5 8.9 %collective-permute-start.14 = (bf16[128,512]{1,0:T(8,128)(2,1)S(1)}, bf16[128,512]{1,0:T(8,128)(2,1)S(1)}, u32[]{:S(2)}, u32[]{:S(2)}) collective-permute-start(bf16[128,512]{1,0:T(8,128)(2,1)S(1)} %get-tuple-element.58), channel_id=1, source_target_pairs={{0,32},{32,64},{64,96},{96,128},{128,160},{160,192},{192,224},{224... | collective-permute-start | bytes 393224 | tf_op jit(solution)/shard_map/ppermute | solution.py:29
  62.7 15.5 %collective-permute-start.15 = (bf16[128,512]{1,0:T(8,128)(2,1)S(1)}, bf16[128,512]{1,0:T(8,128)(2,1)S(1)}, u32[]{:S(2)}, u32[]{:S(2)}) collective-permute-start(bf16[128,512]{1,0:T(8,128)(2,1)S(1)} %get-tuple-element.59), channel_id=1, source_target_pairs={{0,160},{32,192},{64,224},{96,0},{128,32},{160,64},{192,96},{224,1... | collective-permute-start | bytes 393224 | tf_op jit(solution)/shard_map/ppermute | solution.py:29
  62.8 15.4 %collective-permute-start.16 = (bf16[128,512]{1,0:T(8,128)(2,1)S(1)}, bf16[128,512]{1,0:T(8,128)(2,1)S(1)}, u32[]{:S(2)}, u32[]{:S(2)}) collective-permute-start(bf16[128,512]{1,0:T(8,128)(2,1)S(1)} %get-tuple-element.60), channel_id=1, source_target_pairs={{0,64},{32,96},{64,128},{96,160},{128,192},{160,224},{192,0},{224,... | collective-permute-start | bytes 393224 | tf_op jit(solution)/shard_map/ppermute | solution.py:29
  66.3 18.2 %collective-permute-start.17 = (bf16[128,512]{1,0:T(8,128)(2,1)S(1)}, bf16[128,512]{1,0:T(8,128)(2,1)S(1)}, u32[]{:S(2)}, u32[]{:S(2)}) collective-permute-start(bf16[128,512]{1,0:T(8,128)(2,1)S(1)} %get-tuple-element.61), channel_id=1, source_target_pairs={{0,192},{32,224},{64,0},{96,32},{128,64},{160,96},{192,128},{224,1... | collective-permute-start | bytes 393224 | tf_op jit(solution)/shard_map/ppermute | solution.py:29
  69.9 14.7 %collective-permute-start.18 = (bf16[128,512]{1,0:T(8,128)(2,1)S(1)}, bf16[128,512]{1,0:T(8,128)(2,1)S(1)}, u32[]{:S(2)}, u32[]{:S(2)}) collective-permute-start(bf16[128,512]{1,0:T(8,128)(2,1)S(1)} %get-tuple-element.62), channel_id=1, source_target_pairs={{0,96},{32,128},{64,160},{96,192},{128,224},{160,0},{192,32},{224,... | collective-permute-start | bytes 393224 | tf_op jit(solution)/shard_map/ppermute | solution.py:29
  70.4 15.4 %collective-permute-start.19 = (bf16[128,512]{1,0:T(8,128)(2,1)S(1)}, bf16[128,512]{1,0:T(8,128)(2,1)S(1)}, u32[]{:S(2)}, u32[]{:S(2)}) collective-permute-start(bf16[128,512]{1,0:T(8,128)(2,1)S(1)} %get-tuple-element.63), channel_id=1, source_target_pairs={{0,224},{32,0},{64,32},{96,64},{128,96},{160,128},{192,160},{224,1... | collective-permute-start | bytes 393224 | tf_op jit(solution)/shard_map/ppermute | solution.py:29
  85.9 2.1 %collective-permute-start.20 = (bf16[128,512]{1,0:T(8,128)(2,1)S(1)}, bf16[128,512]{1,0:T(8,128)(2,1)S(1)}, u32[]{:S(2)}, u32[]{:S(2)}) collective-permute-start(bf16[128,512]{1,0:T(8,128)(2,1)S(1)} %add_convert_fusion.mine.grad), channel_id=1, source_target_pairs={{0,1},{1,0},{2,3},{3,2},{4,5},{5,4},{6,7},{7,6},{8,9},{9,8},{10,11... | collective-permute-start | bytes 393224 | tf_op jit(solution)/shard_map/ppermute | solution.py:29
  88.5 4.8 %collective-permute-start.21 = (bf16[10,16,128]{2,1,0:T(8,128)(2,1)S(1)}, bf16[10,16,128]{2,1,0:T(8,128)(2,1)S(1)}, u32[]{:S(2)}, u32[]{:S(2)}) collective-permute-start(bf16[10,16,128]{2,1,0:T(8,128)(2,1)S(1)} %get-tuple-element.65), channel_id=1, source_target_pairs={{0,2},{2,4},{4,6},{6,0},{1,3},{3,5},{5,7},{7,1},{8,10},{10,12},{12... | collective-permute-start | bytes 122888 | tf_op jit(solution)/shard_map/ppermute | solution.py:29
  89.8 4.6 %collective-permute-start.22 = (bf16[10,16,128]{2,1,0:T(8,128)(2,1)S(1)}, bf16[10,16,128]{2,1,0:T(8,128)(2,1)S(1)}, u32[]{:S(2)}, u32[]{:S(2)}) collective-permute-start(bf16[10,16,128]{2,1,0:T(8,128)(2,1)S(1)} %get-tuple-element.66), channel_id=1, source_target_pairs={{0,4},{2,6},{4,0},{6,2},{1,5},{3,7},{5,1},{7,3},{8,12},{10,14},{12... | collective-permute-start | bytes 122888 | tf_op jit(solution)/shard_map/ppermute | solution.py:29
  92.1 3.1 %collective-permute-start.23 = (bf16[10,16,128]{2,1,0:T(8,128)(2,1)S(1)}, bf16[10,16,128]{2,1,0:T(8,128)(2,1)S(1)}, u32[]{:S(2)}, u32[]{:S(2)}) collective-permute-start(bf16[10,16,128]{2,1,0:T(8,128)(2,1)S(1)} %get-tuple-element.67), channel_id=1, source_target_pairs={{0,6},{2,0},{4,2},{6,4},{1,7},{3,1},{5,3},{7,5},{8,14},{10,8},{12,... | collective-permute-start | bytes 122888 | tf_op jit(solution)/shard_map/ppermute | solution.py:29
  96.0 15.3 %all-to-all-start = ((bf16[8,10,16,128]{3,2,1,0:T(8,128)(2,1)}), bf16[8,10,16,128]{3,2,1,0:T(8,128)(2,1)S(1)}, u32[]{:S(2)}, u32[]{:S(2)}) async-start(bf16[8,10,16,128]{3,2,1,0:T(8,128)(2,1)} %broadcast_in_dim.15), calls=%async_computation | async-start | bytes 655360 | tf_op jit(solution)/shard_map/all_to_all | solution.py:349
  111.4 0.7 copy-start.4
  112.7 5.0 %collective-permute-start.24 = (bf16[3,10,16,128]{3,2,1,0:T(8,128)(2,1)S(1)}, bf16[3,10,16,128]{3,2,1,0:T(8,128)(2,1)S(1)}, u32[]{:S(2)}, u32[]{:S(2)}) collective-permute-start(bf16[3,10,16,128]{3,2,1,0:T(8,128)(2,1)S(1)} %get-tuple-element.77), channel_id=1, source_target_pairs={{0,8},{8,16},{16,24},{24,0},{1,9},{9,17},{17,25},{25,1},{2,10},{10... | collective-permute-start | bytes 368648 | tf_op jit(solution)/shard_map/ppermute | solution.py:29
  114.1 5.2 %collective-permute-start.25 = (bf16[3,10,16,128]{3,2,1,0:T(8,128)(2,1)S(1)}, bf16[3,10,16,128]{3,2,1,0:T(8,128)(2,1)S(1)}, u32[]{:S(2)}, u32[]{:S(2)}) collective-permute-start(bf16[3,10,16,128]{3,2,1,0:T(8,128)(2,1)S(1)} %get-tuple-element.78), channel_id=1, source_target_pairs={{0,16},{8,24},{16,0},{24,8},{1,17},{9,25},{17,1},{25,9},{2,18},{10... | collective-permute-start | bytes 368648 | tf_op jit(solution)/shard_map/ppermute | solution.py:29
  114.8 4.9 %collective-permute-start.26 = (bf16[3,10,16,128]{3,2,1,0:T(8,128)(2,1)S(1)}, bf16[3,10,16,128]{3,2,1,0:T(8,128)(2,1)S(1)}, u32[]{:S(2)}, u32[]{:S(2)}) collective-permute-start(bf16[3,10,16,128]{3,2,1,0:T(8,128)(2,1)S(1)} %get-tuple-element.79), channel_id=1, source_target_pairs={{0,24},{8,0},{16,8},{24,16},{1,25},{9,1},{17,9},{25,17},{2,26},{10... | collective-permute-start | bytes 368648 | tf_op jit(solution)/shard_map/ppermute | solution.py:29
  119.7 9.6 %collective-permute-start.27 = (bf16[3,10,16,128]{3,2,1,0:T(8,128)(2,1)S(1)}, bf16[3,10,16,128]{3,2,1,0:T(8,128)(2,1)S(1)}, u32[]{:S(2)}, u32[]{:S(2)}) collective-permute-start(bf16[3,10,16,128]{3,2,1,0:T(8,128)(2,1)S(1)} %add_add_fusion.refs_0_), channel_id=1, source_target_pairs={{0,2},{2,4},{4,6},{6,0},{1,3},{3,5},{5,7},{7,1},{8,10},{10,12},{12... | collective-permute-start | bytes 368648 | tf_op jit(solution)/shard_map/ppermute | solution.py:29
  120.6 10.5 %collective-permute-start.28 = (bf16[3,10,16,128]{3,2,1,0:T(8,128)(2,1)S(1)}, bf16[3,10,16,128]{3,2,1,0:T(8,128)(2,1)S(1)}, u32[]{:S(2)}, u32[]{:S(2)}) collective-permute-start(bf16[3,10,16,128]{3,2,1,0:T(8,128)(2,1)S(1)} %add_add_fusion.refs_0_), channel_id=1, source_target_pairs={{0,4},{2,6},{4,0},{6,2},{1,5},{3,7},{5,1},{7,3},{8,12},{10,14},{12... | collective-permute-start | bytes 368648 | tf_op jit(solution)/shard_map/ppermute | solution.py:29
  122.8 10.4 %collective-permute-start.29 = (bf16[3,10,16,128]{3,2,1,0:T(8,128)(2,1)S(1)}, bf16[3,10,16,128]{3,2,1,0:T(8,128)(2,1)S(1)}, u32[]{:S(2)}, u32[]{:S(2)}) collective-permute-start(bf16[3,10,16,128]{3,2,1,0:T(8,128)(2,1)S(1)} %add_add_fusion.refs_0_), channel_id=1, source_target_pairs={{0,6},{2,0},{4,2},{6,4},{1,7},{3,1},{5,3},{7,5},{8,14},{10,8},{12,... | collective-permute-start | bytes 368648 | tf_op jit(solution)/shard_map/ppermute | solution.py:29
  123.7 10.2 %collective-permute-start.30 = (bf16[3,10,16,128]{3,2,1,0:T(8,128)(2,1)S(1)}, bf16[3,10,16,128]{3,2,1,0:T(8,128)(2,1)S(1)}, u32[]{:S(2)}, u32[]{:S(2)}) collective-permute-start(bf16[3,10,16,128]{3,2,1,0:T(8,128)(2,1)S(1)} %add_add_fusion.refs_0_), channel_id=1, source_target_pairs={{0,1},{1,0},{2,3},{3,2},{4,5},{5,4},{6,7},{7,6},{8,9},{9,8},{10,11... | collective-permute-start | bytes 368648 | tf_op jit(solution)/shard_map/ppermute | solution.py:29
  129.3 4.6 %collective-permute-start.31 = (bf16[3,10,16,128]{3,2,1,0:T(8,128)(2,1)S(1)}, bf16[3,10,16,128]{3,2,1,0:T(8,128)(2,1)S(1)}, u32[]{:S(2)}, u32[]{:S(2)}) collective-permute-start(bf16[3,10,16,128]{3,2,1,0:T(8,128)(2,1)S(1)} %collective-permute-done.27.refs_1_), channel_id=1, source_target_pairs={{0,1},{1,0},{2,3},{3,2},{4,5},{5,4},{6,7},{7,6},{8,9},{9,8},{10,11... | collective-permute-start | bytes 368648 | tf_op jit(solution)/shard_map/ppermute | solution.py:29
  131.1 3.0 %collective-permute-start.32 = (bf16[3,10,16,128]{3,2,1,0:T(8,128)(2,1)S(1)}, bf16[3,10,16,128]{3,2,1,0:T(8,128)(2,1)S(1)}, u32[]{:S(2)}, u32[]{:S(2)}) collective-permute-start(bf16[3,10,16,128]{3,2,1,0:T(8,128)(2,1)S(1)} %collective-permute-done.28.refs_2_), channel_id=1, source_target_pairs={{0,1},{1,0},{2,3},{3,2},{4,5},{5,4},{6,7},{7,6},{8,9},{9,8},{10,11... | collective-permute-start | bytes 368648 | tf_op jit(solution)/shard_map/ppermute | solution.py:29
  133.2 1.7 %collective-permute-start.33 = (bf16[3,10,16,128]{3,2,1,0:T(8,128)(2,1)S(1)}, bf16[3,10,16,128]{3,2,1,0:T(8,128)(2,1)S(1)}, u32[]{:S(2)}, u32[]{:S(2)}) collective-permute-start(bf16[3,10,16,128]{3,2,1,0:T(8,128)(2,1)S(1)} %collective-permute-done.29.refs_3_), channel_id=1, source_target_pairs={{0,1},{1,0},{2,3},{3,2},{4,5},{5,4},{6,7},{7,6},{8,9},{9,8},{10,11... | collective-permute-start | bytes 368648 | tf_op jit(solution)/shard_map/ppermute | solution.py:29

commit v3 on v2

--- a/solution.py
+++ b/solution.py
@@ -15,7 +15,6 @@
 SMEM = pl.BlockSpec(memory_space=pltpu.SMEM)
 VMEM = pl.BlockSpec(memory_space=pltpu.VMEM)
 HBM = pl.BlockSpec(memory_space=pltpu.HBM)
-CHUNKS = ((0, 1, 2, 3),)
 
 
 def vmem(mebibytes):
@@ -41,25 +40,20 @@
     return ((place[0] + k) & 3) * 4 + ((place[1] + offset) & 3)
 
 
-def pack_kernel(ks, with_cots, act, cot, *refs):
-    outs, own, sems = refs[:3], refs[3], refs[4]
+def pack_kernel(act, cot, *refs):
+    outs, sems = refs[:3], refs[3]
     place = position()
-    c = place[3]
+    half = pl.ds(pl.multiple_of(place[3] * 128, 128), 128)
     copies = []
     for o in (1, 2, 3):
         out = outs[o - 1]
-        for i, k in enumerate(ks):
+        for k in range(4):
             column = pl.multiple_of(feature_block(place, k, o) * 512, 512)
-            source = act.at[pl.ds(pl.multiple_of(c * 128, 128), 128), pl.ds(column, 512)]
-            copies.append((source, out.at[:, pl.ds(i * 512, 512)]))
-        if with_cots:
-            for h in range(2):
-                for m in range(2):
-                    lane = len(ks) * 512 + h * 256 + m * 128
-                    copies.append((cot.at[m, pl.ds(h * 128, 128), :], out.at[:, pl.ds(lane, 128)]))
-    for i, k in enumerate(ks):
-        column = pl.multiple_of(feature_block(place, k, 0) * 512, 512)
-        copies.append((act.at[:, pl.ds(column, 512)], own.at[:, pl.ds(i * 512, 512)]))
+            copies.append((act.at[half, pl.ds(column, 512)], out.at[:, pl.ds(k * 512, 512)]))
+        for h in range(2):
+            for m in range(2):
+                lane = 2048 + h * 256 + m * 128
+                copies.append((cot.at[m, pl.ds(h * 128, 128), :], out.at[:, pl.ds(lane, 128)]))
     started = []
     for n, (source, target) in enumerate(copies):
         copy = pltpu.make_async_copy(source, target, sems.at[n])
@@ -69,60 +63,105 @@
         copy.wait()
 
 
-def pack(act, cot, ks, with_cots):
-    width = len(ks) * 512 + (512 if with_cots else 0)
-    count = 3 * (len(ks) + (4 if with_cots else 0)) + len(ks)
-    return pl.pallas_call(
-        functools.partial(pack_kernel, ks, with_cots),
-        out_shape=[struct((128, width), BF)] * 3 + [struct((256, len(ks) * 512), BF)],
+def pack(act, cot):
+    return pl.pallas_call(
+        pack_kernel,
+        out_shape=[struct((128, 2560), BF)] * 3,
         in_specs=[HBM, HBM],
-        out_specs=[VMEM] * 4,
-        scratch_shapes=[pltpu.SemaphoreType.DMA((count,))],
-        compiler_params=vmem(12),
+        out_specs=[VMEM] * 3,
+        scratch_shapes=[pltpu.SemaphoreType.DMA((24,))],
+        compiler_params=vmem(60),
         name="pack",
     )(act, cot)
 
 
-def product_kernel(ks, lane0, own, cot, *refs):
-    count = 2 * len(ks)
-    cots, pieces, swaps, outs = refs[:3], refs[3:6], refs[6:9], refs[9 : 9 + count]
-    lhs, acc = refs[9 + count :]
+def own_kernel(act, own, sems):
+    place = position()
+    copies = []
+    for k in range(4):
+        column = pl.multiple_of(feature_block(place, k, 0) * 512, 512)
+        copies.append(pltpu.make_async_copy(act.at[:, pl.ds(column, 512)], own.at[:, pl.ds(k * 512, 512)], sems.at[k]))
+        copies[k].start()
+    for copy in copies:
+        copy.wait()
+
+
+def keep_own(act):
+    return pl.pallas_call(
+        own_kernel,
+        out_shape=struct((256, 2048), BF),
+        in_specs=[HBM],
+        out_specs=VMEM,
+        scratch_shapes=[pltpu.SemaphoreType.DMA((4,))],
+        compiler_params=vmem(60),
+        name="own",
+    )(act)
+
+
+def product_kernel(own, cot, *refs):
+    pieces, swaps, (kept, two, six, up, down, half0, half1), (lhs, acc) = refs[:3], refs[3:6], refs[6:13], refs[13:]
     z, _, _, c = position()
-    near = pl.multiple_of(c * 256, 256)
-    far = pl.multiple_of(256 - c * 256, 256)
+    straight = pl.multiple_of(c * 256, 256)
+    crossed = pl.multiple_of(256 - c * 256, 256)
     for m in range(2):
         lhs[pl.ds(m * 128, 128), pl.ds(0, 256)] = cot[m].T
     for o in range(3):
-        for n, lane in enumerate((near, far)):
-            lhs[:, pl.ds(256 + (2 * o + n) * 128, 128)] = cots[o][:, pl.ds(lane0 + lane, 256)].T
-    for i, k in enumerate(ks):
+        for n, lane in enumerate((straight, crossed)):
+            lhs[:, pl.ds(256 + (2 * o + n) * 128, 128)] = pieces[o][:, pl.ds(2048 + lane, 256)].T
+    for k in range(4):
         m = ((z + k) & 7) >> 2
         for half in range(2):
-            column = pl.ds(i * 512 + half * 256, 256)
+            column = pl.ds(k * 512 + half * 256, 256)
             total = jnp.dot(lhs[:, pl.ds(0, 256)], own[:, column], preferred_element_type=F32)
             for o in range(3):
                 for n, piece in enumerate((pieces[o], swaps[o])):
                     left = lhs[:, pl.ds(256 + (2 * o + n) * 128, 128)]
                     total = total + jnp.dot(left, piece[:, column], preferred_element_type=F32)
             acc[...] = total
-            for j, matrix in enumerate((m, 1 - m)):
-                row = pl.multiple_of(matrix * 128, 128)
-                out = outs[2 * i + j]
-                out[:, pl.ds(half * 256, 256)] = acc[pl.ds(row, 128), :].astype(out.dtype)
-
-
-def products(own, cot, cots, pieces, swaps, ks, lane0):
-    types = [F32 if k == 0 and j == 0 else BF for k in ks for j in range(2)]
-    return pl.pallas_call(
-        functools.partial(product_kernel, ks, lane0),
-        out_shape=[struct((128, 512), dtype) for dtype in types],
-        in_specs=[VMEM] * 11,
-        out_specs=[VMEM] * len(types),
+            lanes = pl.ds(half * 256, 256)
+            near = acc[pl.ds(pl.multiple_of(m * 128, 128), 128), :]
+            far = acc[pl.ds(pl.multiple_of(128 - m * 128, 128), 128), :]
+            if k == 0:
+                kept[:, lanes] = near
+                half0[:, lanes] = far[:64].astype(BF)
+                half1[:, lanes] = far[64:].astype(BF)
+            elif k == 2:
+                two[:, lanes] = near
+                six[:, lanes] = far
+            else:
+                up[k // 2, :, lanes] = near.astype(BF)
+                down[1 - k // 2, :, lanes] = far.astype(BF)
+
+
+def products(own, cot, pieces, swaps):
+    return pl.pallas_call(
+        product_kernel,
+        out_shape=[struct((128, 512), F32)] * 3 + [struct((2, 128, 512), BF)] * 2 + [struct((64, 512), BF)] * 2,
+        in_specs=[VMEM] * 8,
+        out_specs=[VMEM] * 7,
         scratch_shapes=[pltpu.VMEM((256, 1024), BF), pltpu.VMEM((256, 256), F32)],
-        compiler_params=vmem(16),
-        cost_estimate=pl.CostEstimate(flops=2 * 512 * 256 * 1024 * len(ks), bytes_accessed=4 << 20, transcendentals=0),
+        compiler_params=vmem(8),
+        cost_estimate=pl.CostEstimate(flops=2 * 2048 * 256 * 1024, bytes_accessed=4 << 20, transcendentals=0),
         name="products",
-    )(own, cot, *cots, *pieces, *swaps)
+    )(own, cot, *pieces, *swaps)
+
+
+def merge_kernel(two, six, up, down, low, high, ahead, back):
+    ahead[pl.ds(0, 64), :] = (two[pl.ds(0, 64), :] + up[1, pl.ds(0, 64), :].astype(F32) + low[...].astype(F32)).astype(BF)
+    ahead[pl.ds(64, 64), :] = (two[pl.ds(64, 64), :] + up[1, pl.ds(64, 64), :].astype(F32)).astype(BF)
+    back[pl.ds(0, 64), :] = (six[pl.ds(0, 64), :] + down[1, pl.ds(0, 64), :].astype(F32)).astype(BF)
+    back[pl.ds(64, 64), :] = (six[pl.ds(64, 64), :] + down[1, pl.ds(64, 64), :].astype(F32) + high[...].astype(F32)).astype(BF)
+
+
+def merge(*parts):
+    return pl.pallas_call(
+        merge_kernel,
+        out_shape=[struct((128, 512), BF)] * 2,
+        in_specs=[VMEM] * 6,
+        out_specs=[VMEM] * 2,
+        compiler_params=vmem(6),
+        name="merge",
+    )(*parts)
 
 
 def mul(left, right):
@@ -148,7 +187,7 @@
         plan[2 * o + 1] = second
         worker = worker_of[target]
         slot = lax.fori_loop(0, target, lambda b, n: n + (worker_of[b] == worker).astype(jnp.int32), jnp.int32(0))
-        plan[8 + o] = jnp.where((worker & 3) == y, ((z - (worker >> 2)) & 7) * 2 + slot, -1)
+        plan[8 + o] = jnp.where((worker & 3) == y, (worker >> 2) * 2 + slot, -1)
     for n in range(12, 16):
         plan[n] = 0
 
@@ -202,7 +241,7 @@
         out_shape=[struct((2, 512, 512), F32), struct((2, 10, 16, 128), BF), struct((2, 8, 128), F32)],
         in_specs=[SMEM, pl.BlockSpec((1, 512, 512), lambda s: (s, 0, 0))],
         out_specs=[pl.BlockSpec((1, 512, 512), lambda s: (s, 0, 0)), pl.BlockSpec((1, 10, 16, 128), lambda s: (s, 0, 0, 0)), pl.BlockSpec((1, 8, 128), lambda s: (s, 0, 0))],
-        compiler_params=vmem(32),
+        compiler_params=vmem(10),
         cost_estimate=pl.CostEstimate(flops=2 * 7 * 2 * 512**3, bytes_accessed=4 << 20, transcendentals=0),
         name="roots",
     )(worker_of, left)
@@ -234,17 +273,14 @@
     )(mine, theirs)
 
 
-def choose_kernel(plan, column, *refs):
-    roots, outs, held = refs[:8], refs[8:12], refs[12]
-    for o in range(8):
-        held[pl.ds(2 * o, 2)] = roots[o][...]
+def choose_kernel(plan, roots, column, *outs):
     for o in range(4):
         for s in range(2):
             index = plan[2 * o + s]
             item = column[jnp.maximum(index, 0)]
             outs[o][s] = jnp.where(index >= 0, item, jnp.zeros_like(item))
         index = plan[8 + o]
-        item = held[jnp.maximum(index, 0)]
+        item = roots[jnp.maximum(index, 0)]
         outs[o][2] = jnp.where(index >= 0, item, jnp.zeros_like(item))
 
 
@@ -252,12 +288,11 @@
     return pl.pallas_call(
         choose_kernel,
         out_shape=[struct((3, 10, 16, 128), BF)] * 4,
-        in_specs=[SMEM] + [VMEM] * 9,
+        in_specs=[SMEM, VMEM, VMEM],
         out_specs=[VMEM] * 4,
-        scratch_shapes=[pltpu.VMEM((16, 10, 16, 128), BF)],
         compiler_params=vmem(8),
         name="choose",
-    )(plan, column, *roots)
+    )(plan, roots, column)
 
 
 def finish_kernel(left, occupied, grad, *refs):
@@ -304,7 +339,7 @@
         + [piece] * 8,
         out_specs=[by_slot, pl.BlockSpec((512, 128), lambda s: (0, 0))],
         scratch_shapes=[pltpu.VMEM((3, 10, 128, 128), BF), pltpu.VMEM((512, 512), BF)],
-        compiler_params=vmem(16),
+        compiler_params=vmem(10),
         name="finish",
     )(left, occupied, grad, *mine, *theirs)
 
@@ -312,33 +347,22 @@
 def local(activations, cotangents, worker_of, left_stats):
     left = left_stats[0]
 
-    packed = [pack(activations, cotangents, ks, n == 0) for n, ks in enumerate(CHUNKS)]
-    sent = packed[0][:3]
-    first = arriving = [shift(p, "y", NY, o + 1) for o, p in enumerate(sent)]
+    sent = pack(activations, cotangents)
+    arrived = [shift(p, "y", NY, o + 1) for o, p in enumerate(sent)]
     later, _ = lax.optimization_barrier((left, sent))
     roots, strips, occupied = make_roots(worker_of, later)
     plan = make_plan(worker_of)
-    root_strips = [strips] + [shift(strips, "z", NZ, o) for o in range(1, 8)]
-    first, arriving, root_strips = lax.optimization_barrier((first, arriving, root_strips))
-    got, kept = [], None
-    for n, ks in enumerate(CHUNKS):
-        if n + 1 < len(CHUNKS):
-            arriving, sent = lax.optimization_barrier((arriving, packed[n + 1][:3]))
-            following = [shift(p, "y", NY, o + 1) for o, p in enumerate(sent)]
-        swapped = [shift(p, "c", NC, 1) for p in arriving]
-        parts = products(packed[n][3], cotangents, first, arriving, swapped, ks, 512 * len(CHUNKS[0]))
-        for i, k in enumerate(ks):
-            near, far = parts[2 * i : 2 * i + 2]
-            if k == 0:
-                kept = near
-            else:
-                got.append(shift(near, "z", NZ, k))
-            got.append(shift(far, "z", NZ, k + 4))
-        if n + 1 < len(CHUNKS):
-            arriving = following
-    total = kept
-    for piece in got:
-        total = total + piece.astype(F32)
+    root_strips = lax.all_to_all(jnp.broadcast_to(strips[None], (8, 2, 10, 16, 128)), "z", 0, 0, tiled=True)
+    later, _ = lax.optimization_barrier((activations, plan))
+    own = keep_own(later)
+    arrived, strips, plan, own = lax.optimization_barrier((arrived, strips, plan, own))
+    swapped = [shift(p, "c", NC, 1) for p in arrived]
+    swapped, root_strips = lax.optimization_barrier((swapped, root_strips))
+    kept, two, six, up, down, half0, half1 = products(own, cotangents, arrived, swapped)
+    up, down = shift(up, "z", NZ, 1), shift(down, "z", NZ, 7)
+    ahead, back = merge(two, six, up, down, shift(half0, "z", NZ, 2), shift(half1, "z", NZ, 6))
+    total = kept + up[0].astype(F32) + down[0].astype(F32)
+    total = total + shift(ahead, "z", NZ, 2).astype(F32) + shift(back, "z", NZ, 6).astype(F32)
     grad = total.astype(BF)
 
     theirs = shift(grad, "c", NC, 1)
@@ -347,7 +371,7 @@
         strip = strip + shift(send, "x", NX, o + 1).astype(F32)
     strip = strip.astype(BF)
     column = lax.all_to_all(jnp.broadcast_to(strip[None], (8, 10, 16, 128)), "z", 0, 0, tiled=True)
-    routed = choose(plan, root_strips, column)
+    routed = choose(plan, root_strips.reshape(16, 10, 16, 128), column)
     arrived = routed[0]
     for o in (1, 2, 3):
         arrived = arrived + shift(routed[o], "y", NY, o)

time: 137 us -> 125 us (0.912)
  waiting for transfers between devices: 48.5 us -> 29.7 us
  blocking collectives: 0 us -> 14 us
  starting transfers between devices: 66.8 us -> 55.3 us
  Pallas kernels: 15.9 us -> 22.3 us
  local copies, waits for them, and re-layouts: 4.52 us -> 2.22 us
    ppermute x34 -> x26, waiting for transfers between devices: 40.4 us -> 23.5 us  [shift(): lax.ppermute(x, axis, [(i, (i + offset) % size) for i in range(size)])]
    ppermute x34 -> x26, starting transfers between devices: 61.9 us -> 47.1 us  [shift(): lax.ppermute(x, axis, [(i, (i + offset) % size) for i in range(size)])]
    all_to_all x0 -> x1, blocking collectives: none -> 14 us  [local(): lax.all_to_all(jnp.broadcast_to(strip[None], (8, 10, 16, 128)), 'z', 0, 0...]
    pallas_call x2 -> x4, Pallas kernels: 3.28 us -> 9.78 us  [the longest x1 4.3 us: products(): pl.pallas_call(product_kernel, out_shape=[struct((128, 512), F32)] * 3 +...]
    all_to_all x1, starting transfers between devices: 4.96 us -> 8.19 us  [local(): lax.all_to_all(jnp.broadcast_to(strips[None], (8, 2, 10, 16, 128)), 'z',...]
    unnamed x12 -> x10, local copies, waits for them, and re-layouts: 3.75 us -> 1.24 us
    all_to_all x1, waiting for transfers between devices: 8.1 us -> 6.2 us  [local(): lax.all_to_all(jnp.broadcast_to(strips[None], (8, 2, 10, 16, 128)), 'z',...]
  transfers between devices with their start and end apart: 35 -> 27, of which waited for: 23 -> 10; matrix products, arithmetic and copies ran while one was open for 0% -> 1% of each run, Pallas kernels for 7% -> 10%
where the time goes in v3:
time: 125 us; the launch traced here: 124 us
  starting transfers between devices  55.3 us (44%)
  waiting for transfers between devices  29.7 us (24%)
  Pallas kernels  22.3 us (18%)
  blocking collectives  14 us (11%)
  local copies, waits for them, and re-layouts  2.22 us (2%)
    ppermute x26, starting transfers between devices, shift(): lax.ppermute(x, axis, [(i, (i + offset) % size) for i in range(size)])  47.1 us
    ppermute x26, waiting for transfers between devices, shift(): lax.ppermute(x, axis, [(i, (i + offset) % size) for i in range(size)])  23.5 us
    all_to_all x1, blocking collectives, local(): lax.all_to_all(jnp.broadcast_to(strip[None], (8, 10, 16, 128)), 'z', 0, 0...  14 us
    all_to_all x1, starting transfers between devices, local(): lax.all_to_all(jnp.broadcast_to(strips[None], (8, 2, 10, 16, 128)), 'z',...  8.19 us
    pallas_call x1, Pallas kernels, make_roots(): pl.pallas_call(root_kernel, grid=(2,), out_shape=[struct((2, 512, 512), F...  7.39 us
    all_to_all x1, waiting for transfers between devices, local(): lax.all_to_all(jnp.broadcast_to(strips[None], (8, 2, 10, 16, 128)), 'z',...  6.2 us
    pallas_call x1, Pallas kernels, products(): pl.pallas_call(product_kernel, out_shape=[struct((128, 512), F32)] * 3 +...  4.3 us
    pallas_call x1, Pallas kernels, pack(): pl.pallas_call(pack_kernel, out_shape=[struct((128, 2560), BF)] * 3, in_s...  3.16 us
  transfers between devices with their start and end apart: 27, of which 10 were waited for; matrix products, arithmetic and copies ran while one was open for 1% of the time, Pallas kernels for 10%

profile of v3, /device:TPU:1, one launch (start us, length us, event | category | flops | bytes accessed | tf_op | source)
XLA Modules:
  0.0 124.4 jit_solution(15112445556926728989)
XLA Ops:
  0.6 0.0 copy-start.4
  0.7 3.2 %pack.1 = (bf16[128,2560]{1,0:T(8,128)(2,1)}, bf16[128,2560]{1,0:T(8,128)(2,1)}, bf16[128,2560]{1,0:T(8,128)(2,1)}) custom-call(bf16[256,8192]{1,0:T(8,128)(2,1)} %act.2, bf16[2,256,128]{2,1,0:T(8,128)(2,1)} %cot.3), custom_call_target="tpu_custom_call" | custom-call | tf_op jit(solution)/shard_map/pack/pallas_call | solution.py:67
  3.8 2.2 %collective-permute-start = (bf16[128,2560]{1,0:T(8,128)(2,1)}, bf16[128,2560]{1,0:T(8,128)(2,1)S(1)}, u32[]{:S(2)}, u32[]{:S(2)}) collective-permute-start(bf16[128,2560]{1,0:T(8,128)(2,1)} %get-tuple-element.39), channel_id=1, source_target_pairs={{0,8},{8,16},{16,24},{24,0},{1,9},{9,17},{17,25},{25,1},{2,10},{10... | collective-permute-start | bytes 1966088 | tf_op jit(solution)/shard_map/ppermute | solution.py:28
  6.0 2.6 %collective-permute-start.1 = (bf16[128,2560]{1,0:T(8,128)(2,1)}, bf16[128,2560]{1,0:T(8,128)(2,1)}, u32[]{:S(2)}, u32[]{:S(2)}) collective-permute-start(bf16[128,2560]{1,0:T(8,128)(2,1)} %get-tuple-element.40), channel_id=1, source_target_pairs={{0,16},{8,24},{16,0},{24,8},{1,17},{9,25},{17,1},{25,9},{2,18},{10... | collective-permute-start | bytes 1966088 | tf_op jit(solution)/shard_map/ppermute | solution.py:28
  8.6 1.1 collective-permute-start.2
  9.7 7.4 %roots.1 = (f32[2,512,512]{2,1,0:T(8,128)}, bf16[2,10,16,128]{3,2,1,0:T(8,128)(2,1)S(1)}, f32[2,8,128]{2,1,0:T(8,128)S(1)}) custom-call(s32[32]{0:T(128)S(1)} %copy-done.4, f32[2,512,512]{2,1,0:T(8,128)S(1)} %bitcast.16), custom_call_target="tpu_custom_call" | custom-call | flops 3758096384 | bytes 4194304 | tf_op jit(solution)/shard_map/roots/pallas_call | solution.py:238
  17.1 0.9 broadcast_in_dim.10
  18.0 8.2 %all-to-all-start = ((bf16[8,2,10,16,128]{4,3,2,1,0:T(8,128)(2,1)}), bf16[8,2,10,16,128]{4,3,2,1,0:T(8,128)(2,1)S(1)}, u32[]{:S(2)}, u32[]{:S(2)}) async-start(bf16[8,2,10,16,128]{4,3,2,1,0:T(8,128)(2,1)} %broadcast_in_dim.10), calls=%async_computation | async-start | bytes 1310720 | tf_op jit(solution)/shard_map/all_to_all | solution.py:355
  26.2 2.3 %plan.1 = s32[16]{0:T(128)} custom-call(s32[32]{0:T(128)} %worker_of.3), custom_call_target="tpu_custom_call" | custom-call | tf_op jit(solution)/shard_map/plan/pallas_call | solution.py:196
  28.5 0.0 copy-start.2
  28.5 2.2 %own.1 = bf16[256,2048]{1,0:T(8,128)(2,1)} custom-call(bf16[256,8192]{1,0:T(8,128)(2,1)} %act.2), custom_call_target="tpu_custom_call" | custom-call | tf_op jit(solution)/shard_map/own/pallas_call | solution.py:90
  30.8 0.0 collective-permute-done.refs_0_
  30.8 6.4 %collective-permute-done.1.refs_1_ = bf16[128,2560]{1,0:T(8,128)(2,1)} collective-permute-done((bf16[128,2560]{1,0:T(8,128)(2,1)}, bf16[128,2560]{1,0:T(8,128)(2,1)}, u32[]{:S(2)}, u32[]{:S(2)}) %collective-permute-start.1) | collective-permute-done | bytes 655392 | tf_op jit(solution)/shard_map/ppermute | solution.py:28
  37.1 0.0 collective-permute-done.2.refs_2_
  37.1 1.5 %collective-permute-start.3 = (bf16[128,2560]{1,0:T(8,128)(2,1)S(1)}, bf16[128,2560]{1,0:T(8,128)(2,1)}, u32[]{:S(2)}, u32[]{:S(2)}) collective-permute-start(bf16[128,2560]{1,0:T(8,128)(2,1)S(1)} %collective-permute-done.refs_0_), channel_id=1, source_target_pairs={{0,1},{1,0},{2,3},{3,2},{4,5},{5,4},{6,7},{7,6},{8,9},{9,8},{10,11... | collective-permute-start | bytes 1966088 | tf_op jit(solution)/shard_map/ppermute | solution.py:28
  38.7 0.0 collective-permute-start.4
  38.7 0.5 collective-permute-start.5
  39.2 6.2 %all-to-all-done = bf16[8,2,10,16,128]{4,3,2,1,0:T(8,128)(2,1)S(1)} async-done(((bf16[8,2,10,16,128]{4,3,2,1,0:T(8,128)(2,1)}), bf16[8,2,10,16,128]{4,3,2,1,0:T(8,128)(2,1)S(1)}, u32[]{:S(2)}, u32[]{:S(2)}) %all-to-all-start) | async-done | bytes 655392 | tf_op jit(solution)/shard_map/all_to_all | solution.py:355
  45.4 0.0 copy-start
  45.4 1.2 copy-done
  46.6 4.3 %products.1 = (f32[128,512]{1,0:T(8,128)S(1)}, f32[128,512]{1,0:T(8,128)S(1)}, f32[128,512]{1,0:T(8,128)S(1)}, bf16[2,128,512]{2,1,0:T(8,128)(2,1)S(1)}, bf16[2,...) custom-call(bf16[256,2048]{1,0:T(8,128)(2,1)S(1)} %copy-done, ...), custom_call_target="tpu_custom_call" | custom-call | flops 1073741824 | bytes 4194304 | tf_op jit(solution)/shard_map/products/pallas_call | solution.py:137
  50.9 0.0 copy-start.3
  51.0 0.1 collective-permute-start.6
  51.1 2.9 %collective-permute-start.7 = (bf16[2,128,512]{2,1,0:T(8,128)(2,1)S(1)}, bf16[2,128,512]{2,1,0:T(8,128)(2,1)S(1)}, u32[]{:S(2)}, u32[]{:S(2)}) collective-permute-start(bf16[2,128,512]{2,1,0:T(8,128)(2,1)S(1)} %get-tuple-element.55), channel_id=1, source_target_pairs={{0,224},{32,0},{64,32},{96,64},{128,96},{160,128},{192,160},{224,1... | collective-permute-start | bytes 786440 | tf_op jit(solution)/shard_map/ppermute | solution.py:28
  53.9 3.6 %collective-permute-start.9 = (bf16[64,512]{1,0:T(8,128)(2,1)S(1)}, bf16[64,512]{1,0:T(8,128)(2,1)S(1)}, u32[]{:S(2)}, u32[]{:S(2)}) collective-permute-start(bf16[64,512]{1,0:T(8,128)(2,1)S(1)} %get-tuple-element.59), channel_id=1, source_target_pairs={{0,192},{32,224},{64,0},{96,32},{128,64},{160,96},{192,128},{224,1... | collective-permute-start | bytes 196616 | tf_op jit(solution)/shard_map/ppermute | solution.py:28
  57.5 5.1 %collective-permute-done.8.low = bf16[64,512]{1,0:T(8,128)(2,1)S(1)} collective-permute-done((bf16[64,512]{1,0:T(8,128)(2,1)S(1)}, bf16[64,512]{1,0:T(8,128)(2,1)S(1)}, u32[]{:S(2)}, u32[]{:S(2)}) %collective-permute-start.8) | collective-permute-done | bytes 65568 | tf_op jit(solution)/shard_map/ppermute | solution.py:28
  62.6 0.0 collective-permute-done.7.down
  62.6 0.1 merge.1
  62.7 3.7 %collective-permute-start.10 = (bf16[128,512]{1,0:T(8,128)(2,1)S(1)}, bf16[128,512]{1,0:T(8,128)(2,1)S(1)}, u32[]{:S(2)}, u32[]{:S(2)}) collective-permute-start(bf16[128,512]{1,0:T(8,128)(2,1)S(1)} %get-tuple-element.60), channel_id=1, source_target_pairs={{0,64},{32,96},{64,128},{96,160},{128,192},{160,224},{192,0},{224,... | collective-permute-start | bytes 393224 | tf_op jit(solution)/shard_map/ppermute | solution.py:28
  66.4 0.0 collective-permute-start.11
  66.4 5.6 %collective-permute-done.10 = bf16[128,512]{1,0:T(8,128)(2,1)S(1)} collective-permute-done((bf16[128,512]{1,0:T(8,128)(2,1)S(1)}, bf16[128,512]{1,0:T(8,128)(2,1)S(1)}, u32[]{:S(2)}, u32[]{:S(2)}) %collective-permute-start.10) | collective-permute-done | bytes 131104 | tf_op jit(solution)/shard_map/ppermute | solution.py:28
  72.0 0.0 collective-permute-done.11
  72.0 0.1 fusion.2.mine.grad
  72.1 3.7 %collective-permute-start.12 = (bf16[128,512]{1,0:T(8,128)(2,1)S(1)}, bf16[128,512]{1,0:T(8,128)(2,1)S(1)}, u32[]{:S(2)}, u32[]{:S(2)}) collective-permute-start(bf16[128,512]{1,0:T(8,128)(2,1)S(1)} %fusion.2.mine.grad), channel_id=1, source_target_pairs={{0,1},{1,0},{2,3},{3,2},{4,5},{5,4},{6,7},{7,6},{8,9},{9,8},{10,11... | collective-permute-start | bytes 393224 | tf_op jit(solution)/shard_map/ppermute | solution.py:28
  75.8 1.0 collective-permute-done.12.theirs
  76.7 0.4 grams.1
  77.2 1.3 %collective-permute-start.13 = (bf16[10,16,128]{2,1,0:T(8,128)(2,1)S(1)}, bf16[10,16,128]{2,1,0:T(8,128)(2,1)S(1)}, u32[]{:S(2)}, u32[]{:S(2)}) collective-permute-start(bf16[10,16,128]{2,1,0:T(8,128)(2,1)S(1)} %get-tuple-element.65), channel_id=1, source_target_pairs={{0,2},{2,4},{4,6},{6,0},{1,3},{3,5},{5,7},{7,1},{8,10},{10,12},{12... | collective-permute-start | bytes 122888 | tf_op jit(solution)/shard_map/ppermute | solution.py:28
  78.5 2.4 %collective-permute-start.14 = (bf16[10,16,128]{2,1,0:T(8,128)(2,1)S(1)}, bf16[10,16,128]{2,1,0:T(8,128)(2,1)S(1)}, u32[]{:S(2)}, u32[]{:S(2)}) collective-permute-start(bf16[10,16,128]{2,1,0:T(8,128)(2,1)S(1)} %get-tuple-element.66), channel_id=1, source_target_pairs={{0,4},{2,6},{4,0},{6,2},{1,5},{3,7},{5,1},{7,3},{8,12},{10,14},{12... | collective-permute-start | bytes 122888 | tf_op jit(solution)/shard_map/ppermute | solution.py:28
  80.9 1.2 collective-permute-start.15
  82.0 0.0 collective-permute-done.13
  82.0 0.9 collective-permute-done.14
  83.0 1.0 collective-permute-done.15
  84.1 14.0 %all_to_all.10.column = bf16[8,10,16,128]{3,2,1,0:T(8,128)(2,1)S(1)} all-to-all(bf16[8,10,16,128]{3,2,1,0:T(8,128)(2,1)S(1)} %broadcast_in_dim.22), channel_id=1, replica_groups=mesh['z'=8,'y'=4,'x'=4,'c'=2] {'z'}, dimensions={0} | all-to-all | bytes 655360 | tf_op jit(solution)/shard_map/all_to_all | solution.py:373
  98.1 0.7 choose.1
  98.8 1.0 collective-permute-start.16
  99.8 2.8 %collective-permute-start.17 = (bf16[3,10,16,128]{3,2,1,0:T(8,128)(2,1)S(1)}, bf16[3,10,16,128]{3,2,1,0:T(8,128)(2,1)S(1)}, u32[]{:S(2)}, u32[]{:S(2)}) collective-permute-start(bf16[3,10,16,128]{3,2,1,0:T(8,128)(2,1)S(1)} %get-tuple-element.70), channel_id=1, source_target_pairs={{0,16},{8,24},{16,0},{24,8},{1,17},{9,25},{17,1},{25,9},{2,18},{10... | collective-permute-start | bytes 368648 | tf_op jit(solution)/shard_map/ppermute | solution.py:28
  102.6 1.3 %collective-permute-start.18 = (bf16[3,10,16,128]{3,2,1,0:T(8,128)(2,1)S(1)}, bf16[3,10,16,128]{3,2,1,0:T(8,128)(2,1)S(1)}, u32[]{:S(2)}, u32[]{:S(2)}) collective-permute-start(bf16[3,10,16,128]{3,2,1,0:T(8,128)(2,1)S(1)} %get-tuple-element.71), channel_id=1, source_target_pairs={{0,24},{8,0},{16,8},{24,16},{1,25},{9,1},{17,9},{25,17},{2,26},{10... | collective-permute-start | bytes 368648 | tf_op jit(solution)/shard_map/ppermute | solution.py:28
  103.9 2.3 %collective-permute-done.17 = bf16[3,10,16,128]{3,2,1,0:T(8,128)(2,1)S(1)} collective-permute-done((bf16[3,10,16,128]{3,2,1,0:T(8,128)(2,1)S(1)}, bf16[3,10,16,128]{3,2,1,0:T(8,128)(2,1)S(1)}, u32[]{:S(2)}, u32[]{:S(2)}) %collective-permute-start.17) | collective-permute-done | bytes 122912 | tf_op jit(solution)/shard_map/ppermute | solution.py:28
  106.1 0.1 collective-permute-done.18
  106.3 1.6 %collective-permute-start.21 = (bf16[3,10,16,128]{3,2,1,0:T(8,128)(2,1)S(1)}, bf16[3,10,16,128]{3,2,1,0:T(8,128)(2,1)S(1)}, u32[]{:S(2)}, u32[]{:S(2)}) collective-permute-start(bf16[3,10,16,128]{3,2,1,0:T(8,128)(2,1)S(1)} %add_add_fusion.refs_0_), channel_id=1, source_target_pairs={{0,6},{2,0},{4,2},{6,4},{1,7},{3,1},{5,3},{7,5},{8,14},{10,8},{12,... | collective-permute-start | bytes 368648 | tf_op jit(solution)/shard_map/ppermute | solution.py:28
  107.9 0.2 collective-permute-start.20
  108.1 0.5 collective-permute-start.19
  108.6 6.6 %collective-permute-start.22 = (bf16[3,10,16,128]{3,2,1,0:T(8,128)(2,1)S(1)}, bf16[3,10,16,128]{3,2,1,0:T(8,128)(2,1)S(1)}, u32[]{:S(2)}, u32[]{:S(2)}) collective-permute-start(bf16[3,10,16,128]{3,2,1,0:T(8,128)(2,1)S(1)} %add_add_fusion.refs_0_), channel_id=1, source_target_pairs={{0,1},{1,0},{2,3},{3,2},{4,5},{5,4},{6,7},{7,6},{8,9},{9,8},{10,11... | collective-permute-start | bytes 368648 | tf_op jit(solution)/shard_map/ppermute | solution.py:28
  115.2 0.0 collective-permute-done.21.refs_3_
  115.2 2.8 %collective-permute-start.25 = (bf16[3,10,16,128]{3,2,1,0:T(8,128)(2,1)S(1)}, bf16[3,10,16,128]{3,2,1,0:T(8,128)(2,1)S(1)}, u32[]{:S(2)}, u32[]{:S(2)}) collective-permute-start(bf16[3,10,16,128]{3,2,1,0:T(8,128)(2,1)S(1)} %collective-permute-done.21.refs_3_), channel_id=1, source_target_pairs={{0,1},{1,0},{2,3},{3,2},{4,5},{5,4},{6,7},{7,6},{8,9},{9,8},{10,11... | collective-permute-start | bytes 368648 | tf_op jit(solution)/shard_map/ppermute | solution.py:28
  118.0 0.0 collective-permute-done.20.refs_2_
  118.0 2.7 %collective-permute-start.24 = (bf16[3,10,16,128]{3,2,1,0:T(8,128)(2,1)S(1)}, bf16[3,10,16,128]{3,2,1,0:T(8,128)(2,1)S(1)}, u32[]{:S(2)}, u32[]{:S(2)}) collective-permute-start(bf16[3,10,16,128]{3,2,1,0:T(8,128)(2,1)S(1)} %collective-permute-done.20.refs_2_), channel_id=1, source_target_pairs={{0,1},{1,0},{2,3},{3,2},{4,5},{5,4},{6,7},{7,6},{8,9},{9,8},{10,11... | collective-permute-start | bytes 368648 | tf_op jit(solution)/shard_map/ppermute | solution.py:28
  120.7 0.0 collective-permute-done.19.refs_1_
  120.7 0.9 collective-permute-start.23
  121.6 0.0 collective-permute-done.22.refs_4_
  121.6 0.0 collective-permute-done.25.refs_7_
  121.6 0.0 collective-permute-done.24.refs_6_
  121.7 0.9 collective-permute-done.23.refs_5_
  122.6 1.8 %finish.1 = (f32[2,512,512]{2,1,0:T(8,128)}, bf16[512,128]{1,0:T(8,128)(2,1)}) custom-call(f32[2,512,512]{2,1,0:T(8,128)S(1)} %bitcast.17, f32[2,8,128]{2,1,0:T(8,128)S(1)} %get-tuple-element.43.occupied, bf16[128,512]{1,0:T(8,128)(2,1)S(1)} %fusion.2.mine.grad, bf16[3,10,16,128]{3,2,1,0:T(8,128)(2,1)S(1)} %add_add_fusion.refs_0_, ...), custom_call_target="tpu_custom_call" | custom-call | tf_op jit(solution)/shard_map/finish/pallas_call | solution.py:334
  (15 shorter events, 0.1 us)
Async XLA Ops:
  0.6 9.1 %copy-start.1 = (f32[1,2,512,512]{3,2,1,0:T(8,128)S(1)}, f32[1,2,512,512]{3,2,1,0:T(8,128)}, u32[]{:S(2)}) copy-start(f32[1,2,512,512]{3,2,1,0:T(8,128)} %param.7) | copy-start | bytes 6291460
  0.6 9.1 %copy-start.4 = (s32[32]{0:T(128)S(1)}, s32[32]{0:T(128)}, u32[]{:S(2)}) copy-start(s32[32]{0:T(128)} %worker_of.3) | copy-start | bytes 388
  3.8 26.9 %collective-permute-start = (bf16[128,2560]{1,0:T(8,128)(2,1)}, bf16[128,2560]{1,0:T(8,128)(2,1)S(1)}, u32[]{:S(2)}, u32[]{:S(2)}) collective-permute-start(bf16[128,2560]{1,0:T(8,128)(2,1)} %get-tuple-element.39), channel_id=1, source_target_pairs={{0,8},{8,16},{16,24},{24,0},{1,9},{9,17},{17,25},{25,1},{2,10},{10... | collective-permute-start | bytes 1966088 | tf_op jit(solution)/shard_map/ppermute | solution.py:28
  6.0 31.1 %collective-permute-start.1 = (bf16[128,2560]{1,0:T(8,128)(2,1)}, bf16[128,2560]{1,0:T(8,128)(2,1)}, u32[]{:S(2)}, u32[]{:S(2)}) collective-permute-start(bf16[128,2560]{1,0:T(8,128)(2,1)} %get-tuple-element.40), channel_id=1, source_target_pairs={{0,16},{8,24},{16,0},{24,8},{1,17},{9,25},{17,1},{25,9},{2,18},{10... | collective-permute-start | bytes 1966088 | tf_op jit(solution)/shard_map/ppermute | solution.py:28
  8.6 28.5 %collective-permute-start.2 = (bf16[128,2560]{1,0:T(8,128)(2,1)}, bf16[128,2560]{1,0:T(8,128)(2,1)}, u32[]{:S(2)}, u32[]{:S(2)}) collective-permute-start(bf16[128,2560]{1,0:T(8,128)(2,1)} %get-tuple-element.41), channel_id=1, source_target_pairs={{0,24},{8,0},{16,8},{24,16},{1,25},{9,1},{17,9},{25,17},{2,26},{10... | collective-permute-start | bytes 1966088 | tf_op jit(solution)/shard_map/ppermute | solution.py:28
  18.0 27.4 %all-to-all-start = ((bf16[8,2,10,16,128]{4,3,2,1,0:T(8,128)(2,1)}), bf16[8,2,10,16,128]{4,3,2,1,0:T(8,128)(2,1)S(1)}, u32[]{:S(2)}, u32[]{:S(2)}) async-start(bf16[8,2,10,16,128]{4,3,2,1,0:T(8,128)(2,1)} %broadcast_in_dim.10), calls=%async_computation | async-start | bytes 1310720 | tf_op jit(solution)/shard_map/all_to_all | solution.py:355
  28.5 16.9 %copy-start.2 = (bf16[2,256,128]{2,1,0:T(8,128)(2,1)S(1)}, bf16[2,256,128]{2,1,0:T(8,128)(2,1)}, u32[]{:S(2)}) copy-start(bf16[2,256,128]{2,1,0:T(8,128)(2,1)} %cot.3) | copy-start | bytes 393220
  37.1 8.3 %collective-permute-start.3 = (bf16[128,2560]{1,0:T(8,128)(2,1)S(1)}, bf16[128,2560]{1,0:T(8,128)(2,1)}, u32[]{:S(2)}, u32[]{:S(2)}) collective-permute-start(bf16[128,2560]{1,0:T(8,128)(2,1)S(1)} %collective-permute-done.refs_0_), channel_id=1, source_target_pairs={{0,1},{1,0},{2,3},{3,2},{4,5},{5,4},{6,7},{7,6},{8,9},{9,8},{10,11... | collective-permute-start | bytes 1966088 | tf_op jit(solution)/shard_map/ppermute | solution.py:28
  38.7 6.7 %collective-permute-start.4 = (bf16[128,2560]{1,0:T(8,128)(2,1)}, bf16[128,2560]{1,0:T(8,128)(2,1)}, u32[]{:S(2)}, u32[]{:S(2)}) collective-permute-start(bf16[128,2560]{1,0:T(8,128)(2,1)} %collective-permute-done.1.refs_1_), channel_id=1, source_target_pairs={{0,1},{1,0},{2,3},{3,2},{4,5},{5,4},{6,7},{7,6},{8,9},{9,8},{10,11... | collective-permute-start | bytes 1966088 | tf_op jit(solution)/shard_map/ppermute | solution.py:28
  38.7 6.7 %collective-permute-start.5 = (bf16[128,2560]{1,0:T(8,128)(2,1)}, bf16[128,2560]{1,0:T(8,128)(2,1)}, u32[]{:S(2)}, u32[]{:S(2)}) collective-permute-start(bf16[128,2560]{1,0:T(8,128)(2,1)} %collective-permute-done.2.refs_2_), channel_id=1, source_target_pairs={{0,1},{1,0},{2,3},{3,2},{4,5},{5,4},{6,7},{7,6},{8,9},{9,8},{10,11... | collective-permute-start | bytes 1966088 | tf_op jit(solution)/shard_map/ppermute | solution.py:28
  45.4 1.2 copy-start
  50.9 47.1 %copy-start.3 = (s32[16]{0:T(128)S(1)}, s32[16]{0:T(128)}, u32[]{:S(2)}) copy-start(s32[16]{0:T(128)} %plan.1) | copy-start | bytes 196
  51.0 11.6 %collective-permute-start.6 = (bf16[2,128,512]{2,1,0:T(8,128)(2,1)S(1)}, bf16[2,128,512]{2,1,0:T(8,128)(2,1)S(1)}, u32[]{:S(2)}, u32[]{:S(2)}) collective-permute-start(bf16[2,128,512]{2,1,0:T(8,128)(2,1)S(1)} %get-tuple-element.54), channel_id=1, source_target_pairs={{0,32},{32,64},{64,96},{96,128},{128,160},{160,192},{192,224},{224... | collective-permute-start | bytes 786440 | tf_op jit(solution)/shard_map/ppermute | solution.py:28
  51.1 11.6 %collective-permute-start.7 = (bf16[2,128,512]{2,1,0:T(8,128)(2,1)S(1)}, bf16[2,128,512]{2,1,0:T(8,128)(2,1)S(1)}, u32[]{:S(2)}, u32[]{:S(2)}) collective-permute-start(bf16[2,128,512]{2,1,0:T(8,128)(2,1)S(1)} %get-tuple-element.55), channel_id=1, source_target_pairs={{0,224},{32,0},{64,32},{96,64},{128,96},{160,128},{192,160},{224,1... | collective-permute-start | bytes 786440 | tf_op jit(solution)/shard_map/ppermute | solution.py:28
  53.9 8.7 %collective-permute-start.8 = (bf16[64,512]{1,0:T(8,128)(2,1)S(1)}, bf16[64,512]{1,0:T(8,128)(2,1)S(1)}, u32[]{:S(2)}, u32[]{:S(2)}) collective-permute-start(bf16[64,512]{1,0:T(8,128)(2,1)S(1)} %get-tuple-element.58), channel_id=1, source_target_pairs={{0,64},{32,96},{64,128},{96,160},{128,192},{160,224},{192,0},{224,... | collective-permute-start | bytes 196616 | tf_op jit(solution)/shard_map/ppermute | solution.py:28
  53.9 8.7 %collective-permute-start.9 = (bf16[64,512]{1,0:T(8,128)(2,1)S(1)}, bf16[64,512]{1,0:T(8,128)(2,1)S(1)}, u32[]{:S(2)}, u32[]{:S(2)}) collective-permute-start(bf16[64,512]{1,0:T(8,128)(2,1)S(1)} %get-tuple-element.59), channel_id=1, source_target_pairs={{0,192},{32,224},{64,0},{96,32},{128,64},{160,96},{192,128},{224,1... | collective-permute-start | bytes 196616 | tf_op jit(solution)/shard_map/ppermute | solution.py:28
  62.7 9.3 %collective-permute-start.10 = (bf16[128,512]{1,0:T(8,128)(2,1)S(1)}, bf16[128,512]{1,0:T(8,128)(2,1)S(1)}, u32[]{:S(2)}, u32[]{:S(2)}) collective-permute-start(bf16[128,512]{1,0:T(8,128)(2,1)S(1)} %get-tuple-element.60), channel_id=1, source_target_pairs={{0,64},{32,96},{64,128},{96,160},{128,192},{160,224},{192,0},{224,... | collective-permute-start | bytes 393224 | tf_op jit(solution)/shard_map/ppermute | solution.py:28
  66.4 5.6 %collective-permute-start.11 = (bf16[128,512]{1,0:T(8,128)(2,1)S(1)}, bf16[128,512]{1,0:T(8,128)(2,1)S(1)}, u32[]{:S(2)}, u32[]{:S(2)}) collective-permute-start(bf16[128,512]{1,0:T(8,128)(2,1)S(1)} %get-tuple-element.61), channel_id=1, source_target_pairs={{0,192},{32,224},{64,0},{96,32},{128,64},{160,96},{192,128},{224,1... | collective-permute-start | bytes 393224 | tf_op jit(solution)/shard_map/ppermute | solution.py:28
  72.1 4.7 %collective-permute-start.12 = (bf16[128,512]{1,0:T(8,128)(2,1)S(1)}, bf16[128,512]{1,0:T(8,128)(2,1)S(1)}, u32[]{:S(2)}, u32[]{:S(2)}) collective-permute-start(bf16[128,512]{1,0:T(8,128)(2,1)S(1)} %fusion.2.mine.grad), channel_id=1, source_target_pairs={{0,1},{1,0},{2,3},{3,2},{4,5},{5,4},{6,7},{7,6},{8,9},{9,8},{10,11... | collective-permute-start | bytes 393224 | tf_op jit(solution)/shard_map/ppermute | solution.py:28
  77.2 4.9 %collective-permute-start.13 = (bf16[10,16,128]{2,1,0:T(8,128)(2,1)S(1)}, bf16[10,16,128]{2,1,0:T(8,128)(2,1)S(1)}, u32[]{:S(2)}, u32[]{:S(2)}) collective-permute-start(bf16[10,16,128]{2,1,0:T(8,128)(2,1)S(1)} %get-tuple-element.65), channel_id=1, source_target_pairs={{0,2},{2,4},{4,6},{6,0},{1,3},{3,5},{5,7},{7,1},{8,10},{10,12},{12... | collective-permute-start | bytes 122888 | tf_op jit(solution)/shard_map/ppermute | solution.py:28
  78.5 4.5 %collective-permute-start.14 = (bf16[10,16,128]{2,1,0:T(8,128)(2,1)S(1)}, bf16[10,16,128]{2,1,0:T(8,128)(2,1)S(1)}, u32[]{:S(2)}, u32[]{:S(2)}) collective-permute-start(bf16[10,16,128]{2,1,0:T(8,128)(2,1)S(1)} %get-tuple-element.66), channel_id=1, source_target_pairs={{0,4},{2,6},{4,0},{6,2},{1,5},{3,7},{5,1},{7,3},{8,12},{10,14},{12... | collective-permute-start | bytes 122888 | tf_op jit(solution)/shard_map/ppermute | solution.py:28
  80.9 3.1 %collective-permute-start.15 = (bf16[10,16,128]{2,1,0:T(8,128)(2,1)S(1)}, bf16[10,16,128]{2,1,0:T(8,128)(2,1)S(1)}, u32[]{:S(2)}, u32[]{:S(2)}) collective-permute-start(bf16[10,16,128]{2,1,0:T(8,128)(2,1)S(1)} %get-tuple-element.67), channel_id=1, source_target_pairs={{0,6},{2,0},{4,2},{6,4},{1,7},{3,1},{5,3},{7,5},{8,14},{10,8},{12,... | collective-permute-start | bytes 122888 | tf_op jit(solution)/shard_map/ppermute | solution.py:28
  98.8 5.1 %collective-permute-start.16 = (bf16[3,10,16,128]{3,2,1,0:T(8,128)(2,1)S(1)}, bf16[3,10,16,128]{3,2,1,0:T(8,128)(2,1)S(1)}, u32[]{:S(2)}, u32[]{:S(2)}) collective-permute-start(bf16[3,10,16,128]{3,2,1,0:T(8,128)(2,1)S(1)} %get-tuple-element.69), channel_id=1, source_target_pairs={{0,8},{8,16},{16,24},{24,0},{1,9},{9,17},{17,25},{25,1},{2,10},{10... | collective-permute-start | bytes 368648 | tf_op jit(solution)/shard_map/ppermute | solution.py:28
  99.8 6.3 %collective-permute-start.17 = (bf16[3,10,16,128]{3,2,1,0:T(8,128)(2,1)S(1)}, bf16[3,10,16,128]{3,2,1,0:T(8,128)(2,1)S(1)}, u32[]{:S(2)}, u32[]{:S(2)}) collective-permute-start(bf16[3,10,16,128]{3,2,1,0:T(8,128)(2,1)S(1)} %get-tuple-element.70), channel_id=1, source_target_pairs={{0,16},{8,24},{16,0},{24,8},{1,17},{9,25},{17,1},{25,9},{2,18},{10... | collective-permute-start | bytes 368648 | tf_op jit(solution)/shard_map/ppermute | solution.py:28
  102.6 3.7 %collective-permute-start.18 = (bf16[3,10,16,128]{3,2,1,0:T(8,128)(2,1)S(1)}, bf16[3,10,16,128]{3,2,1,0:T(8,128)(2,1)S(1)}, u32[]{:S(2)}, u32[]{:S(2)}) collective-permute-start(bf16[3,10,16,128]{3,2,1,0:T(8,128)(2,1)S(1)} %get-tuple-element.71), channel_id=1, source_target_pairs={{0,24},{8,0},{16,8},{24,16},{1,25},{9,1},{17,9},{25,17},{2,26},{10... | collective-permute-start | bytes 368648 | tf_op jit(solution)/shard_map/ppermute | solution.py:28
  106.3 8.9 %collective-permute-start.21 = (bf16[3,10,16,128]{3,2,1,0:T(8,128)(2,1)S(1)}, bf16[3,10,16,128]{3,2,1,0:T(8,128)(2,1)S(1)}, u32[]{:S(2)}, u32[]{:S(2)}) collective-permute-start(bf16[3,10,16,128]{3,2,1,0:T(8,128)(2,1)S(1)} %add_add_fusion.refs_0_), channel_id=1, source_target_pairs={{0,6},{2,0},{4,2},{6,4},{1,7},{3,1},{5,3},{7,5},{8,14},{10,8},{12,... | collective-permute-start | bytes 368648 | tf_op jit(solution)/shard_map/ppermute | solution.py:28
  107.9 10.1 %collective-permute-start.20 = (bf16[3,10,16,128]{3,2,1,0:T(8,128)(2,1)S(1)}, bf16[3,10,16,128]{3,2,1,0:T(8,128)(2,1)S(1)}, u32[]{:S(2)}, u32[]{:S(2)}) collective-permute-start(bf16[3,10,16,128]{3,2,1,0:T(8,128)(2,1)S(1)} %add_add_fusion.refs_0_), channel_id=1, source_target_pairs={{0,4},{2,6},{4,0},{6,2},{1,5},{3,7},{5,1},{7,3},{8,12},{10,14},{12... | collective-permute-start | bytes 368648 | tf_op jit(solution)/shard_map/ppermute | solution.py:28
  108.1 12.6 %collective-permute-start.19 = (bf16[3,10,16,128]{3,2,1,0:T(8,128)(2,1)S(1)}, bf16[3,10,16,128]{3,2,1,0:T(8,128)(2,1)S(1)}, u32[]{:S(2)}, u32[]{:S(2)}) collective-permute-start(bf16[3,10,16,128]{3,2,1,0:T(8,128)(2,1)S(1)} %add_add_fusion.refs_0_), channel_id=1, source_target_pairs={{0,2},{2,4},{4,6},{6,0},{1,3},{3,5},{5,7},{7,1},{8,10},{10,12},{12... | collective-permute-start | bytes 368648 | tf_op jit(solution)/shard_map/ppermute | solution.py:28
  108.6 13.1 %collective-permute-start.22 = (bf16[3,10,16,128]{3,2,1,0:T(8,128)(2,1)S(1)}, bf16[3,10,16,128]{3,2,1,0:T(8,128)(2,1)S(1)}, u32[]{:S(2)}, u32[]{:S(2)}) collective-permute-start(bf16[3,10,16,128]{3,2,1,0:T(8,128)(2,1)S(1)} %add_add_fusion.refs_0_), channel_id=1, source_target_pairs={{0,1},{1,0},{2,3},{3,2},{4,5},{5,4},{6,7},{7,6},{8,9},{9,8},{10,11... | collective-permute-start | bytes 368648 | tf_op jit(solution)/shard_map/ppermute | solution.py:28
  115.2 6.5 %collective-permute-start.25 = (bf16[3,10,16,128]{3,2,1,0:T(8,128)(2,1)S(1)}, bf16[3,10,16,128]{3,2,1,0:T(8,128)(2,1)S(1)}, u32[]{:S(2)}, u32[]{:S(2)}) collective-permute-start(bf16[3,10,16,128]{3,2,1,0:T(8,128)(2,1)S(1)} %collective-permute-done.21.refs_3_), channel_id=1, source_target_pairs={{0,1},{1,0},{2,3},{3,2},{4,5},{5,4},{6,7},{7,6},{8,9},{9,8},{10,11... | collective-permute-start | bytes 368648 | tf_op jit(solution)/shard_map/ppermute | solution.py:28
  118.0 3.7 %collective-permute-start.24 = (bf16[3,10,16,128]{3,2,1,0:T(8,128)(2,1)S(1)}, bf16[3,10,16,128]{3,2,1,0:T(8,128)(2,1)S(1)}, u32[]{:S(2)}, u32[]{:S(2)}) collective-permute-start(bf16[3,10,16,128]{3,2,1,0:T(8,128)(2,1)S(1)} %collective-permute-done.20.refs_2_), channel_id=1, source_target_pairs={{0,1},{1,0},{2,3},{3,2},{4,5},{5,4},{6,7},{7,6},{8,9},{9,8},{10,11... | collective-permute-start | bytes 368648 | tf_op jit(solution)/shard_map/ppermute | solution.py:28
  120.7 1.9 %collective-permute-start.23 = (bf16[3,10,16,128]{3,2,1,0:T(8,128)(2,1)S(1)}, bf16[3,10,16,128]{3,2,1,0:T(8,128)(2,1)S(1)}, u32[]{:S(2)}, u32[]{:S(2)}) collective-permute-start(bf16[3,10,16,128]{3,2,1,0:T(8,128)(2,1)S(1)} %collective-permute-done.19.refs_1_), channel_id=1, source_target_pairs={{0,1},{1,0},{2,3},{3,2},{4,5},{5,4},{6,7},{7,6},{8,9},{9,8},{10,11... | collective-permute-start | bytes 368648 | tf_op jit(solution)/shard_map/ppermute | solution.py:28

commit v4 on v3

--- a/solution.py
+++ b/solution.py
@@ -93,34 +93,59 @@
         in_specs=[HBM],
         out_specs=VMEM,
         scratch_shapes=[pltpu.SemaphoreType.DMA((4,))],
-        compiler_params=vmem(60),
+        compiler_params=vmem(8),
         name="own",
     )(act)
 
 
-def product_kernel(own, cot, *refs):
-    pieces, swaps, (kept, two, six, up, down, half0, half1), (lhs, acc) = refs[:3], refs[3:6], refs[6:13], refs[13:]
-    z, _, _, c = position()
+def first_kernel(own, cot, *refs):
+    pieces, acc, crossed, lhs = refs[:3], refs[3], refs[4], refs[5]
+    c = position()[3]
     straight = pl.multiple_of(c * 256, 256)
-    crossed = pl.multiple_of(256 - c * 256, 256)
+    other = pl.multiple_of(256 - c * 256, 256)
     for m in range(2):
         lhs[pl.ds(m * 128, 128), pl.ds(0, 256)] = cot[m].T
     for o in range(3):
-        for n, lane in enumerate((straight, crossed)):
-            lhs[:, pl.ds(256 + (2 * o + n) * 128, 128)] = pieces[o][:, pl.ds(2048 + lane, 256)].T
+        lhs[:, pl.ds(256 + o * 128, 128)] = pieces[o][:, pl.ds(2048 + straight, 256)].T
+        crossed[:, pl.ds(o * 128, 128)] = pieces[o][:, pl.ds(2048 + other, 256)].T
+    for n in range(8):
+        column = pl.ds(n * 256, 256)
+        total = jnp.dot(lhs[:, pl.ds(0, 256)], own[:, column], preferred_element_type=F32)
+        for o in range(3):
+            left = lhs[:, pl.ds(256 + o * 128, 128)]
+            total = total + jnp.dot(left, pieces[o][:, column], preferred_element_type=F32)
+        acc[:, column] = total
+
+
+def first_products(own, cot, pieces):
+    return pl.pallas_call(
+        first_kernel,
+        out_shape=[struct((256, 2048), F32), struct((256, 384), BF)],
+        in_specs=[VMEM] * 5,
+        out_specs=[VMEM] * 2,
+        scratch_shapes=[pltpu.VMEM((256, 640), BF)],
+        compiler_params=vmem(10),
+        cost_estimate=pl.CostEstimate(flops=2048 * 256 * 1024, bytes_accessed=4 << 20, transcendentals=0),
+        name="first",
+    )(own, cot, *pieces)
+
+
+def second_kernel(acc, crossed, *refs):
+    swaps, (kept, two, six, up, down, half0, half1, total) = refs[:3], refs[3:]
+    z = position()[0]
     for k in range(4):
         m = ((z + k) & 7) >> 2
         for half in range(2):
             column = pl.ds(k * 512 + half * 256, 256)
-            total = jnp.dot(lhs[:, pl.ds(0, 256)], own[:, column], preferred_element_type=F32)
+            value = acc[:, column]
             for o in range(3):
-                for n, piece in enumerate((pieces[o], swaps[o])):
-                    left = lhs[:, pl.ds(256 + (2 * o + n) * 128, 128)]
-                    total = total + jnp.dot(left, piece[:, column], preferred_element_type=F32)
-            acc[...] = total
+                value = value + jnp.dot(
+                    crossed[:, pl.ds(o * 128, 128)], swaps[o][:, column], preferred_element_type=F32
+                )
+            total[...] = value
             lanes = pl.ds(half * 256, 256)
-            near = acc[pl.ds(pl.multiple_of(m * 128, 128), 128), :]
-            far = acc[pl.ds(pl.multiple_of(128 - m * 128, 128), 128), :]
+            near = total[pl.ds(pl.multiple_of(m * 128, 128), 128), :]
+            far = total[pl.ds(pl.multiple_of(128 - m * 128, 128), 128), :]
             if k == 0:
                 kept[:, lanes] = near
                 half0[:, lanes] = far[:64].astype(BF)
@@ -133,17 +158,17 @@
                 down[1 - k // 2, :, lanes] = far.astype(BF)
 
 
-def products(own, cot, pieces, swaps):
-    return pl.pallas_call(
-        product_kernel,
+def second_products(acc, crossed, swaps):
+    return pl.pallas_call(
+        second_kernel,
         out_shape=[struct((128, 512), F32)] * 3 + [struct((2, 128, 512), BF)] * 2 + [struct((64, 512), BF)] * 2,
-        in_specs=[VMEM] * 8,
+        in_specs=[VMEM] * 5,
         out_specs=[VMEM] * 7,
-        scratch_shapes=[pltpu.VMEM((256, 1024), BF), pltpu.VMEM((256, 256), F32)],
-        compiler_params=vmem(8),
-        cost_estimate=pl.CostEstimate(flops=2 * 2048 * 256 * 1024, bytes_accessed=4 << 20, transcendentals=0),
-        name="products",
-    )(own, cot, *pieces, *swaps)
+        scratch_shapes=[pltpu.VMEM((256, 256), F32)],
+        compiler_params=vmem(10),
+        cost_estimate=pl.CostEstimate(flops=2048 * 256 * 1024, bytes_accessed=4 << 20, transcendentals=0),
+        name="second",
+    )(acc, crossed, *swaps)
 
 
 def merge_kernel(two, six, up, down, low, high, ahead, back):
@@ -357,10 +382,11 @@
     own = keep_own(later)
     arrived, strips, plan, own = lax.optimization_barrier((arrived, strips, plan, own))
     swapped = [shift(p, "c", NC, 1) for p in arrived]
-    swapped, root_strips = lax.optimization_barrier((swapped, root_strips))
-    kept, two, six, up, down, half0, half1 = products(own, cotangents, arrived, swapped)
+    acc, crossed = first_products(own, cotangents, arrived)
+    kept, two, six, up, down, half0, half1 = second_products(acc, crossed, swapped)
     up, down = shift(up, "z", NZ, 1), shift(down, "z", NZ, 7)
     ahead, back = merge(two, six, up, down, shift(half0, "z", NZ, 2), shift(half1, "z", NZ, 6))
+    kept, root_strips = lax.optimization_barrier((kept, root_strips))
     total = kept + up[0].astype(F32) + down[0].astype(F32)
     total = total + shift(ahead, "z", NZ, 2).astype(F32) + shift(back, "z", NZ, 6).astype(F32)
     grad = total.astype(BF)

time: 125 us -> 121 us (0.968)
  waiting for transfers between devices: 29.7 us -> 24.3 us
  Pallas kernels: 22.3 us -> 20.4 us
    all_to_all x1, waiting for transfers between devices: 6.2 us -> 0.01 us  [local(): lax.all_to_all(jnp.broadcast_to(strips[None], (8, 2, 10, 16, 128)), 'z',...]
    pallas_call x1, Pallas kernels: 2.25 us -> 0.13 us  [keep_own(): pl.pallas_call(own_kernel, out_shape=struct((256, 2048), BF), in_specs=[H...]
    pallas_call x1 -> x2, Pallas kernels: 4.3 us -> 3.86 us  [the longest x1 2.58 us: first_products(): pl.pallas_call(first_kernel, out_shape=[struct((256, 2048), F32), struct(...]
  transfers between devices with their start and end apart: 27 -> 27, of which waited for: 10 -> 12; matrix products, arithmetic and copies ran while one was open for 1% -> 1% of each run, Pallas kernels for 10% -> 12%
where the time goes in v4:
time: 121 us
  starting transfers between devices  56.4 us (47%)
  waiting for transfers between devices  24.3 us (20%)
  Pallas kernels  20.4 us (17%)
  blocking collectives  14.6 us (12%)
  local copies, waits for them, and re-layouts  3.18 us (3%)
    ppermute x26, starting transfers between devices, shift(): lax.ppermute(x, axis, [(i, (i + offset) % size) for i in range(size)])  48.2 us
    ppermute x26, waiting for transfers between devices, shift(): lax.ppermute(x, axis, [(i, (i + offset) % size) for i in range(size)])  24.3 us
    all_to_all x1, blocking collectives, local(): lax.all_to_all(jnp.broadcast_to(strip[None], (8, 10, 16, 128)), 'z', 0, 0...  14.6 us
    all_to_all x1, starting transfers between devices, local(): lax.all_to_all(jnp.broadcast_to(strips[None], (8, 2, 10, 16, 128)), 'z',...  8.19 us
    pallas_call x1, Pallas kernels, make_roots(): pl.pallas_call(root_kernel, grid=(2,), out_shape=[struct((2, 512, 512), F...  7.39 us
    pallas_call x1, Pallas kernels, pack(): pl.pallas_call(pack_kernel, out_shape=[struct((128, 2560), BF)] * 3, in_s...  3.18 us
    pallas_call x1, Pallas kernels, first_products(): pl.pallas_call(first_kernel, out_shape=[struct((256, 2048), F32), struct(...  2.58 us
  transfers between devices with their start and end apart: 27, of which 12 were waited for; matrix products, arithmetic and copies ran while one was open for 1% of the time, Pallas kernels for 12%

profile of v4, /device:TPU:1, one launch (start us, length us, event | category | flops | bytes accessed | tf_op | source)
XLA Modules:
  0.0 120.9 jit_solution(18047487987112085082)
XLA Ops:
  0.6 0.0 copy-start.4
  0.7 3.2 %pack.1 = (bf16[128,2560]{1,0:T(8,128)(2,1)}, bf16[128,2560]{1,0:T(8,128)(2,1)}, bf16[128,2560]{1,0:T(8,128)(2,1)}) custom-call(bf16[256,8192]{1,0:T(8,128)(2,1)} %act.2, bf16[2,256,128]{2,1,0:T(8,128)(2,1)} %cot.3), custom_call_target="tpu_custom_call" | custom-call | tf_op jit(solution)/shard_map/pack/pallas_call | solution.py:67
  3.8 2.2 %collective-permute-start = (bf16[128,2560]{1,0:T(8,128)(2,1)}, bf16[128,2560]{1,0:T(8,128)(2,1)S(1)}, u32[]{:S(2)}, u32[]{:S(2)}) collective-permute-start(bf16[128,2560]{1,0:T(8,128)(2,1)} %get-tuple-element.39), channel_id=1, source_target_pairs={{0,8},{8,16},{16,24},{24,0},{1,9},{9,17},{17,25},{25,1},{2,10},{10... | collective-permute-start | bytes 1966088 | tf_op jit(solution)/shard_map/ppermute | solution.py:28
  6.0 2.6 %collective-permute-start.1 = (bf16[128,2560]{1,0:T(8,128)(2,1)}, bf16[128,2560]{1,0:T(8,128)(2,1)}, u32[]{:S(2)}, u32[]{:S(2)}) collective-permute-start(bf16[128,2560]{1,0:T(8,128)(2,1)} %get-tuple-element.40), channel_id=1, source_target_pairs={{0,16},{8,24},{16,0},{24,8},{1,17},{9,25},{17,1},{25,9},{2,18},{10... | collective-permute-start | bytes 1966088 | tf_op jit(solution)/shard_map/ppermute | solution.py:28
  8.7 1.1 collective-permute-start.2
  9.7 7.4 %roots.1 = (f32[2,512,512]{2,1,0:T(8,128)}, bf16[2,10,16,128]{3,2,1,0:T(8,128)(2,1)S(1)}, f32[2,8,128]{2,1,0:T(8,128)S(1)}) custom-call(s32[32]{0:T(128)S(1)} %copy-done.4, f32[2,512,512]{2,1,0:T(8,128)S(1)} %bitcast.16), custom_call_target="tpu_custom_call" | custom-call | flops 3758096384 | bytes 4194304 | tf_op jit(solution)/shard_map/roots/pallas_call | solution.py:263
  17.1 0.9 broadcast_in_dim.10
  18.1 8.2 %all-to-all-start = ((bf16[8,2,10,16,128]{4,3,2,1,0:T(8,128)(2,1)}), bf16[8,2,10,16,128]{4,3,2,1,0:T(8,128)(2,1)S(1)}, u32[]{:S(2)}, u32[]{:S(2)}) async-start(bf16[8,2,10,16,128]{4,3,2,1,0:T(8,128)(2,1)} %broadcast_in_dim.10), calls=%async_computation | async-start | bytes 1310720 | tf_op jit(solution)/shard_map/all_to_all | solution.py:380
  26.3 2.3 %plan.1 = s32[16]{0:T(128)} custom-call(s32[32]{0:T(128)} %worker_of.3), custom_call_target="tpu_custom_call" | custom-call | tf_op jit(solution)/shard_map/plan/pallas_call | solution.py:221
  28.5 0.0 copy-start
  28.5 2.2 %copy-done = bf16[256,8192]{1,0:T(8,128)(2,1)S(1)} copy-done((bf16[256,8192]{1,0:T(8,128)(2,1)S(1)}, bf16[256,8192]{1,0:T(8,128)(2,1)}, u32[]{:S(2)}) %copy-start) | copy-done | bytes 4194328
  30.7 0.1 own.1
  30.9 0.0 collective-permute-done.refs_0_
  30.9 6.3 %collective-permute-done.1.refs_1_ = bf16[128,2560]{1,0:T(8,128)(2,1)} collective-permute-done((bf16[128,2560]{1,0:T(8,128)(2,1)}, bf16[128,2560]{1,0:T(8,128)(2,1)}, u32[]{:S(2)}, u32[]{:S(2)}) %collective-permute-start.1) | collective-permute-done | bytes 655392 | tf_op jit(solution)/shard_map/ppermute | solution.py:28
  37.2 0.0 collective-permute-done.2.refs_2_
  37.2 1.5 %collective-permute-start.3 = (bf16[128,2560]{1,0:T(8,128)(2,1)S(1)}, bf16[128,2560]{1,0:T(8,128)(2,1)S(1)}, u32[]{:S(2)}, u32[]{:S(2)}) collective-permute-start(bf16[128,2560]{1,0:T(8,128)(2,1)S(1)} %collective-permute-done.refs_0_), channel_id=1, source_target_pairs={{0,1},{1,0},{2,3},{3,2},{4,5},{5,4},{6,7},{7,6},{8,9},{9,8},{10,11... | collective-permute-start | bytes 1966088 | tf_op jit(solution)/shard_map/ppermute | solution.py:28
  38.7 0.0 collective-permute-start.4
  38.7 0.5 collective-permute-start.5
  39.2 2.6 %first.1 = (f32[256,2048]{1,0:T(8,128)S(1)}, bf16[256,384]{1,0:T(8,128)(2,1)S(1)}) custom-call(bf16[256,2048]{1,0:T(8,128)(2,1)S(1)} %own.1, bf16[2,256,128]{2,1,0:T(8,128)(2,1)S(1)} %copy-done.2, bf16[128,2560]{1,0:T(8,128)(2,1)S(1)} %collective-permute-done.refs_0_, bf16[128,2560]{1,0:T(8,128)(2,1)} %collective-permute-done.1.refs_1_, ...), custom_call_target="tpu_custom_call" | custom-call | flops 536870912 | bytes 4194304 | tf_op jit(solution)/shard_map/first/pallas_call | solution.py:121
  41.8 0.0 collective-permute-done.3.refs_0_
  41.8 0.0 collective-permute-done.4.refs_1_
  41.8 0.7 collective-permute-done.5.refs_2_
  42.5 1.3 %second.1 = (f32[128,512]{1,0:T(8,128)S(1)}, f32[128,512]{1,0:T(8,128)S(1)}, f32[128,512]{1,0:T(8,128)S(1)}, bf16[2,128,512]{2,1,0:T(8,128)(2,1)S(1)}, bf16[2,12...) custom-call(f32[256,2048]{1,0:T(8,128)S(1)} %get-tuple-element.50.acc, ...), custom_call_target="tpu_custom_call" | custom-call | flops 536870912 | bytes 4194304 | tf_op jit(solution)/shard_map/second/pallas_call | solution.py:162
  43.8 1.7 %collective-permute-start.6 = (bf16[2,128,512]{2,1,0:T(8,128)(2,1)S(1)}, bf16[2,128,512]{2,1,0:T(8,128)(2,1)S(1)}, u32[]{:S(2)}, u32[]{:S(2)}) collective-permute-start(bf16[2,128,512]{2,1,0:T(8,128)(2,1)S(1)} %get-tuple-element.54), channel_id=1, source_target_pairs={{0,32},{32,64},{64,96},{96,128},{128,160},{160,192},{192,224},{224... | collective-permute-start | bytes 786440 | tf_op jit(solution)/shard_map/ppermute | solution.py:28
  45.5 4.0 %collective-permute-start.7 = (bf16[2,128,512]{2,1,0:T(8,128)(2,1)S(1)}, bf16[2,128,512]{2,1,0:T(8,128)(2,1)S(1)}, u32[]{:S(2)}, u32[]{:S(2)}) collective-permute-start(bf16[2,128,512]{2,1,0:T(8,128)(2,1)S(1)} %get-tuple-element.55), channel_id=1, source_target_pairs={{0,224},{32,0},{64,32},{96,64},{128,96},{160,128},{192,160},{224,1... | collective-permute-start | bytes 786440 | tf_op jit(solution)/shard_map/ppermute | solution.py:28
  49.6 0.0 collective-permute-start.8
  49.6 3.6 %collective-permute-start.9 = (bf16[64,512]{1,0:T(8,128)(2,1)S(1)}, bf16[64,512]{1,0:T(8,128)(2,1)S(1)}, u32[]{:S(2)}, u32[]{:S(2)}) collective-permute-start(bf16[64,512]{1,0:T(8,128)(2,1)S(1)} %get-tuple-element.59), channel_id=1, source_target_pairs={{0,192},{32,224},{64,0},{96,32},{128,64},{160,96},{192,128},{224,1... | collective-permute-start | bytes 196616 | tf_op jit(solution)/shard_map/ppermute | solution.py:28
  53.1 5.2 %collective-permute-done.8.low = bf16[64,512]{1,0:T(8,128)(2,1)S(1)} collective-permute-done((bf16[64,512]{1,0:T(8,128)(2,1)S(1)}, bf16[64,512]{1,0:T(8,128)(2,1)S(1)}, u32[]{:S(2)}, u32[]{:S(2)}) %collective-permute-start.8) | collective-permute-done | bytes 65568 | tf_op jit(solution)/shard_map/ppermute | solution.py:28
  58.3 0.0 collective-permute-done.9.high
  58.3 0.0 collective-permute-done.6.up
  58.3 0.0 collective-permute-done.7.down
  58.3 0.7 merge.1
  59.1 3.7 %collective-permute-start.10 = (bf16[128,512]{1,0:T(8,128)(2,1)}, bf16[128,512]{1,0:T(8,128)(2,1)}, u32[]{:S(2)}, u32[]{:S(2)}) collective-permute-start(bf16[128,512]{1,0:T(8,128)(2,1)} %get-tuple-element.60), channel_id=1, source_target_pairs={{0,64},{32,96},{64,128},{96,160},{128,192},{160,224},{192,0},{224,... | collective-permute-start | bytes 393224 | tf_op jit(solution)/shard_map/ppermute | solution.py:28
  62.8 0.0 collective-permute-start.11
  62.8 0.0 all-to-all-done
  62.8 5.7 %collective-permute-done.10 = bf16[128,512]{1,0:T(8,128)(2,1)} collective-permute-done((bf16[128,512]{1,0:T(8,128)(2,1)}, bf16[128,512]{1,0:T(8,128)(2,1)}, u32[]{:S(2)}, u32[]{:S(2)}) %collective-permute-start.10) | collective-permute-done | bytes 131104 | tf_op jit(solution)/shard_map/ppermute | solution.py:28
  68.5 1.1 fusion.2.mine.grad
  69.6 3.7 %collective-permute-start.12 = (bf16[128,512]{1,0:T(8,128)(2,1)S(1)}, bf16[128,512]{1,0:T(8,128)(2,1)S(1)}, u32[]{:S(2)}, u32[]{:S(2)}) collective-permute-start(bf16[128,512]{1,0:T(8,128)(2,1)S(1)} %fusion.2.mine.grad), channel_id=1, source_target_pairs={{0,1},{1,0},{2,3},{3,2},{4,5},{5,4},{6,7},{7,6},{8,9},{9,8},{10,11... | collective-permute-start | bytes 393224 | tf_op jit(solution)/shard_map/ppermute | solution.py:28
  73.3 1.0 collective-permute-done.12.theirs
  74.3 0.4 grams.1
  74.7 1.3 %collective-permute-start.13 = (bf16[10,16,128]{2,1,0:T(8,128)(2,1)S(1)}, bf16[10,16,128]{2,1,0:T(8,128)(2,1)S(1)}, u32[]{:S(2)}, u32[]{:S(2)}) collective-permute-start(bf16[10,16,128]{2,1,0:T(8,128)(2,1)S(1)} %get-tuple-element.65), channel_id=1, source_target_pairs={{0,2},{2,4},{4,6},{6,0},{1,3},{3,5},{5,7},{7,1},{8,10},{10,12},{12... | collective-permute-start | bytes 122888 | tf_op jit(solution)/shard_map/ppermute | solution.py:28
  76.0 2.4 %collective-permute-start.14 = (bf16[10,16,128]{2,1,0:T(8,128)(2,1)S(1)}, bf16[10,16,128]{2,1,0:T(8,128)(2,1)S(1)}, u32[]{:S(2)}, u32[]{:S(2)}) collective-permute-start(bf16[10,16,128]{2,1,0:T(8,128)(2,1)S(1)} %get-tuple-element.66), channel_id=1, source_target_pairs={{0,4},{2,6},{4,0},{6,2},{1,5},{3,7},{5,1},{7,3},{8,12},{10,14},{12... | collective-permute-start | bytes 122888 | tf_op jit(solution)/shard_map/ppermute | solution.py:28
  78.4 1.2 collective-permute-start.15
  79.6 0.9 collective-permute-done.14
  80.5 1.1 collective-permute-done.15
  81.7 14.6 %all_to_all.10.column = bf16[8,10,16,128]{3,2,1,0:T(8,128)(2,1)S(1)} all-to-all(bf16[8,10,16,128]{3,2,1,0:T(8,128)(2,1)S(1)} %broadcast_in_dim.22), channel_id=1, replica_groups=mesh['z'=8,'y'=4,'x'=4,'c'=2] {'z'}, dimensions={0} | all-to-all | bytes 655360 | tf_op jit(solution)/shard_map/all_to_all | solution.py:399
  96.3 0.7 choose.1
  97.0 1.1 collective-permute-start.16
  98.0 2.1 %collective-permute-start.17 = (bf16[3,10,16,128]{3,2,1,0:T(8,128)(2,1)S(1)}, bf16[3,10,16,128]{3,2,1,0:T(8,128)(2,1)S(1)}, u32[]{:S(2)}, u32[]{:S(2)}) collective-permute-start(bf16[3,10,16,128]{3,2,1,0:T(8,128)(2,1)S(1)} %get-tuple-element.70), channel_id=1, source_target_pairs={{0,16},{8,24},{16,0},{24,8},{1,17},{9,25},{17,1},{25,9},{2,18},{10... | collective-permute-start | bytes 368648 | tf_op jit(solution)/shard_map/ppermute | solution.py:28
  100.1 1.3 %collective-permute-start.18 = (bf16[3,10,16,128]{3,2,1,0:T(8,128)(2,1)S(1)}, bf16[3,10,16,128]{3,2,1,0:T(8,128)(2,1)S(1)}, u32[]{:S(2)}, u32[]{:S(2)}) collective-permute-start(bf16[3,10,16,128]{3,2,1,0:T(8,128)(2,1)S(1)} %get-tuple-element.71), channel_id=1, source_target_pairs={{0,24},{8,0},{16,8},{24,16},{1,25},{9,1},{17,9},{25,17},{2,26},{10... | collective-permute-start | bytes 368648 | tf_op jit(solution)/shard_map/ppermute | solution.py:28
  101.4 0.6 collective-permute-done.16
  102.0 1.7 %collective-permute-done.17 = bf16[3,10,16,128]{3,2,1,0:T(8,128)(2,1)S(1)} collective-permute-done((bf16[3,10,16,128]{3,2,1,0:T(8,128)(2,1)S(1)}, bf16[3,10,16,128]{3,2,1,0:T(8,128)(2,1)S(1)}, u32[]{:S(2)}, u32[]{:S(2)}) %collective-permute-start.17) | collective-permute-done | bytes 122912 | tf_op jit(solution)/shard_map/ppermute | solution.py:28
  103.7 0.2 collective-permute-done.18
  103.9 0.1 collective-permute-start.19
  104.0 2.6 %collective-permute-start.20 = (bf16[3,10,16,128]{3,2,1,0:T(8,128)(2,1)S(1)}, bf16[3,10,16,128]{3,2,1,0:T(8,128)(2,1)S(1)}, u32[]{:S(2)}, u32[]{:S(2)}) collective-permute-start(bf16[3,10,16,128]{3,2,1,0:T(8,128)(2,1)S(1)} %add_add_fusion.refs_0_), channel_id=1, source_target_pairs={{0,4},{2,6},{4,0},{6,2},{1,5},{3,7},{5,1},{7,3},{8,12},{10,14},{12... | collective-permute-start | bytes 368648 | tf_op jit(solution)/shard_map/ppermute | solution.py:28
  106.6 0.5 collective-permute-start.21
  107.1 6.4 %collective-permute-start.22 = (bf16[3,10,16,128]{3,2,1,0:T(8,128)(2,1)S(1)}, bf16[3,10,16,128]{3,2,1,0:T(8,128)(2,1)S(1)}, u32[]{:S(2)}, u32[]{:S(2)}) collective-permute-start(bf16[3,10,16,128]{3,2,1,0:T(8,128)(2,1)S(1)} %add_add_fusion.refs_0_), channel_id=1, source_target_pairs={{0,1},{1,0},{2,3},{3,2},{4,5},{5,4},{6,7},{7,6},{8,9},{9,8},{10,11... | collective-permute-start | bytes 368648 | tf_op jit(solution)/shard_map/ppermute | solution.py:28
  113.5 2.0 %collective-permute-start.23 = (bf16[3,10,16,128]{3,2,1,0:T(8,128)(2,1)S(1)}, bf16[3,10,16,128]{3,2,1,0:T(8,128)(2,1)S(1)}, u32[]{:S(2)}, u32[]{:S(2)}) collective-permute-start(bf16[3,10,16,128]{3,2,1,0:T(8,128)(2,1)S(1)} %collective-permute-done.19.refs_1_), channel_id=1, source_target_pairs={{0,1},{1,0},{2,3},{3,2},{4,5},{5,4},{6,7},{7,6},{8,9},{9,8},{10,11... | collective-permute-start | bytes 368648 | tf_op jit(solution)/shard_map/ppermute | solution.py:28
  115.5 1.9 %collective-permute-start.24 = (bf16[3,10,16,128]{3,2,1,0:T(8,128)(2,1)S(1)}, bf16[3,10,16,128]{3,2,1,0:T(8,128)(2,1)S(1)}, u32[]{:S(2)}, u32[]{:S(2)}) collective-permute-start(bf16[3,10,16,128]{3,2,1,0:T(8,128)(2,1)S(1)} %collective-permute-done.20.refs_2_), channel_id=1, source_target_pairs={{0,1},{1,0},{2,3},{3,2},{4,5},{5,4},{6,7},{7,6},{8,9},{9,8},{10,11... | collective-permute-start | bytes 368648 | tf_op jit(solution)/shard_map/ppermute | solution.py:28
  117.4 0.7 collective-permute-start.25
  118.1 0.0 collective-permute-done.23.refs_5_
  118.1 0.3 collective-permute-done.24.refs_6_
  118.3 0.7 collective-permute-done.25.refs_7_
  119.1 1.8 %finish.1 = (f32[2,512,512]{2,1,0:T(8,128)}, bf16[512,128]{1,0:T(8,128)(2,1)}) custom-call(f32[2,512,512]{2,1,0:T(8,128)S(1)} %bitcast.17, f32[2,8,128]{2,1,0:T(8,128)S(1)} %get-tuple-element.43.occupied, bf16[128,512]{1,0:T(8,128)(2,1)S(1)} %fusion.2.mine.grad, bf16[3,10,16,128]{3,2,1,0:T(8,128)(2,1)S(1)} %add_add_fusion.refs_0_, ...), custom_call_target="tpu_custom_call" | custom-call | tf_op jit(solution)/shard_map/finish/pallas_call | solution.py:359
  (16 shorter events, 0.1 us)
Async XLA Ops:
  0.6 9.1 %copy-start.1 = (f32[1,2,512,512]{3,2,1,0:T(8,128)S(1)}, f32[1,2,512,512]{3,2,1,0:T(8,128)}, u32[]{:S(2)}) copy-start(f32[1,2,512,512]{3,2,1,0:T(8,128)} %param.7) | copy-start | bytes 6291460
  0.6 9.1 %copy-start.4 = (s32[32]{0:T(128)S(1)}, s32[32]{0:T(128)}, u32[]{:S(2)}) copy-start(s32[32]{0:T(128)} %worker_of.3) | copy-start | bytes 388
  3.8 27.0 %collective-permute-start = (bf16[128,2560]{1,0:T(8,128)(2,1)}, bf16[128,2560]{1,0:T(8,128)(2,1)S(1)}, u32[]{:S(2)}, u32[]{:S(2)}) collective-permute-start(bf16[128,2560]{1,0:T(8,128)(2,1)} %get-tuple-element.39), channel_id=1, source_target_pairs={{0,8},{8,16},{16,24},{24,0},{1,9},{9,17},{17,25},{25,1},{2,10},{10... | collective-permute-start | bytes 1966088 | tf_op jit(solution)/shard_map/ppermute | solution.py:28
  6.0 31.1 %collective-permute-start.1 = (bf16[128,2560]{1,0:T(8,128)(2,1)}, bf16[128,2560]{1,0:T(8,128)(2,1)}, u32[]{:S(2)}, u32[]{:S(2)}) collective-permute-start(bf16[128,2560]{1,0:T(8,128)(2,1)} %get-tuple-element.40), channel_id=1, source_target_pairs={{0,16},{8,24},{16,0},{24,8},{1,17},{9,25},{17,1},{25,9},{2,18},{10... | collective-permute-start | bytes 1966088 | tf_op jit(solution)/shard_map/ppermute | solution.py:28
  8.7 28.5 %collective-permute-start.2 = (bf16[128,2560]{1,0:T(8,128)(2,1)}, bf16[128,2560]{1,0:T(8,128)(2,1)}, u32[]{:S(2)}, u32[]{:S(2)}) collective-permute-start(bf16[128,2560]{1,0:T(8,128)(2,1)} %get-tuple-element.41), channel_id=1, source_target_pairs={{0,24},{8,0},{16,8},{24,16},{1,25},{9,1},{17,9},{25,17},{2,26},{10... | collective-permute-start | bytes 1966088 | tf_op jit(solution)/shard_map/ppermute | solution.py:28
  18.1 44.7 %all-to-all-start = ((bf16[8,2,10,16,128]{4,3,2,1,0:T(8,128)(2,1)}), bf16[8,2,10,16,128]{4,3,2,1,0:T(8,128)(2,1)S(1)}, u32[]{:S(2)}, u32[]{:S(2)}) async-start(bf16[8,2,10,16,128]{4,3,2,1,0:T(8,128)(2,1)} %broadcast_in_dim.10), calls=%async_computation | async-start | bytes 1310720 | tf_op jit(solution)/shard_map/all_to_all | solution.py:380
  28.5 2.2 %copy-start = (bf16[256,8192]{1,0:T(8,128)(2,1)S(1)}, bf16[256,8192]{1,0:T(8,128)(2,1)}, u32[]{:S(2)}) copy-start(bf16[256,8192]{1,0:T(8,128)(2,1)} %act.2) | copy-start | bytes 12582916
  30.7 8.5 %copy-start.2 = (bf16[2,256,128]{2,1,0:T(8,128)(2,1)S(1)}, bf16[2,256,128]{2,1,0:T(8,128)(2,1)}, u32[]{:S(2)}) copy-start(bf16[2,256,128]{2,1,0:T(8,128)(2,1)} %cot.3) | copy-start | bytes 393220
  37.2 4.6 %collective-permute-start.3 = (bf16[128,2560]{1,0:T(8,128)(2,1)S(1)}, bf16[128,2560]{1,0:T(8,128)(2,1)S(1)}, u32[]{:S(2)}, u32[]{:S(2)}) collective-permute-start(bf16[128,2560]{1,0:T(8,128)(2,1)S(1)} %collective-permute-done.refs_0_), channel_id=1, source_target_pairs={{0,1},{1,0},{2,3},{3,2},{4,5},{5,4},{6,7},{7,6},{8,9},{9,8},{10,11... | collective-permute-start | bytes 1966088 | tf_op jit(solution)/shard_map/ppermute | solution.py:28
  38.7 3.1 %collective-permute-start.4 = (bf16[128,2560]{1,0:T(8,128)(2,1)}, bf16[128,2560]{1,0:T(8,128)(2,1)S(1)}, u32[]{:S(2)}, u32[]{:S(2)}) collective-permute-start(bf16[128,2560]{1,0:T(8,128)(2,1)} %collective-permute-done.1.refs_1_), channel_id=1, source_target_pairs={{0,1},{1,0},{2,3},{3,2},{4,5},{5,4},{6,7},{7,6},{8,9},{9,8},{10,11... | collective-permute-start | bytes 1966088 | tf_op jit(solution)/shard_map/ppermute | solution.py:28
  38.7 3.8 %collective-permute-start.5 = (bf16[128,2560]{1,0:T(8,128)(2,1)}, bf16[128,2560]{1,0:T(8,128)(2,1)S(1)}, u32[]{:S(2)}, u32[]{:S(2)}) collective-permute-start(bf16[128,2560]{1,0:T(8,128)(2,1)} %collective-permute-done.2.refs_2_), channel_id=1, source_target_pairs={{0,1},{1,0},{2,3},{3,2},{4,5},{5,4},{6,7},{7,6},{8,9},{9,8},{10,11... | collective-permute-start | bytes 1966088 | tf_op jit(solution)/shard_map/ppermute | solution.py:28
  43.8 52.5 %copy-start.3 = (s32[16]{0:T(128)S(1)}, s32[16]{0:T(128)}, u32[]{:S(2)}) copy-start(s32[16]{0:T(128)} %plan.1) | copy-start | bytes 196
  43.8 14.5 %collective-permute-start.6 = (bf16[2,128,512]{2,1,0:T(8,128)(2,1)S(1)}, bf16[2,128,512]{2,1,0:T(8,128)(2,1)S(1)}, u32[]{:S(2)}, u32[]{:S(2)}) collective-permute-start(bf16[2,128,512]{2,1,0:T(8,128)(2,1)S(1)} %get-tuple-element.54), channel_id=1, source_target_pairs={{0,32},{32,64},{64,96},{96,128},{128,160},{160,192},{192,224},{224... | collective-permute-start | bytes 786440 | tf_op jit(solution)/shard_map/ppermute | solution.py:28
  45.5 12.8 %collective-permute-start.7 = (bf16[2,128,512]{2,1,0:T(8,128)(2,1)S(1)}, bf16[2,128,512]{2,1,0:T(8,128)(2,1)S(1)}, u32[]{:S(2)}, u32[]{:S(2)}) collective-permute-start(bf16[2,128,512]{2,1,0:T(8,128)(2,1)S(1)} %get-tuple-element.55), channel_id=1, source_target_pairs={{0,224},{32,0},{64,32},{96,64},{128,96},{160,128},{192,160},{224,1... | collective-permute-start | bytes 786440 | tf_op jit(solution)/shard_map/ppermute | solution.py:28
  49.6 8.7 %collective-permute-start.8 = (bf16[64,512]{1,0:T(8,128)(2,1)S(1)}, bf16[64,512]{1,0:T(8,128)(2,1)S(1)}, u32[]{:S(2)}, u32[]{:S(2)}) collective-permute-start(bf16[64,512]{1,0:T(8,128)(2,1)S(1)} %get-tuple-element.58), channel_id=1, source_target_pairs={{0,64},{32,96},{64,128},{96,160},{128,192},{160,224},{192,0},{224,... | collective-permute-start | bytes 196616 | tf_op jit(solution)/shard_map/ppermute | solution.py:28
  49.6 8.7 %collective-permute-start.9 = (bf16[64,512]{1,0:T(8,128)(2,1)S(1)}, bf16[64,512]{1,0:T(8,128)(2,1)S(1)}, u32[]{:S(2)}, u32[]{:S(2)}) collective-permute-start(bf16[64,512]{1,0:T(8,128)(2,1)S(1)} %get-tuple-element.59), channel_id=1, source_target_pairs={{0,192},{32,224},{64,0},{96,32},{128,64},{160,96},{192,128},{224,1... | collective-permute-start | bytes 196616 | tf_op jit(solution)/shard_map/ppermute | solution.py:28
  59.1 9.4 %collective-permute-start.10 = (bf16[128,512]{1,0:T(8,128)(2,1)}, bf16[128,512]{1,0:T(8,128)(2,1)}, u32[]{:S(2)}, u32[]{:S(2)}) collective-permute-start(bf16[128,512]{1,0:T(8,128)(2,1)} %get-tuple-element.60), channel_id=1, source_target_pairs={{0,64},{32,96},{64,128},{96,160},{128,192},{160,224},{192,0},{224,... | collective-permute-start | bytes 393224 | tf_op jit(solution)/shard_map/ppermute | solution.py:28
  62.8 5.8 %collective-permute-start.11 = (bf16[128,512]{1,0:T(8,128)(2,1)}, bf16[128,512]{1,0:T(8,128)(2,1)}, u32[]{:S(2)}, u32[]{:S(2)}) collective-permute-start(bf16[128,512]{1,0:T(8,128)(2,1)} %get-tuple-element.61), channel_id=1, source_target_pairs={{0,192},{32,224},{64,0},{96,32},{128,64},{160,96},{192,128},{224,1... | collective-permute-start | bytes 393224 | tf_op jit(solution)/shard_map/ppermute | solution.py:28
  69.6 4.7 %collective-permute-start.12 = (bf16[128,512]{1,0:T(8,128)(2,1)S(1)}, bf16[128,512]{1,0:T(8,128)(2,1)S(1)}, u32[]{:S(2)}, u32[]{:S(2)}) collective-permute-start(bf16[128,512]{1,0:T(8,128)(2,1)S(1)} %fusion.2.mine.grad), channel_id=1, source_target_pairs={{0,1},{1,0},{2,3},{3,2},{4,5},{5,4},{6,7},{7,6},{8,9},{9,8},{10,11... | collective-permute-start | bytes 393224 | tf_op jit(solution)/shard_map/ppermute | solution.py:28
  74.7 4.9 %collective-permute-start.13 = (bf16[10,16,128]{2,1,0:T(8,128)(2,1)S(1)}, bf16[10,16,128]{2,1,0:T(8,128)(2,1)S(1)}, u32[]{:S(2)}, u32[]{:S(2)}) collective-permute-start(bf16[10,16,128]{2,1,0:T(8,128)(2,1)S(1)} %get-tuple-element.65), channel_id=1, source_target_pairs={{0,2},{2,4},{4,6},{6,0},{1,3},{3,5},{5,7},{7,1},{8,10},{10,12},{12... | collective-permute-start | bytes 122888 | tf_op jit(solution)/shard_map/ppermute | solution.py:28
  76.0 4.5 %collective-permute-start.14 = (bf16[10,16,128]{2,1,0:T(8,128)(2,1)S(1)}, bf16[10,16,128]{2,1,0:T(8,128)(2,1)S(1)}, u32[]{:S(2)}, u32[]{:S(2)}) collective-permute-start(bf16[10,16,128]{2,1,0:T(8,128)(2,1)S(1)} %get-tuple-element.66), channel_id=1, source_target_pairs={{0,4},{2,6},{4,0},{6,2},{1,5},{3,7},{5,1},{7,3},{8,12},{10,14},{12... | collective-permute-start | bytes 122888 | tf_op jit(solution)/shard_map/ppermute | solution.py:28
  78.4 3.1 %collective-permute-start.15 = (bf16[10,16,128]{2,1,0:T(8,128)(2,1)S(1)}, bf16[10,16,128]{2,1,0:T(8,128)(2,1)S(1)}, u32[]{:S(2)}, u32[]{:S(2)}) collective-permute-start(bf16[10,16,128]{2,1,0:T(8,128)(2,1)S(1)} %get-tuple-element.67), channel_id=1, source_target_pairs={{0,6},{2,0},{4,2},{6,4},{1,7},{3,1},{5,3},{7,5},{8,14},{10,8},{12,... | collective-permute-start | bytes 122888 | tf_op jit(solution)/shard_map/ppermute | solution.py:28
  97.0 5.0 %collective-permute-start.16 = (bf16[3,10,16,128]{3,2,1,0:T(8,128)(2,1)S(1)}, bf16[3,10,16,128]{3,2,1,0:T(8,128)(2,1)S(1)}, u32[]{:S(2)}, u32[]{:S(2)}) collective-permute-start(bf16[3,10,16,128]{3,2,1,0:T(8,128)(2,1)S(1)} %get-tuple-element.69), channel_id=1, source_target_pairs={{0,8},{8,16},{16,24},{24,0},{1,9},{9,17},{17,25},{25,1},{2,10},{10... | collective-permute-start | bytes 368648 | tf_op jit(solution)/shard_map/ppermute | solution.py:28
  98.0 5.7 %collective-permute-start.17 = (bf16[3,10,16,128]{3,2,1,0:T(8,128)(2,1)S(1)}, bf16[3,10,16,128]{3,2,1,0:T(8,128)(2,1)S(1)}, u32[]{:S(2)}, u32[]{:S(2)}) collective-permute-start(bf16[3,10,16,128]{3,2,1,0:T(8,128)(2,1)S(1)} %get-tuple-element.70), channel_id=1, source_target_pairs={{0,16},{8,24},{16,0},{24,8},{1,17},{9,25},{17,1},{25,9},{2,18},{10... | collective-permute-start | bytes 368648 | tf_op jit(solution)/shard_map/ppermute | solution.py:28
  100.1 3.8 %collective-permute-start.18 = (bf16[3,10,16,128]{3,2,1,0:T(8,128)(2,1)S(1)}, bf16[3,10,16,128]{3,2,1,0:T(8,128)(2,1)S(1)}, u32[]{:S(2)}, u32[]{:S(2)}) collective-permute-start(bf16[3,10,16,128]{3,2,1,0:T(8,128)(2,1)S(1)} %get-tuple-element.71), channel_id=1, source_target_pairs={{0,24},{8,0},{16,8},{24,16},{1,25},{9,1},{17,9},{25,17},{2,26},{10... | collective-permute-start | bytes 368648 | tf_op jit(solution)/shard_map/ppermute | solution.py:28
  103.9 9.6 %collective-permute-start.19 = (bf16[3,10,16,128]{3,2,1,0:T(8,128)(2,1)S(1)}, bf16[3,10,16,128]{3,2,1,0:T(8,128)(2,1)S(1)}, u32[]{:S(2)}, u32[]{:S(2)}) collective-permute-start(bf16[3,10,16,128]{3,2,1,0:T(8,128)(2,1)S(1)} %add_add_fusion.refs_0_), channel_id=1, source_target_pairs={{0,2},{2,4},{4,6},{6,0},{1,3},{3,5},{5,7},{7,1},{8,10},{10,12},{12... | collective-permute-start | bytes 368648 | tf_op jit(solution)/shard_map/ppermute | solution.py:28
  104.0 11.5 %collective-permute-start.20 = (bf16[3,10,16,128]{3,2,1,0:T(8,128)(2,1)S(1)}, bf16[3,10,16,128]{3,2,1,0:T(8,128)(2,1)S(1)}, u32[]{:S(2)}, u32[]{:S(2)}) collective-permute-start(bf16[3,10,16,128]{3,2,1,0:T(8,128)(2,1)S(1)} %add_add_fusion.refs_0_), channel_id=1, source_target_pairs={{0,4},{2,6},{4,0},{6,2},{1,5},{3,7},{5,1},{7,3},{8,12},{10,14},{12... | collective-permute-start | bytes 368648 | tf_op jit(solution)/shard_map/ppermute | solution.py:28
  106.6 10.8 %collective-permute-start.21 = (bf16[3,10,16,128]{3,2,1,0:T(8,128)(2,1)S(1)}, bf16[3,10,16,128]{3,2,1,0:T(8,128)(2,1)S(1)}, u32[]{:S(2)}, u32[]{:S(2)}) collective-permute-start(bf16[3,10,16,128]{3,2,1,0:T(8,128)(2,1)S(1)} %add_add_fusion.refs_0_), channel_id=1, source_target_pairs={{0,6},{2,0},{4,2},{6,4},{1,7},{3,1},{5,3},{7,5},{8,14},{10,8},{12,... | collective-permute-start | bytes 368648 | tf_op jit(solution)/shard_map/ppermute | solution.py:28
  107.1 11.0 %collective-permute-start.22 = (bf16[3,10,16,128]{3,2,1,0:T(8,128)(2,1)S(1)}, bf16[3,10,16,128]{3,2,1,0:T(8,128)(2,1)S(1)}, u32[]{:S(2)}, u32[]{:S(2)}) collective-permute-start(bf16[3,10,16,128]{3,2,1,0:T(8,128)(2,1)S(1)} %add_add_fusion.refs_0_), channel_id=1, source_target_pairs={{0,1},{1,0},{2,3},{3,2},{4,5},{5,4},{6,7},{7,6},{8,9},{9,8},{10,11... | collective-permute-start | bytes 368648 | tf_op jit(solution)/shard_map/ppermute | solution.py:28
  113.5 4.6 %collective-permute-start.23 = (bf16[3,10,16,128]{3,2,1,0:T(8,128)(2,1)S(1)}, bf16[3,10,16,128]{3,2,1,0:T(8,128)(2,1)S(1)}, u32[]{:S(2)}, u32[]{:S(2)}) collective-permute-start(bf16[3,10,16,128]{3,2,1,0:T(8,128)(2,1)S(1)} %collective-permute-done.19.refs_1_), channel_id=1, source_target_pairs={{0,1},{1,0},{2,3},{3,2},{4,5},{5,4},{6,7},{7,6},{8,9},{9,8},{10,11... | collective-permute-start | bytes 368648 | tf_op jit(solution)/shard_map/ppermute | solution.py:28
  115.5 2.9 %collective-permute-start.24 = (bf16[3,10,16,128]{3,2,1,0:T(8,128)(2,1)S(1)}, bf16[3,10,16,128]{3,2,1,0:T(8,128)(2,1)S(1)}, u32[]{:S(2)}, u32[]{:S(2)}) collective-permute-start(bf16[3,10,16,128]{3,2,1,0:T(8,128)(2,1)S(1)} %collective-permute-done.20.refs_2_), channel_id=1, source_target_pairs={{0,1},{1,0},{2,3},{3,2},{4,5},{5,4},{6,7},{7,6},{8,9},{9,8},{10,11... | collective-permute-start | bytes 368648 | tf_op jit(solution)/shard_map/ppermute | solution.py:28
  117.4 1.7 %collective-permute-start.25 = (bf16[3,10,16,128]{3,2,1,0:T(8,128)(2,1)S(1)}, bf16[3,10,16,128]{3,2,1,0:T(8,128)(2,1)S(1)}, u32[]{:S(2)}, u32[]{:S(2)}) collective-permute-start(bf16[3,10,16,128]{3,2,1,0:T(8,128)(2,1)S(1)} %collective-permute-done.21.refs_3_), channel_id=1, source_target_pairs={{0,1},{1,0},{2,3},{3,2},{4,5},{5,4},{6,7},{7,6},{8,9},{9,8},{10,11... | collective-permute-start | bytes 368648 | tf_op jit(solution)/shard_map/ppermute | solution.py:28

commit v5 on v4

--- a/solution.py
+++ b/solution.py
@@ -380,7 +380,8 @@
     root_strips = lax.all_to_all(jnp.broadcast_to(strips[None], (8, 2, 10, 16, 128)), "z", 0, 0, tiled=True)
     later, _ = lax.optimization_barrier((activations, plan))
     own = keep_own(later)
-    arrived, strips, plan, own = lax.optimization_barrier((arrived, strips, plan, own))
+    last, strips, plan, own = lax.optimization_barrier((arrived[2], strips, plan, own))
+    arrived = arrived[:2] + [last]
     swapped = [shift(p, "c", NC, 1) for p in arrived]
     acc, crossed = first_products(own, cotangents, arrived)
     kept, two, six, up, down, half0, half1 = second_products(acc, crossed, swapped)

time: 121 us -> 122 us (level)
  no operation moved by 1% of the time
where the time goes in v5:
time: 122 us; the launch traced here: 121 us
  starting transfers between devices  57 us (47%)
  waiting for transfers between devices  24.1 us (20%)
  Pallas kernels  20.5 us (17%)
  blocking collectives  14.6 us (12%)
  local copies, waits for them, and re-layouts  3.18 us (3%)
    ppermute x26, starting transfers between devices, shift(): lax.ppermute(x, axis, [(i, (i + offset) % size) for i in range(size)])  48.8 us
    ppermute x26, waiting for transfers between devices, shift(): lax.ppermute(x, axis, [(i, (i + offset) % size) for i in range(size)])  24.1 us
    all_to_all x1, blocking collectives, local(): lax.all_to_all(jnp.broadcast_to(strip[None], (8, 10, 16, 128)), 'z', 0, 0...  14.6 us
    all_to_all x1, starting transfers between devices, local(): lax.all_to_all(jnp.broadcast_to(strips[None], (8, 2, 10, 16, 128)), 'z',...  8.18 us
    pallas_call x1, Pallas kernels, make_roots(): pl.pallas_call(root_kernel, grid=(2,), out_shape=[struct((2, 512, 512), F...  7.4 us
    pallas_call x1, Pallas kernels, pack(): pl.pallas_call(pack_kernel, out_shape=[struct((128, 2560), BF)] * 3, in_s...  3.18 us
    pallas_call x1, Pallas kernels, first_products(): pl.pallas_call(first_kernel, out_shape=[struct((256, 2048), F32), struct(...  2.58 us
  transfers between devices with their start and end apart: 27, of which 12 were waited for; matrix products, arithmetic and copies ran while one was open for 1% of the time, Pallas kernels for 12%

profile of v5, /device:TPU:1, one launch (start us, length us, event | category | flops | bytes accessed | tf_op | source)
XLA Modules:
  0.0 121.2 jit_solution(11195264574371876936)
XLA Ops:
  0.6 0.0 copy-start.4
  0.7 3.2 %pack.1 = (bf16[128,2560]{1,0:T(8,128)(2,1)}, bf16[128,2560]{1,0:T(8,128)(2,1)}, bf16[128,2560]{1,0:T(8,128)(2,1)}) custom-call(bf16[256,8192]{1,0:T(8,128)(2,1)} %act.2, bf16[2,256,128]{2,1,0:T(8,128)(2,1)} %cot.3), custom_call_target="tpu_custom_call" | custom-call | tf_op jit(solution)/shard_map/pack/pallas_call | solution.py:67
  3.8 3.6 %collective-permute-start = (bf16[128,2560]{1,0:T(8,128)(2,1)}, bf16[128,2560]{1,0:T(8,128)(2,1)S(1)}, u32[]{:S(2)}, u32[]{:S(2)}) collective-permute-start(bf16[128,2560]{1,0:T(8,128)(2,1)} %get-tuple-element.39), channel_id=1, source_target_pairs={{0,24},{8,0},{16,8},{24,16},{1,25},{9,1},{17,9},{25,17},{2,26},{10... | collective-permute-start | bytes 1966088 | tf_op jit(solution)/shard_map/ppermute | solution.py:28
  7.5 0.0 collective-permute-start.1
  7.5 1.6 %collective-permute-start.2 = (bf16[128,2560]{1,0:T(8,128)(2,1)}, bf16[128,2560]{1,0:T(8,128)(2,1)}, u32[]{:S(2)}, u32[]{:S(2)}) collective-permute-start(bf16[128,2560]{1,0:T(8,128)(2,1)} %get-tuple-element.38), channel_id=1, source_target_pairs={{0,16},{8,24},{16,0},{24,8},{1,17},{9,25},{17,1},{25,9},{2,18},{10... | collective-permute-start | bytes 1966088 | tf_op jit(solution)/shard_map/ppermute | solution.py:28
  9.1 7.4 %roots.1 = (f32[2,512,512]{2,1,0:T(8,128)}, bf16[2,10,16,128]{3,2,1,0:T(8,128)(2,1)S(1)}, f32[2,8,128]{2,1,0:T(8,128)S(1)}) custom-call(s32[32]{0:T(128)S(1)} %copy-done.4, f32[2,512,512]{2,1,0:T(8,128)S(1)} %bitcast.16), custom_call_target="tpu_custom_call" | custom-call | flops 3758096384 | bytes 4194304 | tf_op jit(solution)/shard_map/roots/pallas_call | solution.py:263
  16.5 0.9 broadcast_in_dim.10
  17.5 8.2 %all-to-all-start = ((bf16[8,2,10,16,128]{4,3,2,1,0:T(8,128)(2,1)}), bf16[8,2,10,16,128]{4,3,2,1,0:T(8,128)(2,1)S(1)}, u32[]{:S(2)}, u32[]{:S(2)}) async-start(bf16[8,2,10,16,128]{4,3,2,1,0:T(8,128)(2,1)} %broadcast_in_dim.10), calls=%async_computation | async-start | bytes 1310720 | tf_op jit(solution)/shard_map/all_to_all | solution.py:380
  25.7 2.3 %plan.1 = s32[16]{0:T(128)} custom-call(s32[32]{0:T(128)} %worker_of.3), custom_call_target="tpu_custom_call" | custom-call | tf_op jit(solution)/shard_map/plan/pallas_call | solution.py:221
  27.9 0.0 copy-start
  27.9 2.2 %copy-done = bf16[256,8192]{1,0:T(8,128)(2,1)S(1)} copy-done((bf16[256,8192]{1,0:T(8,128)(2,1)S(1)}, bf16[256,8192]{1,0:T(8,128)(2,1)}, u32[]{:S(2)}) %copy-start) | copy-done | bytes 4194328
  30.1 0.1 own.1
  30.3 4.8 %collective-permute-done.refs_2_ = bf16[128,2560]{1,0:T(8,128)(2,1)S(1)} collective-permute-done((bf16[128,2560]{1,0:T(8,128)(2,1)}, bf16[128,2560]{1,0:T(8,128)(2,1)S(1)}, u32[]{:S(2)}, u32[]{:S(2)}) %collective-permute-start) | collective-permute-done | bytes 655392 | tf_op jit(solution)/shard_map/ppermute | solution.py:28
  35.1 1.7 %collective-permute-start.5 = (bf16[128,2560]{1,0:T(8,128)(2,1)S(1)}, bf16[128,2560]{1,0:T(8,128)(2,1)S(1)}, u32[]{:S(2)}, u32[]{:S(2)}) collective-permute-start(bf16[128,2560]{1,0:T(8,128)(2,1)S(1)} %collective-permute-done.refs_2_), channel_id=1, source_target_pairs={{0,1},{1,0},{2,3},{3,2},{4,5},{5,4},{6,7},{7,6},{8,9},{9,8},{10,11... | collective-permute-start | bytes 1966088 | tf_op jit(solution)/shard_map/ppermute | solution.py:28
  36.8 0.0 collective-permute-done.1.refs_0_
  36.8 3.4 %collective-permute-start.3 = (bf16[128,2560]{1,0:T(8,128)(2,1)}, bf16[128,2560]{1,0:T(8,128)(2,1)S(1)}, u32[]{:S(2)}, u32[]{:S(2)}) collective-permute-start(bf16[128,2560]{1,0:T(8,128)(2,1)} %collective-permute-done.1.refs_0_), channel_id=1, source_target_pairs={{0,1},{1,0},{2,3},{3,2},{4,5},{5,4},{6,7},{7,6},{8,9},{9,8},{10,11... | collective-permute-start | bytes 1966088 | tf_op jit(solution)/shard_map/ppermute | solution.py:28
  40.2 0.0 collective-permute-done.2.refs_1_
  40.2 0.0 collective-permute-start.4
  40.2 2.6 %first.1 = (f32[256,2048]{1,0:T(8,128)S(1)}, bf16[256,384]{1,0:T(8,128)(2,1)S(1)}) custom-call(bf16[256,2048]{1,0:T(8,128)(2,1)S(1)} %own.1, bf16[2,256,128]{2,1,0:T(8,128)(2,1)S(1)} %copy-done.2, bf16[128,2560]{1,0:T(8,128)(2,1)} %collective-permute-done.1.refs_0_, bf16[128,2560]{1,0:T(8,128)(2,1)} %collective-permute-done.2.refs_1_, ...), custom_call_target="tpu_custom_call" | custom-call | flops 536870912 | bytes 4194304 | tf_op jit(solution)/shard_map/first/pallas_call | solution.py:121
  42.8 0.0 collective-permute-done.5.refs_2_
  42.8 0.3 collective-permute-done.4.refs_1_
  43.1 1.3 %second.1 = (f32[128,512]{1,0:T(8,128)S(1)}, f32[128,512]{1,0:T(8,128)S(1)}, f32[128,512]{1,0:T(8,128)S(1)}, bf16[2,128,512]{2,1,0:T(8,128)(2,1)S(1)}, bf16[2,12...) custom-call(f32[256,2048]{1,0:T(8,128)S(1)} %get-tuple-element.46.acc, ...), custom_call_target="tpu_custom_call" | custom-call | flops 536870912 | bytes 4194304 | tf_op jit(solution)/shard_map/second/pallas_call | solution.py:162
  44.4 1.7 %collective-permute-start.6 = (bf16[2,128,512]{2,1,0:T(8,128)(2,1)S(1)}, bf16[2,128,512]{2,1,0:T(8,128)(2,1)S(1)}, u32[]{:S(2)}, u32[]{:S(2)}) collective-permute-start(bf16[2,128,512]{2,1,0:T(8,128)(2,1)S(1)} %get-tuple-element.50), channel_id=1, source_target_pairs={{0,32},{32,64},{64,96},{96,128},{128,160},{160,192},{192,224},{224... | collective-permute-start | bytes 786440 | tf_op jit(solution)/shard_map/ppermute | solution.py:28
  46.1 4.0 %collective-permute-start.7 = (bf16[2,128,512]{2,1,0:T(8,128)(2,1)S(1)}, bf16[2,128,512]{2,1,0:T(8,128)(2,1)S(1)}, u32[]{:S(2)}, u32[]{:S(2)}) collective-permute-start(bf16[2,128,512]{2,1,0:T(8,128)(2,1)S(1)} %get-tuple-element.51), channel_id=1, source_target_pairs={{0,224},{32,0},{64,32},{96,64},{128,96},{160,128},{192,160},{224,1... | collective-permute-start | bytes 786440 | tf_op jit(solution)/shard_map/ppermute | solution.py:28
  50.1 0.0 collective-permute-start.8
  50.1 3.6 %collective-permute-start.9 = (bf16[64,512]{1,0:T(8,128)(2,1)S(1)}, bf16[64,512]{1,0:T(8,128)(2,1)S(1)}, u32[]{:S(2)}, u32[]{:S(2)}) collective-permute-start(bf16[64,512]{1,0:T(8,128)(2,1)S(1)} %get-tuple-element.55), channel_id=1, source_target_pairs={{0,192},{32,224},{64,0},{96,32},{128,64},{160,96},{192,128},{224,1... | collective-permute-start | bytes 196616 | tf_op jit(solution)/shard_map/ppermute | solution.py:28
  53.7 5.1 %collective-permute-done.8.low = bf16[64,512]{1,0:T(8,128)(2,1)S(1)} collective-permute-done((bf16[64,512]{1,0:T(8,128)(2,1)S(1)}, bf16[64,512]{1,0:T(8,128)(2,1)S(1)}, u32[]{:S(2)}, u32[]{:S(2)}) %collective-permute-start.8) | collective-permute-done | bytes 65568 | tf_op jit(solution)/shard_map/ppermute | solution.py:28
  58.8 0.0 collective-permute-done.9.high
  58.8 0.0 collective-permute-done.6.up
  58.8 0.0 collective-permute-done.7.down
  58.8 0.7 merge.1
  59.6 3.7 %collective-permute-start.10 = (bf16[128,512]{1,0:T(8,128)(2,1)}, bf16[128,512]{1,0:T(8,128)(2,1)}, u32[]{:S(2)}, u32[]{:S(2)}) collective-permute-start(bf16[128,512]{1,0:T(8,128)(2,1)} %get-tuple-element.56), channel_id=1, source_target_pairs={{0,64},{32,96},{64,128},{96,160},{128,192},{160,224},{192,0},{224,... | collective-permute-start | bytes 393224 | tf_op jit(solution)/shard_map/ppermute | solution.py:28
  63.3 0.0 collective-permute-start.11
  63.3 5.4 %collective-permute-done.10 = bf16[128,512]{1,0:T(8,128)(2,1)} collective-permute-done((bf16[128,512]{1,0:T(8,128)(2,1)}, bf16[128,512]{1,0:T(8,128)(2,1)}, u32[]{:S(2)}, u32[]{:S(2)}) %collective-permute-start.10) | collective-permute-done | bytes 131104 | tf_op jit(solution)/shard_map/ppermute | solution.py:28
  68.8 0.2 collective-permute-done.11
  69.0 1.1 fusion.2.mine.grad
  70.0 3.8 %collective-permute-start.12 = (bf16[128,512]{1,0:T(8,128)(2,1)S(1)}, bf16[128,512]{1,0:T(8,128)(2,1)S(1)}, u32[]{:S(2)}, u32[]{:S(2)}) collective-permute-start(bf16[128,512]{1,0:T(8,128)(2,1)S(1)} %fusion.2.mine.grad), channel_id=1, source_target_pairs={{0,1},{1,0},{2,3},{3,2},{4,5},{5,4},{6,7},{7,6},{8,9},{9,8},{10,11... | collective-permute-start | bytes 393224 | tf_op jit(solution)/shard_map/ppermute | solution.py:28
  73.8 1.0 collective-permute-done.12.theirs
  74.8 0.4 grams.1
  75.2 1.3 %collective-permute-start.13 = (bf16[10,16,128]{2,1,0:T(8,128)(2,1)S(1)}, bf16[10,16,128]{2,1,0:T(8,128)(2,1)S(1)}, u32[]{:S(2)}, u32[]{:S(2)}) collective-permute-start(bf16[10,16,128]{2,1,0:T(8,128)(2,1)S(1)} %get-tuple-element.61), channel_id=1, source_target_pairs={{0,2},{2,4},{4,6},{6,0},{1,3},{3,5},{5,7},{7,1},{8,10},{10,12},{12... | collective-permute-start | bytes 122888 | tf_op jit(solution)/shard_map/ppermute | solution.py:28
  76.5 2.5 %collective-permute-start.14 = (bf16[10,16,128]{2,1,0:T(8,128)(2,1)S(1)}, bf16[10,16,128]{2,1,0:T(8,128)(2,1)S(1)}, u32[]{:S(2)}, u32[]{:S(2)}) collective-permute-start(bf16[10,16,128]{2,1,0:T(8,128)(2,1)S(1)} %get-tuple-element.62), channel_id=1, source_target_pairs={{0,4},{2,6},{4,0},{6,2},{1,5},{3,7},{5,1},{7,3},{8,12},{10,14},{12... | collective-permute-start | bytes 122888 | tf_op jit(solution)/shard_map/ppermute | solution.py:28
  79.0 1.1 collective-permute-start.15
  80.1 0.0 collective-permute-done.13
  80.1 0.9 collective-permute-done.14
  81.0 1.1 collective-permute-done.15
  82.2 14.6 %all_to_all.10.column = bf16[8,10,16,128]{3,2,1,0:T(8,128)(2,1)S(1)} all-to-all(bf16[8,10,16,128]{3,2,1,0:T(8,128)(2,1)S(1)} %broadcast_in_dim.22), channel_id=1, replica_groups=mesh['z'=8,'y'=4,'x'=4,'c'=2] {'z'}, dimensions={0} | all-to-all | bytes 655360 | tf_op jit(solution)/shard_map/all_to_all | solution.py:400
  96.8 0.7 choose.1
  97.5 0.1 collective-permute-start.16
  97.6 2.0 %collective-permute-start.17 = (bf16[3,10,16,128]{3,2,1,0:T(8,128)(2,1)S(1)}, bf16[3,10,16,128]{3,2,1,0:T(8,128)(2,1)S(1)}, u32[]{:S(2)}, u32[]{:S(2)}) collective-permute-start(bf16[3,10,16,128]{3,2,1,0:T(8,128)(2,1)S(1)} %get-tuple-element.66), channel_id=1, source_target_pairs={{0,16},{8,24},{16,0},{24,8},{1,17},{9,25},{17,1},{25,9},{2,18},{10... | collective-permute-start | bytes 368648 | tf_op jit(solution)/shard_map/ppermute | solution.py:28
  99.6 0.7 collective-permute-start.18
  100.3 3.6 %collective-permute-done.16 = bf16[3,10,16,128]{3,2,1,0:T(8,128)(2,1)S(1)} collective-permute-done((bf16[3,10,16,128]{3,2,1,0:T(8,128)(2,1)S(1)}, bf16[3,10,16,128]{3,2,1,0:T(8,128)(2,1)S(1)}, u32[]{:S(2)}, u32[]{:S(2)}) %collective-permute-start.16) | collective-permute-done | bytes 122912 | tf_op jit(solution)/shard_map/ppermute | solution.py:28
  103.9 0.6 collective-permute-done.18
  104.5 0.1 collective-permute-start.19
  104.6 2.6 %collective-permute-start.20 = (bf16[3,10,16,128]{3,2,1,0:T(8,128)(2,1)S(1)}, bf16[3,10,16,128]{3,2,1,0:T(8,128)(2,1)S(1)}, u32[]{:S(2)}, u32[]{:S(2)}) collective-permute-start(bf16[3,10,16,128]{3,2,1,0:T(8,128)(2,1)S(1)} %add_add_fusion.refs_0_), channel_id=1, source_target_pairs={{0,4},{2,6},{4,0},{6,2},{1,5},{3,7},{5,1},{7,3},{8,12},{10,14},{12... | collective-permute-start | bytes 368648 | tf_op jit(solution)/shard_map/ppermute | solution.py:28
  107.2 0.5 collective-permute-start.21
  107.7 6.1 %collective-permute-start.22 = (bf16[3,10,16,128]{3,2,1,0:T(8,128)(2,1)S(1)}, bf16[3,10,16,128]{3,2,1,0:T(8,128)(2,1)S(1)}, u32[]{:S(2)}, u32[]{:S(2)}) collective-permute-start(bf16[3,10,16,128]{3,2,1,0:T(8,128)(2,1)S(1)} %add_add_fusion.refs_0_), channel_id=1, source_target_pairs={{0,1},{1,0},{2,3},{3,2},{4,5},{5,4},{6,7},{7,6},{8,9},{9,8},{10,11... | collective-permute-start | bytes 368648 | tf_op jit(solution)/shard_map/ppermute | solution.py:28
  113.9 2.0 %collective-permute-start.23 = (bf16[3,10,16,128]{3,2,1,0:T(8,128)(2,1)S(1)}, bf16[3,10,16,128]{3,2,1,0:T(8,128)(2,1)S(1)}, u32[]{:S(2)}, u32[]{:S(2)}) collective-permute-start(bf16[3,10,16,128]{3,2,1,0:T(8,128)(2,1)S(1)} %collective-permute-done.19.refs_1_), channel_id=1, source_target_pairs={{0,1},{1,0},{2,3},{3,2},{4,5},{5,4},{6,7},{7,6},{8,9},{9,8},{10,11... | collective-permute-start | bytes 368648 | tf_op jit(solution)/shard_map/ppermute | solution.py:28
  115.8 1.9 %collective-permute-start.24 = (bf16[3,10,16,128]{3,2,1,0:T(8,128)(2,1)S(1)}, bf16[3,10,16,128]{3,2,1,0:T(8,128)(2,1)S(1)}, u32[]{:S(2)}, u32[]{:S(2)}) collective-permute-start(bf16[3,10,16,128]{3,2,1,0:T(8,128)(2,1)S(1)} %collective-permute-done.20.refs_2_), channel_id=1, source_target_pairs={{0,1},{1,0},{2,3},{3,2},{4,5},{5,4},{6,7},{7,6},{8,9},{9,8},{10,11... | collective-permute-start | bytes 368648 | tf_op jit(solution)/shard_map/ppermute | solution.py:28
  117.7 0.0 collective-permute-done.21.refs_3_
  117.7 0.7 collective-permute-start.25
  118.4 0.0 collective-permute-done.22.refs_4_
  118.4 0.3 collective-permute-done.24.refs_6_
  118.7 0.7 collective-permute-done.25.refs_7_
  119.4 1.8 %finish.1 = (f32[2,512,512]{2,1,0:T(8,128)}, bf16[512,128]{1,0:T(8,128)(2,1)}) custom-call(f32[2,512,512]{2,1,0:T(8,128)S(1)} %bitcast.17, f32[2,8,128]{2,1,0:T(8,128)S(1)} %get-tuple-element.41.occupied, bf16[128,512]{1,0:T(8,128)(2,1)S(1)} %fusion.2.mine.grad, bf16[3,10,16,128]{3,2,1,0:T(8,128)(2,1)S(1)} %add_add_fusion.refs_0_, ...), custom_call_target="tpu_custom_call" | custom-call | tf_op jit(solution)/shard_map/finish/pallas_call | solution.py:359
  (16 shorter events, 0.1 us)
Async XLA Ops:
  0.6 8.5 %copy-start.1 = (f32[1,2,512,512]{3,2,1,0:T(8,128)S(1)}, f32[1,2,512,512]{3,2,1,0:T(8,128)}, u32[]{:S(2)}) copy-start(f32[1,2,512,512]{3,2,1,0:T(8,128)} %param.7) | copy-start | bytes 6291460
  0.6 8.5 %copy-start.4 = (s32[32]{0:T(128)S(1)}, s32[32]{0:T(128)}, u32[]{:S(2)}) copy-start(s32[32]{0:T(128)} %worker_of.3) | copy-start | bytes 388
  3.8 31.3 %collective-permute-start = (bf16[128,2560]{1,0:T(8,128)(2,1)}, bf16[128,2560]{1,0:T(8,128)(2,1)S(1)}, u32[]{:S(2)}, u32[]{:S(2)}) collective-permute-start(bf16[128,2560]{1,0:T(8,128)(2,1)} %get-tuple-element.39), channel_id=1, source_target_pairs={{0,24},{8,0},{16,8},{24,16},{1,25},{9,1},{17,9},{25,17},{2,26},{10... | collective-permute-start | bytes 1966088 | tf_op jit(solution)/shard_map/ppermute | solution.py:28
  7.5 29.3 %collective-permute-start.1 = (bf16[128,2560]{1,0:T(8,128)(2,1)}, bf16[128,2560]{1,0:T(8,128)(2,1)}, u32[]{:S(2)}, u32[]{:S(2)}) collective-permute-start(bf16[128,2560]{1,0:T(8,128)(2,1)} %get-tuple-element.37), channel_id=1, source_target_pairs={{0,8},{8,16},{16,24},{24,0},{1,9},{9,17},{17,25},{25,1},{2,10},{10... | collective-permute-start | bytes 1966088 | tf_op jit(solution)/shard_map/ppermute | solution.py:28
  7.5 32.7 %collective-permute-start.2 = (bf16[128,2560]{1,0:T(8,128)(2,1)}, bf16[128,2560]{1,0:T(8,128)(2,1)}, u32[]{:S(2)}, u32[]{:S(2)}) collective-permute-start(bf16[128,2560]{1,0:T(8,128)(2,1)} %get-tuple-element.38), channel_id=1, source_target_pairs={{0,16},{8,24},{16,0},{24,8},{1,17},{9,25},{17,1},{25,9},{2,18},{10... | collective-permute-start | bytes 1966088 | tf_op jit(solution)/shard_map/ppermute | solution.py:28
  17.5 45.9 %all-to-all-start = ((bf16[8,2,10,16,128]{4,3,2,1,0:T(8,128)(2,1)}), bf16[8,2,10,16,128]{4,3,2,1,0:T(8,128)(2,1)S(1)}, u32[]{:S(2)}, u32[]{:S(2)}) async-start(bf16[8,2,10,16,128]{4,3,2,1,0:T(8,128)(2,1)} %broadcast_in_dim.10), calls=%async_computation | async-start | bytes 1310720 | tf_op jit(solution)/shard_map/all_to_all | solution.py:380
  27.9 2.2 %copy-start = (bf16[256,8192]{1,0:T(8,128)(2,1)S(1)}, bf16[256,8192]{1,0:T(8,128)(2,1)}, u32[]{:S(2)}) copy-start(bf16[256,8192]{1,0:T(8,128)(2,1)} %act.2) | copy-start | bytes 12582916
  30.1 10.1 %copy-start.2 = (bf16[2,256,128]{2,1,0:T(8,128)(2,1)S(1)}, bf16[2,256,128]{2,1,0:T(8,128)(2,1)}, u32[]{:S(2)}) copy-start(bf16[2,256,128]{2,1,0:T(8,128)(2,1)} %cot.3) | copy-start | bytes 393220
  35.1 7.7 %collective-permute-start.5 = (bf16[128,2560]{1,0:T(8,128)(2,1)S(1)}, bf16[128,2560]{1,0:T(8,128)(2,1)S(1)}, u32[]{:S(2)}, u32[]{:S(2)}) collective-permute-start(bf16[128,2560]{1,0:T(8,128)(2,1)S(1)} %collective-permute-done.refs_2_), channel_id=1, source_target_pairs={{0,1},{1,0},{2,3},{3,2},{4,5},{5,4},{6,7},{7,6},{8,9},{9,8},{10,11... | collective-permute-start | bytes 1966088 | tf_op jit(solution)/shard_map/ppermute | solution.py:28
  36.8 6.0 %collective-permute-start.3 = (bf16[128,2560]{1,0:T(8,128)(2,1)}, bf16[128,2560]{1,0:T(8,128)(2,1)S(1)}, u32[]{:S(2)}, u32[]{:S(2)}) collective-permute-start(bf16[128,2560]{1,0:T(8,128)(2,1)} %collective-permute-done.1.refs_0_), channel_id=1, source_target_pairs={{0,1},{1,0},{2,3},{3,2},{4,5},{5,4},{6,7},{7,6},{8,9},{9,8},{10,11... | collective-permute-start | bytes 1966088 | tf_op jit(solution)/shard_map/ppermute | solution.py:28
  40.2 2.9 %collective-permute-start.4 = (bf16[128,2560]{1,0:T(8,128)(2,1)}, bf16[128,2560]{1,0:T(8,128)(2,1)S(1)}, u32[]{:S(2)}, u32[]{:S(2)}) collective-permute-start(bf16[128,2560]{1,0:T(8,128)(2,1)} %collective-permute-done.2.refs_1_), channel_id=1, source_target_pairs={{0,1},{1,0},{2,3},{3,2},{4,5},{5,4},{6,7},{7,6},{8,9},{9,8},{10,11... | collective-permute-start | bytes 1966088 | tf_op jit(solution)/shard_map/ppermute | solution.py:28
  44.4 52.5 %copy-start.3 = (s32[16]{0:T(128)S(1)}, s32[16]{0:T(128)}, u32[]{:S(2)}) copy-start(s32[16]{0:T(128)} %plan.1) | copy-start | bytes 196
  44.4 14.5 %collective-permute-start.6 = (bf16[2,128,512]{2,1,0:T(8,128)(2,1)S(1)}, bf16[2,128,512]{2,1,0:T(8,128)(2,1)S(1)}, u32[]{:S(2)}, u32[]{:S(2)}) collective-permute-start(bf16[2,128,512]{2,1,0:T(8,128)(2,1)S(1)} %get-tuple-element.50), channel_id=1, source_target_pairs={{0,32},{32,64},{64,96},{96,128},{128,160},{160,192},{192,224},{224... | collective-permute-start | bytes 786440 | tf_op jit(solution)/shard_map/ppermute | solution.py:28
  46.1 12.7 %collective-permute-start.7 = (bf16[2,128,512]{2,1,0:T(8,128)(2,1)S(1)}, bf16[2,128,512]{2,1,0:T(8,128)(2,1)S(1)}, u32[]{:S(2)}, u32[]{:S(2)}) collective-permute-start(bf16[2,128,512]{2,1,0:T(8,128)(2,1)S(1)} %get-tuple-element.51), channel_id=1, source_target_pairs={{0,224},{32,0},{64,32},{96,64},{128,96},{160,128},{192,160},{224,1... | collective-permute-start | bytes 786440 | tf_op jit(solution)/shard_map/ppermute | solution.py:28
  50.1 8.7 %collective-permute-start.8 = (bf16[64,512]{1,0:T(8,128)(2,1)S(1)}, bf16[64,512]{1,0:T(8,128)(2,1)S(1)}, u32[]{:S(2)}, u32[]{:S(2)}) collective-permute-start(bf16[64,512]{1,0:T(8,128)(2,1)S(1)} %get-tuple-element.54), channel_id=1, source_target_pairs={{0,64},{32,96},{64,128},{96,160},{128,192},{160,224},{192,0},{224,... | collective-permute-start | bytes 196616 | tf_op jit(solution)/shard_map/ppermute | solution.py:28
  50.1 8.7 %collective-permute-start.9 = (bf16[64,512]{1,0:T(8,128)(2,1)S(1)}, bf16[64,512]{1,0:T(8,128)(2,1)S(1)}, u32[]{:S(2)}, u32[]{:S(2)}) collective-permute-start(bf16[64,512]{1,0:T(8,128)(2,1)S(1)} %get-tuple-element.55), channel_id=1, source_target_pairs={{0,192},{32,224},{64,0},{96,32},{128,64},{160,96},{192,128},{224,1... | collective-permute-start | bytes 196616 | tf_op jit(solution)/shard_map/ppermute | solution.py:28
  59.6 9.2 %collective-permute-start.10 = (bf16[128,512]{1,0:T(8,128)(2,1)}, bf16[128,512]{1,0:T(8,128)(2,1)}, u32[]{:S(2)}, u32[]{:S(2)}) collective-permute-start(bf16[128,512]{1,0:T(8,128)(2,1)} %get-tuple-element.56), channel_id=1, source_target_pairs={{0,64},{32,96},{64,128},{96,160},{128,192},{160,224},{192,0},{224,... | collective-permute-start | bytes 393224 | tf_op jit(solution)/shard_map/ppermute | solution.py:28
  63.3 5.6 %collective-permute-start.11 = (bf16[128,512]{1,0:T(8,128)(2,1)}, bf16[128,512]{1,0:T(8,128)(2,1)}, u32[]{:S(2)}, u32[]{:S(2)}) collective-permute-start(bf16[128,512]{1,0:T(8,128)(2,1)} %get-tuple-element.57), channel_id=1, source_target_pairs={{0,192},{32,224},{64,0},{96,32},{128,64},{160,96},{192,128},{224,1... | collective-permute-start | bytes 393224 | tf_op jit(solution)/shard_map/ppermute | solution.py:28
  70.0 4.8 %collective-permute-start.12 = (bf16[128,512]{1,0:T(8,128)(2,1)S(1)}, bf16[128,512]{1,0:T(8,128)(2,1)S(1)}, u32[]{:S(2)}, u32[]{:S(2)}) collective-permute-start(bf16[128,512]{1,0:T(8,128)(2,1)S(1)} %fusion.2.mine.grad), channel_id=1, source_target_pairs={{0,1},{1,0},{2,3},{3,2},{4,5},{5,4},{6,7},{7,6},{8,9},{9,8},{10,11... | collective-permute-start | bytes 393224 | tf_op jit(solution)/shard_map/ppermute | solution.py:28
  75.2 4.9 %collective-permute-start.13 = (bf16[10,16,128]{2,1,0:T(8,128)(2,1)S(1)}, bf16[10,16,128]{2,1,0:T(8,128)(2,1)S(1)}, u32[]{:S(2)}, u32[]{:S(2)}) collective-permute-start(bf16[10,16,128]{2,1,0:T(8,128)(2,1)S(1)} %get-tuple-element.61), channel_id=1, source_target_pairs={{0,2},{2,4},{4,6},{6,0},{1,3},{3,5},{5,7},{7,1},{8,10},{10,12},{12... | collective-permute-start | bytes 122888 | tf_op jit(solution)/shard_map/ppermute | solution.py:28
  76.5 4.5 %collective-permute-start.14 = (bf16[10,16,128]{2,1,0:T(8,128)(2,1)S(1)}, bf16[10,16,128]{2,1,0:T(8,128)(2,1)S(1)}, u32[]{:S(2)}, u32[]{:S(2)}) collective-permute-start(bf16[10,16,128]{2,1,0:T(8,128)(2,1)S(1)} %get-tuple-element.62), channel_id=1, source_target_pairs={{0,4},{2,6},{4,0},{6,2},{1,5},{3,7},{5,1},{7,3},{8,12},{10,14},{12... | collective-permute-start | bytes 122888 | tf_op jit(solution)/shard_map/ppermute | solution.py:28
  79.0 3.1 %collective-permute-start.15 = (bf16[10,16,128]{2,1,0:T(8,128)(2,1)S(1)}, bf16[10,16,128]{2,1,0:T(8,128)(2,1)S(1)}, u32[]{:S(2)}, u32[]{:S(2)}) collective-permute-start(bf16[10,16,128]{2,1,0:T(8,128)(2,1)S(1)} %get-tuple-element.63), channel_id=1, source_target_pairs={{0,6},{2,0},{4,2},{6,4},{1,7},{3,1},{5,3},{7,5},{8,14},{10,8},{12,... | collective-permute-start | bytes 122888 | tf_op jit(solution)/shard_map/ppermute | solution.py:28
  97.5 6.3 %collective-permute-start.16 = (bf16[3,10,16,128]{3,2,1,0:T(8,128)(2,1)S(1)}, bf16[3,10,16,128]{3,2,1,0:T(8,128)(2,1)S(1)}, u32[]{:S(2)}, u32[]{:S(2)}) collective-permute-start(bf16[3,10,16,128]{3,2,1,0:T(8,128)(2,1)S(1)} %get-tuple-element.65), channel_id=1, source_target_pairs={{0,8},{8,16},{16,24},{24,0},{1,9},{9,17},{17,25},{25,1},{2,10},{10... | collective-permute-start | bytes 368648 | tf_op jit(solution)/shard_map/ppermute | solution.py:28
  97.6 6.2 %collective-permute-start.17 = (bf16[3,10,16,128]{3,2,1,0:T(8,128)(2,1)S(1)}, bf16[3,10,16,128]{3,2,1,0:T(8,128)(2,1)S(1)}, u32[]{:S(2)}, u32[]{:S(2)}) collective-permute-start(bf16[3,10,16,128]{3,2,1,0:T(8,128)(2,1)S(1)} %get-tuple-element.66), channel_id=1, source_target_pairs={{0,16},{8,24},{16,0},{24,8},{1,17},{9,25},{17,1},{25,9},{2,18},{10... | collective-permute-start | bytes 368648 | tf_op jit(solution)/shard_map/ppermute | solution.py:28
  99.6 4.9 %collective-permute-start.18 = (bf16[3,10,16,128]{3,2,1,0:T(8,128)(2,1)S(1)}, bf16[3,10,16,128]{3,2,1,0:T(8,128)(2,1)S(1)}, u32[]{:S(2)}, u32[]{:S(2)}) collective-permute-start(bf16[3,10,16,128]{3,2,1,0:T(8,128)(2,1)S(1)} %get-tuple-element.67), channel_id=1, source_target_pairs={{0,24},{8,0},{16,8},{24,16},{1,25},{9,1},{17,9},{25,17},{2,26},{10... | collective-permute-start | bytes 368648 | tf_op jit(solution)/shard_map/ppermute | solution.py:28
  104.5 9.4 %collective-permute-start.19 = (bf16[3,10,16,128]{3,2,1,0:T(8,128)(2,1)S(1)}, bf16[3,10,16,128]{3,2,1,0:T(8,128)(2,1)S(1)}, u32[]{:S(2)}, u32[]{:S(2)}) collective-permute-start(bf16[3,10,16,128]{3,2,1,0:T(8,128)(2,1)S(1)} %add_add_fusion.refs_0_), channel_id=1, source_target_pairs={{0,2},{2,4},{4,6},{6,0},{1,3},{3,5},{5,7},{7,1},{8,10},{10,12},{12... | collective-permute-start | bytes 368648 | tf_op jit(solution)/shard_map/ppermute | solution.py:28
  104.6 11.2 %collective-permute-start.20 = (bf16[3,10,16,128]{3,2,1,0:T(8,128)(2,1)S(1)}, bf16[3,10,16,128]{3,2,1,0:T(8,128)(2,1)S(1)}, u32[]{:S(2)}, u32[]{:S(2)}) collective-permute-start(bf16[3,10,16,128]{3,2,1,0:T(8,128)(2,1)S(1)} %add_add_fusion.refs_0_), channel_id=1, source_target_pairs={{0,4},{2,6},{4,0},{6,2},{1,5},{3,7},{5,1},{7,3},{8,12},{10,14},{12... | collective-permute-start | bytes 368648 | tf_op jit(solution)/shard_map/ppermute | solution.py:28
  107.2 10.5 %collective-permute-start.21 = (bf16[3,10,16,128]{3,2,1,0:T(8,128)(2,1)S(1)}, bf16[3,10,16,128]{3,2,1,0:T(8,128)(2,1)S(1)}, u32[]{:S(2)}, u32[]{:S(2)}) collective-permute-start(bf16[3,10,16,128]{3,2,1,0:T(8,128)(2,1)S(1)} %add_add_fusion.refs_0_), channel_id=1, source_target_pairs={{0,6},{2,0},{4,2},{6,4},{1,7},{3,1},{5,3},{7,5},{8,14},{10,8},{12,... | collective-permute-start | bytes 368648 | tf_op jit(solution)/shard_map/ppermute | solution.py:28
  107.7 10.7 %collective-permute-start.22 = (bf16[3,10,16,128]{3,2,1,0:T(8,128)(2,1)S(1)}, bf16[3,10,16,128]{3,2,1,0:T(8,128)(2,1)S(1)}, u32[]{:S(2)}, u32[]{:S(2)}) collective-permute-start(bf16[3,10,16,128]{3,2,1,0:T(8,128)(2,1)S(1)} %add_add_fusion.refs_0_), channel_id=1, source_target_pairs={{0,1},{1,0},{2,3},{3,2},{4,5},{5,4},{6,7},{7,6},{8,9},{9,8},{10,11... | collective-permute-start | bytes 368648 | tf_op jit(solution)/shard_map/ppermute | solution.py:28
  113.9 4.6 %collective-permute-start.23 = (bf16[3,10,16,128]{3,2,1,0:T(8,128)(2,1)S(1)}, bf16[3,10,16,128]{3,2,1,0:T(8,128)(2,1)S(1)}, u32[]{:S(2)}, u32[]{:S(2)}) collective-permute-start(bf16[3,10,16,128]{3,2,1,0:T(8,128)(2,1)S(1)} %collective-permute-done.19.refs_1_), channel_id=1, source_target_pairs={{0,1},{1,0},{2,3},{3,2},{4,5},{5,4},{6,7},{7,6},{8,9},{9,8},{10,11... | collective-permute-start | bytes 368648 | tf_op jit(solution)/shard_map/ppermute | solution.py:28
  115.8 2.9 %collective-permute-start.24 = (bf16[3,10,16,128]{3,2,1,0:T(8,128)(2,1)S(1)}, bf16[3,10,16,128]{3,2,1,0:T(8,128)(2,1)S(1)}, u32[]{:S(2)}, u32[]{:S(2)}) collective-permute-start(bf16[3,10,16,128]{3,2,1,0:T(8,128)(2,1)S(1)} %collective-permute-done.20.refs_2_), channel_id=1, source_target_pairs={{0,1},{1,0},{2,3},{3,2},{4,5},{5,4},{6,7},{7,6},{8,9},{9,8},{10,11... | collective-permute-start | bytes 368648 | tf_op jit(solution)/shard_map/ppermute | solution.py:28
  117.7 1.7 %collective-permute-start.25 = (bf16[3,10,16,128]{3,2,1,0:T(8,128)(2,1)S(1)}, bf16[3,10,16,128]{3,2,1,0:T(8,128)(2,1)S(1)}, u32[]{:S(2)}, u32[]{:S(2)}) collective-permute-start(bf16[3,10,16,128]{3,2,1,0:T(8,128)(2,1)S(1)} %collective-permute-done.21.refs_3_), channel_id=1, source_target_pairs={{0,1},{1,0},{2,3},{3,2},{4,5},{5,4},{6,7},{7,6},{8,9},{9,8},{10,11... | collective-permute-start | bytes 368648 | tf_op jit(solution)/shard_map/ppermute | solution.py:28

commit v6 on v4

--- a/solution.py
+++ b/solution.py
@@ -386,7 +386,6 @@
     kept, two, six, up, down, half0, half1 = second_products(acc, crossed, swapped)
     up, down = shift(up, "z", NZ, 1), shift(down, "z", NZ, 7)
     ahead, back = merge(two, six, up, down, shift(half0, "z", NZ, 2), shift(half1, "z", NZ, 6))
-    kept, root_strips = lax.optimization_barrier((kept, root_strips))
     total = kept + up[0].astype(F32) + down[0].astype(F32)
     total = total + shift(ahead, "z", NZ, 2).astype(F32) + shift(back, "z", NZ, 6).astype(F32)
     grad = total.astype(BF)
@@ -395,7 +394,7 @@
     strip, *sends = grams(grad, theirs)
     for o, send in enumerate(sends):
         strip = strip + shift(send, "x", NX, o + 1).astype(F32)
-    strip = strip.astype(BF)
+    strip, root_strips = lax.optimization_barrier((strip.astype(BF), root_strips))
     column = lax.all_to_all(jnp.broadcast_to(strip[None], (8, 10, 16, 128)), "z", 0, 0, tiled=True)
     routed = choose(plan, root_strips.reshape(16, 10, 16, 128), column)
     arrived = routed[0]

time: 121 us -> 136 us (1.12)
  waiting for transfers between devices: 24.3 us -> 38.6 us
  starting transfers between devices: 56.4 us -> 52.9 us
  local copies, waits for them, and re-layouts: 3.18 us -> 6.19 us
  blocking collectives: 14.6 us -> 16.2 us
    ppermute x26, waiting for transfers between devices: 24.3 us -> 38.6 us  [shift(): lax.ppermute(x, axis, [(i, (i + offset) % size) for i in range(size)])]
    ppermute x26, starting transfers between devices: 48.2 us -> 44.7 us  [shift(): lax.ppermute(x, axis, [(i, (i + offset) % size) for i in range(size)])]
    unnamed x10 -> x12, local copies, waits for them, and re-layouts: 2.2 us -> 5.23 us
    all_to_all x1, blocking collectives: 14.6 us -> 16.2 us  [local(): lax.all_to_all(jnp.broadcast_to(strip[None], (8, 10, 16, 128)), 'z', 0, 0...]
    pallas_call x1, Pallas kernels: 1.28 us -> 2.79 us  [second_products(): pl.pallas_call(second_kernel, out_shape=[struct((128, 512), F32)] * 3 + [...]
  transfers between devices with their start and end apart: 27 -> 27, of which waited for: 12 -> 12; matrix products, arithmetic and copies ran while one was open for 1% -> 1% of each run, Pallas kernels for 12% -> 11%
where the time goes in v6:
time: 136 us
  starting transfers between devices  52.9 us (39%)
  waiting for transfers between devices  38.6 us (28%)
  Pallas kernels  21 us (15%)
  blocking collectives  16.2 us (12%)
  local copies, waits for them, and re-layouts  6.19 us (5%)
    ppermute x26, starting transfers between devices, shift(): lax.ppermute(x, axis, [(i, (i + offset) % size) for i in range(size)])  44.7 us
    ppermute x26, waiting for transfers between devices, shift(): lax.ppermute(x, axis, [(i, (i + offset) % size) for i in range(size)])  38.6 us
    all_to_all x1, blocking collectives, local(): lax.all_to_all(jnp.broadcast_to(strip[None], (8, 10, 16, 128)), 'z', 0, 0...  16.2 us
    all_to_all x1, starting transfers between devices, local(): lax.all_to_all(jnp.broadcast_to(strips[None], (8, 2, 10, 16, 128)), 'z',...  8.19 us
    pallas_call x1, Pallas kernels, make_roots(): pl.pallas_call(root_kernel, grid=(2,), out_shape=[struct((2, 512, 512), F...  7.39 us
    unnamed x12, local copies, waits for them, and re-layouts  5.23 us
    pallas_call x1, Pallas kernels, pack(): pl.pallas_call(pack_kernel, out_shape=[struct((128, 2560), BF)] * 3, in_s...  3.06 us
    pallas_call x1, Pallas kernels, second_products(): pl.pallas_call(second_kernel, out_shape=[struct((128, 512), F32)] * 3 + [...  2.79 us
  transfers between devices with their start and end apart: 27, of which 12 were waited for; matrix products, arithmetic and copies ran while one was open for 1% of the time, Pallas kernels for 11%

profile of v6, /device:TPU:1, one launch (start us, length us, event | category | flops | bytes accessed | tf_op | source)
XLA Modules:
  0.0 135.8 jit_solution(5897595569852880184)
XLA Ops:
  0.6 3.1 %pack.1 = (bf16[128,2560]{1,0:T(8,128)(2,1)}, bf16[128,2560]{1,0:T(8,128)(2,1)}, bf16[128,2560]{1,0:T(8,128)(2,1)}) custom-call(bf16[256,8192]{1,0:T(8,128)(2,1)} %act.2, bf16[2,256,128]{2,1,0:T(8,128)(2,1)} %cot.3), custom_call_target="tpu_custom_call" | custom-call | tf_op jit(solution)/shard_map/pack/pallas_call | solution.py:67
  3.7 2.2 %collective-permute-start = (bf16[128,2560]{1,0:T(8,128)(2,1)}, bf16[128,2560]{1,0:T(8,128)(2,1)S(1)}, u32[]{:S(2)}, u32[]{:S(2)}) collective-permute-start(bf16[128,2560]{1,0:T(8,128)(2,1)} %get-tuple-element.39), channel_id=1, source_target_pairs={{0,8},{8,16},{16,24},{24,0},{1,9},{9,17},{17,25},{25,1},{2,10},{10... | collective-permute-start | bytes 1966088 | tf_op jit(solution)/shard_map/ppermute | solution.py:28
  5.9 2.6 %collective-permute-start.1 = (bf16[128,2560]{1,0:T(8,128)(2,1)}, bf16[128,2560]{1,0:T(8,128)(2,1)S(1)}, u32[]{:S(2)}, u32[]{:S(2)}) collective-permute-start(bf16[128,2560]{1,0:T(8,128)(2,1)} %get-tuple-element.40), channel_id=1, source_target_pairs={{0,16},{8,24},{16,0},{24,8},{1,17},{9,25},{17,1},{25,9},{2,18},{10... | collective-permute-start | bytes 1966088 | tf_op jit(solution)/shard_map/ppermute | solution.py:28
  8.5 1.1 collective-permute-start.2
  9.6 2.3 %plan.1 = s32[16]{0:T(128)} custom-call(s32[32]{0:T(128)} %worker_of.3), custom_call_target="tpu_custom_call" | custom-call | tf_op jit(solution)/shard_map/plan/pallas_call | solution.py:221
  11.9 0.0 copy-start
  11.9 2.2 %copy-done = bf16[256,8192]{1,0:T(8,128)(2,1)S(1)} copy-done((bf16[256,8192]{1,0:T(8,128)(2,1)S(1)}, bf16[256,8192]{1,0:T(8,128)(2,1)}, u32[]{:S(2)}) %copy-start) | copy-done | bytes 4194328
  14.1 0.1 own.1
  14.2 1.4 %copy-done.1 = f32[1,2,512,512]{3,2,1,0:T(8,128)S(1)} copy-done((f32[1,2,512,512]{3,2,1,0:T(8,128)S(1)}, f32[1,2,512,512]{3,2,1,0:T(8,128)}, u32[]{:S(2)}) %copy-start.1) | copy-done | bytes 2097176
  15.6 7.4 %roots.1 = (f32[2,512,512]{2,1,0:T(8,128)}, bf16[2,10,16,128]{3,2,1,0:T(8,128)(2,1)S(1)}, f32[2,8,128]{2,1,0:T(8,128)S(1)}) custom-call(s32[32]{0:T(128)S(1)} %copy-done.5, f32[2,512,512]{2,1,0:T(8,128)S(1)} %bitcast.16), custom_call_target="tpu_custom_call" | custom-call | flops 3758096384 | bytes 4194304 | tf_op jit(solution)/shard_map/roots/pallas_call | solution.py:263
  23.0 0.0 collective-permute-done.refs_0_
  23.0 13.9 %collective-permute-done.1.refs_1_ = bf16[128,2560]{1,0:T(8,128)(2,1)S(1)} collective-permute-done((bf16[128,2560]{1,0:T(8,128)(2,1)}, bf16[128,2560]{1,0:T(8,128)(2,1)S(1)}, u32[]{:S(2)}, u32[]{:S(2)}) %collective-permute-start.1) | collective-permute-done | bytes 655392 | tf_op jit(solution)/shard_map/ppermute | solution.py:28
  36.9 0.0 collective-permute-done.2.refs_2_
  36.9 1.5 %collective-permute-start.3 = (bf16[128,2560]{1,0:T(8,128)(2,1)S(1)}, bf16[128,2560]{1,0:T(8,128)(2,1)}, u32[]{:S(2)}, u32[]{:S(2)}) collective-permute-start(bf16[128,2560]{1,0:T(8,128)(2,1)S(1)} %collective-permute-done.refs_0_), channel_id=1, source_target_pairs={{0,1},{1,0},{2,3},{3,2},{4,5},{5,4},{6,7},{7,6},{8,9},{9,8},{10,11... | collective-permute-start | bytes 1966088 | tf_op jit(solution)/shard_map/ppermute | solution.py:28
  38.5 0.0 collective-permute-start.4
  38.5 0.5 collective-permute-start.5
  39.0 0.9 broadcast_in_dim.10
  39.9 8.2 %all-to-all-start = ((bf16[8,2,10,16,128]{4,3,2,1,0:T(8,128)(2,1)}), bf16[8,2,10,16,128]{4,3,2,1,0:T(8,128)(2,1)S(1)}, u32[]{:S(2)}, u32[]{:S(2)}) async-start(bf16[8,2,10,16,128]{4,3,2,1,0:T(8,128)(2,1)} %broadcast_in_dim.10), calls=%async_computation | async-start | bytes 1310720 | tf_op jit(solution)/shard_map/all_to_all | solution.py:380
  48.1 2.4 %first.1 = (f32[256,2048]{1,0:T(8,128)S(1)}, bf16[256,384]{1,0:T(8,128)(2,1)S(1)}) custom-call(bf16[256,2048]{1,0:T(8,128)(2,1)S(1)} %own.1, bf16[2,256,128]{2,1,0:T(8,128)(2,1)S(1)} %copy-done.3, bf16[128,2560]{1,0:T(8,128)(2,1)S(1)} %collective-permute-done.refs_0_, bf16[128,2560]{1,0:T(8,128)(2,1)S(1)} %collective-permute-done.1.refs_1_, ...), custom_call_target="tpu_custom_call" | custom-call | flops 536870912 | bytes 4194304 | tf_op jit(solution)/shard_map/first/pallas_call | solution.py:121
  50.5 0.0 collective-permute-done.3.refs_0_
  50.5 0.0 collective-permute-done.5.refs_2_
  50.5 2.8 %second.1 = (f32[128,512]{1,0:T(8,128)S(1)}, f32[128,512]{1,0:T(8,128)S(1)}, f32[128,512]{1,0:T(8,128)S(1)}, bf16[2,128,512]{2,1,0:T(8,128)(2,1)S(1)}, bf16[2,12...) custom-call(f32[256,2048]{1,0:T(8,128)S(1)} %get-tuple-element.50.acc, ...), custom_call_target="tpu_custom_call" | custom-call | flops 536870912 | bytes 4194304 | tf_op jit(solution)/shard_map/second/pallas_call | solution.py:162
  53.3 0.0 copy-start.4
  53.3 1.5 %collective-permute-start.6 = (bf16[2,128,512]{2,1,0:T(8,128)(2,1)S(1)}, bf16[2,128,512]{2,1,0:T(8,128)(2,1)S(1)}, u32[]{:S(2)}, u32[]{:S(2)}) collective-permute-start(bf16[2,128,512]{2,1,0:T(8,128)(2,1)S(1)} %get-tuple-element.53), channel_id=1, source_target_pairs={{0,32},{32,64},{64,96},{96,128},{128,160},{160,192},{192,224},{224... | collective-permute-start | bytes 786440 | tf_op jit(solution)/shard_map/ppermute | solution.py:28
  54.8 1.3 collective-permute-start.7
  56.2 1.1 collective-permute-start.8
  57.2 2.5 %collective-permute-start.9 = (bf16[64,512]{1,0:T(8,128)(2,1)S(1)}, bf16[64,512]{1,0:T(8,128)(2,1)S(1)}, u32[]{:S(2)}, u32[]{:S(2)}) collective-permute-start(bf16[64,512]{1,0:T(8,128)(2,1)S(1)} %get-tuple-element.58), channel_id=1, source_target_pairs={{0,192},{32,224},{64,0},{96,32},{128,64},{160,96},{192,128},{224,1... | collective-permute-start | bytes 196616 | tf_op jit(solution)/shard_map/ppermute | solution.py:28
  59.7 14.0 %collective-permute-done.8.low = bf16[64,512]{1,0:T(8,128)(2,1)S(1)} collective-permute-done((bf16[64,512]{1,0:T(8,128)(2,1)S(1)}, bf16[64,512]{1,0:T(8,128)(2,1)S(1)}, u32[]{:S(2)}, u32[]{:S(2)}) %collective-permute-start.8) | collective-permute-done | bytes 65568 | tf_op jit(solution)/shard_map/ppermute | solution.py:28
  73.8 0.1 merge.1
  73.8 2.4 %collective-permute-start.10 = (bf16[128,512]{1,0:T(8,128)(2,1)S(1)}, bf16[128,512]{1,0:T(8,128)(2,1)S(1)}, u32[]{:S(2)}, u32[]{:S(2)}) collective-permute-start(bf16[128,512]{1,0:T(8,128)(2,1)S(1)} %get-tuple-element.59), channel_id=1, source_target_pairs={{0,64},{32,96},{64,128},{96,160},{128,192},{160,224},{192,0},{224,... | collective-permute-start | bytes 393224 | tf_op jit(solution)/shard_map/ppermute | solution.py:28
  76.2 1.5 %collective-permute-start.11 = (bf16[128,512]{1,0:T(8,128)(2,1)S(1)}, bf16[128,512]{1,0:T(8,128)(2,1)S(1)}, u32[]{:S(2)}, u32[]{:S(2)}) collective-permute-start(bf16[128,512]{1,0:T(8,128)(2,1)S(1)} %get-tuple-element.60), channel_id=1, source_target_pairs={{0,192},{32,224},{64,0},{96,32},{128,64},{160,96},{192,128},{224,1... | collective-permute-start | bytes 393224 | tf_op jit(solution)/shard_map/ppermute | solution.py:28
  77.7 4.0 %collective-permute-done.10 = bf16[128,512]{1,0:T(8,128)(2,1)S(1)} collective-permute-done((bf16[128,512]{1,0:T(8,128)(2,1)S(1)}, bf16[128,512]{1,0:T(8,128)(2,1)S(1)}, u32[]{:S(2)}, u32[]{:S(2)}) %collective-permute-start.10) | collective-permute-done | bytes 131104 | tf_op jit(solution)/shard_map/ppermute | solution.py:28
  81.6 0.3 collective-permute-done.11
  81.9 0.1 fusion.2.mine.grad
  82.0 2.9 %collective-permute-start.12 = (bf16[128,512]{1,0:T(8,128)(2,1)S(1)}, bf16[128,512]{1,0:T(8,128)(2,1)S(1)}, u32[]{:S(2)}, u32[]{:S(2)}) collective-permute-start(bf16[128,512]{1,0:T(8,128)(2,1)S(1)} %fusion.2.mine.grad), channel_id=1, source_target_pairs={{0,1},{1,0},{2,3},{3,2},{4,5},{5,4},{6,7},{7,6},{8,9},{9,8},{10,11... | collective-permute-start | bytes 393224 | tf_op jit(solution)/shard_map/ppermute | solution.py:28
  84.9 1.0 collective-permute-done.12.theirs
  85.9 0.4 grams.1
  86.3 1.3 collective-permute-start.13
  87.6 2.5 %collective-permute-start.14 = (bf16[10,16,128]{2,1,0:T(8,128)(2,1)S(1)}, bf16[10,16,128]{2,1,0:T(8,128)(2,1)S(1)}, u32[]{:S(2)}, u32[]{:S(2)}) collective-permute-start(bf16[10,16,128]{2,1,0:T(8,128)(2,1)S(1)} %get-tuple-element.64), channel_id=1, source_target_pairs={{0,4},{2,6},{4,0},{6,2},{1,5},{3,7},{5,1},{7,3},{8,12},{10,14},{12... | collective-permute-start | bytes 122888 | tf_op jit(solution)/shard_map/ppermute | solution.py:28
  90.1 1.2 collective-permute-start.15
  91.2 0.9 collective-permute-done.14
  92.1 1.1 collective-permute-done.15
  93.3 16.2 %all_to_all.10.column = bf16[8,10,16,128]{3,2,1,0:T(8,128)(2,1)S(1)} all-to-all(bf16[8,10,16,128]{3,2,1,0:T(8,128)(2,1)S(1)} %broadcast_in_dim.22), channel_id=1, replica_groups=mesh['z'=8,'y'=4,'x'=4,'c'=2] {'z'}, dimensions={0} | all-to-all | bytes 655360 | tf_op jit(solution)/shard_map/all_to_all | solution.py:398
  109.5 0.7 choose.1
  110.2 1.1 collective-permute-start.16
  111.3 2.1 %collective-permute-start.17 = (bf16[3,10,16,128]{3,2,1,0:T(8,128)(2,1)S(1)}, bf16[3,10,16,128]{3,2,1,0:T(8,128)(2,1)S(1)}, u32[]{:S(2)}, u32[]{:S(2)}) collective-permute-start(bf16[3,10,16,128]{3,2,1,0:T(8,128)(2,1)S(1)} %get-tuple-element.70), channel_id=1, source_target_pairs={{0,16},{8,24},{16,0},{24,8},{1,17},{9,25},{17,1},{25,9},{2,18},{10... | collective-permute-start | bytes 368648 | tf_op jit(solution)/shard_map/ppermute | solution.py:28
  113.4 1.3 collective-permute-start.18
  114.7 0.5 collective-permute-done.16
  115.2 1.8 %collective-permute-done.17 = bf16[3,10,16,128]{3,2,1,0:T(8,128)(2,1)S(1)} collective-permute-done((bf16[3,10,16,128]{3,2,1,0:T(8,128)(2,1)S(1)}, bf16[3,10,16,128]{3,2,1,0:T(8,128)(2,1)S(1)}, u32[]{:S(2)}, u32[]{:S(2)}) %collective-permute-start.17) | collective-permute-done | bytes 122912 | tf_op jit(solution)/shard_map/ppermute | solution.py:28
  117.0 0.1 collective-permute-done.18
  117.2 0.1 collective-permute-start.19
  117.3 2.6 %collective-permute-start.20 = (bf16[3,10,16,128]{3,2,1,0:T(8,128)(2,1)S(1)}, bf16[3,10,16,128]{3,2,1,0:T(8,128)(2,1)S(1)}, u32[]{:S(2)}, u32[]{:S(2)}) collective-permute-start(bf16[3,10,16,128]{3,2,1,0:T(8,128)(2,1)S(1)} %add_add_fusion.refs_0_), channel_id=1, source_target_pairs={{0,4},{2,6},{4,0},{6,2},{1,5},{3,7},{5,1},{7,3},{8,12},{10,14},{12... | collective-permute-start | bytes 368648 | tf_op jit(solution)/shard_map/ppermute | solution.py:28
  119.9 0.5 collective-permute-start.21
  120.4 6.4 %collective-permute-start.22 = (bf16[3,10,16,128]{3,2,1,0:T(8,128)(2,1)S(1)}, bf16[3,10,16,128]{3,2,1,0:T(8,128)(2,1)S(1)}, u32[]{:S(2)}, u32[]{:S(2)}) collective-permute-start(bf16[3,10,16,128]{3,2,1,0:T(8,128)(2,1)S(1)} %add_add_fusion.refs_0_), channel_id=1, source_target_pairs={{0,1},{1,0},{2,3},{3,2},{4,5},{5,4},{6,7},{7,6},{8,9},{9,8},{10,11... | collective-permute-start | bytes 368648 | tf_op jit(solution)/shard_map/ppermute | solution.py:28
  126.8 0.0 collective-permute-done.19.refs_1_
  126.8 2.0 %collective-permute-start.23 = (bf16[3,10,16,128]{3,2,1,0:T(8,128)(2,1)S(1)}, bf16[3,10,16,128]{3,2,1,0:T(8,128)(2,1)S(1)}, u32[]{:S(2)}, u32[]{:S(2)}) collective-permute-start(bf16[3,10,16,128]{3,2,1,0:T(8,128)(2,1)S(1)} %collective-permute-done.19.refs_1_), channel_id=1, source_target_pairs={{0,1},{1,0},{2,3},{3,2},{4,5},{5,4},{6,7},{7,6},{8,9},{9,8},{10,11... | collective-permute-start | bytes 368648 | tf_op jit(solution)/shard_map/ppermute | solution.py:28
  128.8 0.0 collective-permute-done.20.refs_2_
  128.8 1.9 %collective-permute-start.24 = (bf16[3,10,16,128]{3,2,1,0:T(8,128)(2,1)S(1)}, bf16[3,10,16,128]{3,2,1,0:T(8,128)(2,1)S(1)}, u32[]{:S(2)}, u32[]{:S(2)}) collective-permute-start(bf16[3,10,16,128]{3,2,1,0:T(8,128)(2,1)S(1)} %collective-permute-done.20.refs_2_), channel_id=1, source_target_pairs={{0,1},{1,0},{2,3},{3,2},{4,5},{5,4},{6,7},{7,6},{8,9},{9,8},{10,11... | collective-permute-start | bytes 368648 | tf_op jit(solution)/shard_map/ppermute | solution.py:28
  130.7 0.0 collective-permute-done.21.refs_3_
  130.7 0.7 collective-permute-start.25
  131.4 0.3 collective-permute-done.24.refs_6_
  131.7 0.7 collective-permute-done.25.refs_7_
  132.4 1.6 %copy-done.2 = f32[1,2,512,512]{3,2,1,0:T(8,128)S(1)} copy-done((f32[1,2,512,512]{3,2,1,0:T(8,128)S(1)}, f32[1,2,512,512]{3,2,1,0:T(8,128)}, u32[]{:S(2)}) %copy-start.2) | copy-done | bytes 2097176
  134.0 1.8 %finish.1 = (f32[2,512,512]{2,1,0:T(8,128)}, bf16[512,128]{1,0:T(8,128)(2,1)}) custom-call(f32[2,512,512]{2,1,0:T(8,128)S(1)} %bitcast.17, f32[2,8,128]{2,1,0:T(8,128)S(1)} %get-tuple-element.43.occupied, bf16[128,512]{1,0:T(8,128)(2,1)S(1)} %fusion.2.mine.grad, bf16[3,10,16,128]{3,2,1,0:T(8,128)(2,1)S(1)} %add_add_fusion.refs_0_, ...), custom_call_target="tpu_custom_call" | custom-call | tf_op jit(solution)/shard_map/finish/pallas_call | solution.py:359
  (18 shorter events, 0.1 us)
Async XLA Ops:
  3.7 19.3 %collective-permute-start = (bf16[128,2560]{1,0:T(8,128)(2,1)}, bf16[128,2560]{1,0:T(8,128)(2,1)S(1)}, u32[]{:S(2)}, u32[]{:S(2)}) collective-permute-start(bf16[128,2560]{1,0:T(8,128)(2,1)} %get-tuple-element.39), channel_id=1, source_target_pairs={{0,8},{8,16},{16,24},{24,0},{1,9},{9,17},{17,25},{25,1},{2,10},{10... | collective-permute-start | bytes 1966088 | tf_op jit(solution)/shard_map/ppermute | solution.py:28
  5.9 31.0 %collective-permute-start.1 = (bf16[128,2560]{1,0:T(8,128)(2,1)}, bf16[128,2560]{1,0:T(8,128)(2,1)S(1)}, u32[]{:S(2)}, u32[]{:S(2)}) collective-permute-start(bf16[128,2560]{1,0:T(8,128)(2,1)} %get-tuple-element.40), channel_id=1, source_target_pairs={{0,16},{8,24},{16,0},{24,8},{1,17},{9,25},{17,1},{25,9},{2,18},{10... | collective-permute-start | bytes 1966088 | tf_op jit(solution)/shard_map/ppermute | solution.py:28
  8.5 28.4 %collective-permute-start.2 = (bf16[128,2560]{1,0:T(8,128)(2,1)}, bf16[128,2560]{1,0:T(8,128)(2,1)}, u32[]{:S(2)}, u32[]{:S(2)}) collective-permute-start(bf16[128,2560]{1,0:T(8,128)(2,1)} %get-tuple-element.41), channel_id=1, source_target_pairs={{0,24},{8,0},{16,8},{24,16},{1,25},{9,1},{17,9},{25,17},{2,26},{10... | collective-permute-start | bytes 1966088 | tf_op jit(solution)/shard_map/ppermute | solution.py:28
  11.9 2.2 %copy-start = (bf16[256,8192]{1,0:T(8,128)(2,1)S(1)}, bf16[256,8192]{1,0:T(8,128)(2,1)}, u32[]{:S(2)}) copy-start(bf16[256,8192]{1,0:T(8,128)(2,1)} %act.2) | copy-start | bytes 12582916
  14.1 1.6 %copy-start.1 = (f32[1,2,512,512]{3,2,1,0:T(8,128)S(1)}, f32[1,2,512,512]{3,2,1,0:T(8,128)}, u32[]{:S(2)}) copy-start(f32[1,2,512,512]{3,2,1,0:T(8,128)} %param.7) | copy-start | bytes 6291460
  14.1 1.6 %copy-start.5 = (s32[32]{0:T(128)S(1)}, s32[32]{0:T(128)}, u32[]{:S(2)}) copy-start(s32[32]{0:T(128)} %worker_of.3) | copy-start | bytes 388
  23.0 25.0 %copy-start.3 = (bf16[2,256,128]{2,1,0:T(8,128)(2,1)S(1)}, bf16[2,256,128]{2,1,0:T(8,128)(2,1)}, u32[]{:S(2)}) copy-start(bf16[2,256,128]{2,1,0:T(8,128)(2,1)} %cot.3) | copy-start | bytes 393220
  36.9 13.6 %collective-permute-start.3 = (bf16[128,2560]{1,0:T(8,128)(2,1)S(1)}, bf16[128,2560]{1,0:T(8,128)(2,1)}, u32[]{:S(2)}, u32[]{:S(2)}) collective-permute-start(bf16[128,2560]{1,0:T(8,128)(2,1)S(1)} %collective-permute-done.refs_0_), channel_id=1, source_target_pairs={{0,1},{1,0},{2,3},{3,2},{4,5},{5,4},{6,7},{7,6},{8,9},{9,8},{10,11... | collective-permute-start | bytes 1966088 | tf_op jit(solution)/shard_map/ppermute | solution.py:28
  38.5 12.0 %collective-permute-start.4 = (bf16[128,2560]{1,0:T(8,128)(2,1)S(1)}, bf16[128,2560]{1,0:T(8,128)(2,1)}, u32[]{:S(2)}, u32[]{:S(2)}) collective-permute-start(bf16[128,2560]{1,0:T(8,128)(2,1)S(1)} %collective-permute-done.1.refs_1_), channel_id=1, source_target_pairs={{0,1},{1,0},{2,3},{3,2},{4,5},{5,4},{6,7},{7,6},{8,9},{9,8},{10,11... | collective-permute-start | bytes 1966088 | tf_op jit(solution)/shard_map/ppermute | solution.py:28
  38.5 12.0 %collective-permute-start.5 = (bf16[128,2560]{1,0:T(8,128)(2,1)}, bf16[128,2560]{1,0:T(8,128)(2,1)}, u32[]{:S(2)}, u32[]{:S(2)}) collective-permute-start(bf16[128,2560]{1,0:T(8,128)(2,1)} %collective-permute-done.2.refs_2_), channel_id=1, source_target_pairs={{0,1},{1,0},{2,3},{3,2},{4,5},{5,4},{6,7},{7,6},{8,9},{9,8},{10,11... | collective-permute-start | bytes 1966088 | tf_op jit(solution)/shard_map/ppermute | solution.py:28
  39.9 53.3 %all-to-all-start = ((bf16[8,2,10,16,128]{4,3,2,1,0:T(8,128)(2,1)}), bf16[8,2,10,16,128]{4,3,2,1,0:T(8,128)(2,1)S(1)}, u32[]{:S(2)}, u32[]{:S(2)}) async-start(bf16[8,2,10,16,128]{4,3,2,1,0:T(8,128)(2,1)} %broadcast_in_dim.10), calls=%async_computation | async-start | bytes 1310720 | tf_op jit(solution)/shard_map/all_to_all | solution.py:380
  53.3 56.2 %copy-start.4 = (s32[16]{0:T(128)S(1)}, s32[16]{0:T(128)}, u32[]{:S(2)}) copy-start(s32[16]{0:T(128)} %plan.1) | copy-start | bytes 196
  53.3 20.5 %collective-permute-start.6 = (bf16[2,128,512]{2,1,0:T(8,128)(2,1)S(1)}, bf16[2,128,512]{2,1,0:T(8,128)(2,1)S(1)}, u32[]{:S(2)}, u32[]{:S(2)}) collective-permute-start(bf16[2,128,512]{2,1,0:T(8,128)(2,1)S(1)} %get-tuple-element.53), channel_id=1, source_target_pairs={{0,32},{32,64},{64,96},{96,128},{128,160},{160,192},{192,224},{224... | collective-permute-start | bytes 786440 | tf_op jit(solution)/shard_map/ppermute | solution.py:28
  54.8 18.9 %collective-permute-start.7 = (bf16[2,128,512]{2,1,0:T(8,128)(2,1)S(1)}, bf16[2,128,512]{2,1,0:T(8,128)(2,1)S(1)}, u32[]{:S(2)}, u32[]{:S(2)}) collective-permute-start(bf16[2,128,512]{2,1,0:T(8,128)(2,1)S(1)} %get-tuple-element.54), channel_id=1, source_target_pairs={{0,224},{32,0},{64,32},{96,64},{128,96},{160,128},{192,160},{224,1... | collective-permute-start | bytes 786440 | tf_op jit(solution)/shard_map/ppermute | solution.py:28
  56.2 17.6 %collective-permute-start.8 = (bf16[64,512]{1,0:T(8,128)(2,1)S(1)}, bf16[64,512]{1,0:T(8,128)(2,1)S(1)}, u32[]{:S(2)}, u32[]{:S(2)}) collective-permute-start(bf16[64,512]{1,0:T(8,128)(2,1)S(1)} %get-tuple-element.57), channel_id=1, source_target_pairs={{0,64},{32,96},{64,128},{96,160},{128,192},{160,224},{192,0},{224,... | collective-permute-start | bytes 196616 | tf_op jit(solution)/shard_map/ppermute | solution.py:28
  57.2 16.6 %collective-permute-start.9 = (bf16[64,512]{1,0:T(8,128)(2,1)S(1)}, bf16[64,512]{1,0:T(8,128)(2,1)S(1)}, u32[]{:S(2)}, u32[]{:S(2)}) collective-permute-start(bf16[64,512]{1,0:T(8,128)(2,1)S(1)} %get-tuple-element.58), channel_id=1, source_target_pairs={{0,192},{32,224},{64,0},{96,32},{128,64},{160,96},{192,128},{224,1... | collective-permute-start | bytes 196616 | tf_op jit(solution)/shard_map/ppermute | solution.py:28
  73.8 7.8 %collective-permute-start.10 = (bf16[128,512]{1,0:T(8,128)(2,1)S(1)}, bf16[128,512]{1,0:T(8,128)(2,1)S(1)}, u32[]{:S(2)}, u32[]{:S(2)}) collective-permute-start(bf16[128,512]{1,0:T(8,128)(2,1)S(1)} %get-tuple-element.59), channel_id=1, source_target_pairs={{0,64},{32,96},{64,128},{96,160},{128,192},{160,224},{192,0},{224,... | collective-permute-start | bytes 393224 | tf_op jit(solution)/shard_map/ppermute | solution.py:28
  76.2 5.7 %collective-permute-start.11 = (bf16[128,512]{1,0:T(8,128)(2,1)S(1)}, bf16[128,512]{1,0:T(8,128)(2,1)S(1)}, u32[]{:S(2)}, u32[]{:S(2)}) collective-permute-start(bf16[128,512]{1,0:T(8,128)(2,1)S(1)} %get-tuple-element.60), channel_id=1, source_target_pairs={{0,192},{32,224},{64,0},{96,32},{128,64},{160,96},{192,128},{224,1... | collective-permute-start | bytes 393224 | tf_op jit(solution)/shard_map/ppermute | solution.py:28
  82.0 3.9 %collective-permute-start.12 = (bf16[128,512]{1,0:T(8,128)(2,1)S(1)}, bf16[128,512]{1,0:T(8,128)(2,1)S(1)}, u32[]{:S(2)}, u32[]{:S(2)}) collective-permute-start(bf16[128,512]{1,0:T(8,128)(2,1)S(1)} %fusion.2.mine.grad), channel_id=1, source_target_pairs={{0,1},{1,0},{2,3},{3,2},{4,5},{5,4},{6,7},{7,6},{8,9},{9,8},{10,11... | collective-permute-start | bytes 393224 | tf_op jit(solution)/shard_map/ppermute | solution.py:28
  86.3 4.9 %collective-permute-start.13 = (bf16[10,16,128]{2,1,0:T(8,128)(2,1)S(1)}, bf16[10,16,128]{2,1,0:T(8,128)(2,1)S(1)}, u32[]{:S(2)}, u32[]{:S(2)}) collective-permute-start(bf16[10,16,128]{2,1,0:T(8,128)(2,1)S(1)} %get-tuple-element.63), channel_id=1, source_target_pairs={{0,2},{2,4},{4,6},{6,0},{1,3},{3,5},{5,7},{7,1},{8,10},{10,12},{12... | collective-permute-start | bytes 122888 | tf_op jit(solution)/shard_map/ppermute | solution.py:28
  87.6 4.5 %collective-permute-start.14 = (bf16[10,16,128]{2,1,0:T(8,128)(2,1)S(1)}, bf16[10,16,128]{2,1,0:T(8,128)(2,1)S(1)}, u32[]{:S(2)}, u32[]{:S(2)}) collective-permute-start(bf16[10,16,128]{2,1,0:T(8,128)(2,1)S(1)} %get-tuple-element.64), channel_id=1, source_target_pairs={{0,4},{2,6},{4,0},{6,2},{1,5},{3,7},{5,1},{7,3},{8,12},{10,14},{12... | collective-permute-start | bytes 122888 | tf_op jit(solution)/shard_map/ppermute | solution.py:28
  90.1 3.1 %collective-permute-start.15 = (bf16[10,16,128]{2,1,0:T(8,128)(2,1)S(1)}, bf16[10,16,128]{2,1,0:T(8,128)(2,1)S(1)}, u32[]{:S(2)}, u32[]{:S(2)}) collective-permute-start(bf16[10,16,128]{2,1,0:T(8,128)(2,1)S(1)} %get-tuple-element.65), channel_id=1, source_target_pairs={{0,6},{2,0},{4,2},{6,4},{1,7},{3,1},{5,3},{7,5},{8,14},{10,8},{12,... | collective-permute-start | bytes 122888 | tf_op jit(solution)/shard_map/ppermute | solution.py:28
  110.2 5.0 %collective-permute-start.16 = (bf16[3,10,16,128]{3,2,1,0:T(8,128)(2,1)S(1)}, bf16[3,10,16,128]{3,2,1,0:T(8,128)(2,1)S(1)}, u32[]{:S(2)}, u32[]{:S(2)}) collective-permute-start(bf16[3,10,16,128]{3,2,1,0:T(8,128)(2,1)S(1)} %get-tuple-element.69), channel_id=1, source_target_pairs={{0,8},{8,16},{16,24},{24,0},{1,9},{9,17},{17,25},{25,1},{2,10},{10... | collective-permute-start | bytes 368648 | tf_op jit(solution)/shard_map/ppermute | solution.py:28
  111.3 5.7 %collective-permute-start.17 = (bf16[3,10,16,128]{3,2,1,0:T(8,128)(2,1)S(1)}, bf16[3,10,16,128]{3,2,1,0:T(8,128)(2,1)S(1)}, u32[]{:S(2)}, u32[]{:S(2)}) collective-permute-start(bf16[3,10,16,128]{3,2,1,0:T(8,128)(2,1)S(1)} %get-tuple-element.70), channel_id=1, source_target_pairs={{0,16},{8,24},{16,0},{24,8},{1,17},{9,25},{17,1},{25,9},{2,18},{10... | collective-permute-start | bytes 368648 | tf_op jit(solution)/shard_map/ppermute | solution.py:28
  113.4 3.7 %collective-permute-start.18 = (bf16[3,10,16,128]{3,2,1,0:T(8,128)(2,1)S(1)}, bf16[3,10,16,128]{3,2,1,0:T(8,128)(2,1)S(1)}, u32[]{:S(2)}, u32[]{:S(2)}) collective-permute-start(bf16[3,10,16,128]{3,2,1,0:T(8,128)(2,1)S(1)} %get-tuple-element.71), channel_id=1, source_target_pairs={{0,24},{8,0},{16,8},{24,16},{1,25},{9,1},{17,9},{25,17},{2,26},{10... | collective-permute-start | bytes 368648 | tf_op jit(solution)/shard_map/ppermute | solution.py:28
  117.2 9.6 %collective-permute-start.19 = (bf16[3,10,16,128]{3,2,1,0:T(8,128)(2,1)S(1)}, bf16[3,10,16,128]{3,2,1,0:T(8,128)(2,1)S(1)}, u32[]{:S(2)}, u32[]{:S(2)}) collective-permute-start(bf16[3,10,16,128]{3,2,1,0:T(8,128)(2,1)S(1)} %add_add_fusion.refs_0_), channel_id=1, source_target_pairs={{0,2},{2,4},{4,6},{6,0},{1,3},{3,5},{5,7},{7,1},{8,10},{10,12},{12... | collective-permute-start | bytes 368648 | tf_op jit(solution)/shard_map/ppermute | solution.py:28
  117.3 11.5 %collective-permute-start.20 = (bf16[3,10,16,128]{3,2,1,0:T(8,128)(2,1)S(1)}, bf16[3,10,16,128]{3,2,1,0:T(8,128)(2,1)S(1)}, u32[]{:S(2)}, u32[]{:S(2)}) collective-permute-start(bf16[3,10,16,128]{3,2,1,0:T(8,128)(2,1)S(1)} %add_add_fusion.refs_0_), channel_id=1, source_target_pairs={{0,4},{2,6},{4,0},{6,2},{1,5},{3,7},{5,1},{7,3},{8,12},{10,14},{12... | collective-permute-start | bytes 368648 | tf_op jit(solution)/shard_map/ppermute | solution.py:28
  119.9 10.8 %collective-permute-start.21 = (bf16[3,10,16,128]{3,2,1,0:T(8,128)(2,1)S(1)}, bf16[3,10,16,128]{3,2,1,0:T(8,128)(2,1)S(1)}, u32[]{:S(2)}, u32[]{:S(2)}) collective-permute-start(bf16[3,10,16,128]{3,2,1,0:T(8,128)(2,1)S(1)} %add_add_fusion.refs_0_), channel_id=1, source_target_pairs={{0,6},{2,0},{4,2},{6,4},{1,7},{3,1},{5,3},{7,5},{8,14},{10,8},{12,... | collective-permute-start | bytes 368648 | tf_op jit(solution)/shard_map/ppermute | solution.py:28
  120.4 11.0 %collective-permute-start.22 = (bf16[3,10,16,128]{3,2,1,0:T(8,128)(2,1)S(1)}, bf16[3,10,16,128]{3,2,1,0:T(8,128)(2,1)S(1)}, u32[]{:S(2)}, u32[]{:S(2)}) collective-permute-start(bf16[3,10,16,128]{3,2,1,0:T(8,128)(2,1)S(1)} %add_add_fusion.refs_0_), channel_id=1, source_target_pairs={{0,1},{1,0},{2,3},{3,2},{4,5},{5,4},{6,7},{7,6},{8,9},{9,8},{10,11... | collective-permute-start | bytes 368648 | tf_op jit(solution)/shard_map/ppermute | solution.py:28
  126.8 4.6 %collective-permute-start.23 = (bf16[3,10,16,128]{3,2,1,0:T(8,128)(2,1)S(1)}, bf16[3,10,16,128]{3,2,1,0:T(8,128)(2,1)S(1)}, u32[]{:S(2)}, u32[]{:S(2)}) collective-permute-start(bf16[3,10,16,128]{3,2,1,0:T(8,128)(2,1)S(1)} %collective-permute-done.19.refs_1_), channel_id=1, source_target_pairs={{0,1},{1,0},{2,3},{3,2},{4,5},{5,4},{6,7},{7,6},{8,9},{9,8},{10,11... | collective-permute-start | bytes 368648 | tf_op jit(solution)/shard_map/ppermute | solution.py:28
  128.8 2.9 %collective-permute-start.24 = (bf16[3,10,16,128]{3,2,1,0:T(8,128)(2,1)S(1)}, bf16[3,10,16,128]{3,2,1,0:T(8,128)(2,1)S(1)}, u32[]{:S(2)}, u32[]{:S(2)}) collective-permute-start(bf16[3,10,16,128]{3,2,1,0:T(8,128)(2,1)S(1)} %collective-permute-done.20.refs_2_), channel_id=1, source_target_pairs={{0,1},{1,0},{2,3},{3,2},{4,5},{5,4},{6,7},{7,6},{8,9},{9,8},{10,11... | collective-permute-start | bytes 368648 | tf_op jit(solution)/shard_map/ppermute | solution.py:28
  130.7 1.7 %collective-permute-start.25 = (bf16[3,10,16,128]{3,2,1,0:T(8,128)(2,1)S(1)}, bf16[3,10,16,128]{3,2,1,0:T(8,128)(2,1)S(1)}, u32[]{:S(2)}, u32[]{:S(2)}) collective-permute-start(bf16[3,10,16,128]{3,2,1,0:T(8,128)(2,1)S(1)} %collective-permute-done.21.refs_3_), channel_id=1, source_target_pairs={{0,1},{1,0},{2,3},{3,2},{4,5},{5,4},{6,7},{7,6},{8,9},{9,8},{10,11... | collective-permute-start | bytes 368648 | tf_op jit(solution)/shard_map/ppermute | solution.py:28
  132.4 1.6 %copy-start.2 = (f32[1,2,512,512]{3,2,1,0:T(8,128)S(1)}, f32[1,2,512,512]{3,2,1,0:T(8,128)}, u32[]{:S(2)}) copy-start(f32[1,2,512,512]{3,2,1,0:T(8,128)} %param.7) | copy-start | bytes 6291460
